TPU v7x, 512 devices: a whole 4x8x8 slice. The times are simulated.
512 devices in a mesh: dp: 64 (over y, z), tp: 8 (over x, core).
Axes of the slice: x: 4, y: 8, z: 8, core: 2. Of those that a mesh axis runs over, the one named last changes fastest.
Arguments:
- hidden: bfloat16 [256, 7168], P('dp', 'tp'), may hold values from -6 to 6
- kva_weight: bfloat16 [7168, 576], P('tp'), may hold values from -0.0625 to 0.0625
- kv_gain: float32 [512], replicated, may hold values from 0.5 to 1.5
- queries: bfloat16 [256, 128, 576], P('dp')
- latent_cache: bfloat16 [6144, 64, 576], P('dp', 'tp'), may hold values from -6 to 6
- outbox: bfloat16 [4096, 64, 576], P('dp', 'tp'), may hold values from -6 to 6
- out_dest: int32 [4096], P('dp'), may hold values from 0 to 63, as said below
- page_table: int32 [256, 40], P('dp'), may hold values from 0 to 223, as said below
- lengths: int32 [256], P('dp'), may hold values from 1025 to 2560, as said below
- give_rows: int32 [128], P('dp'), may hold values from 0 to 3, as said below
Outputs:
- attended: bfloat16 [256, 128, 512], P('dp', 'tp')
- new_latent: bfloat16 [256, 576], P('dp')
Inputs may be any that keep to these rules, and one draw needn't show every extreme that they name: `out_dest`: no group sends more than 2 pages to one group; every group sends exactly 2 pages to some group. `page_table`: each row lists its resident pages (entries below 96, no resident page in two rows of a group), then exactly 16 filled arrival slots (entry 96 + s * 2 + k), then entries that its length leaves unused; every request has at least one full resident page. `lengths`: tokens covered: all listed pages but the last arrived one are full; some row of each group has the full 40 * 64. `give_rows`: 2 different rows of each group.
All inputs are finite; a program needn't handle non-finite values.
Results may differ from a plain program's by a relative error of at most 0.012.
Values may be sent and summed in bfloat16 or wider, within the bound.
No kernel may reach another device: no remote copies, remote signals or barrier semaphores. Data moves between devices by JAX's collectives and lax.ppermute only.
A program may use at most 64 MiB of HBM per device.

v0:
```python
import jax
import jax.numpy as jnp
from jax import lax
from jax.sharding import PartitionSpec as P

KVL = 512
PAGE = 64
CAP = 2


EPSILON = 1e-06
SCORE_SCALE = 192.0 ** (-0.5)


def from_partner(array, axis, stride):
    return lax.ppermute(array, axis, [(i, i ^ 1 << stride) for i in range(lax.axis_size(axis))])


def normalize(raw_latent, kv_gain):
    head_part = raw_latent[:, :KVL]
    inverse = lax.rsqrt(jnp.mean(head_part * head_part, axis=1, keepdims=True) + EPSILON)
    return jnp.concatenate(
        [head_part * inverse * kv_gain[None, :], raw_latent[:, KVL:]], axis=1
    ).astype(jnp.bfloat16)


def shards(
    hidden,
    kva_weight,
    kv_gain,
    queries,
    latent_cache,
    outbox,
    out_dest,
    page_table,
    lengths,
    give_rows,
):
    group_count = lax.axis_size("dp")
    shard_count = lax.axis_size("tp")
    tp_index = lax.axis_index("tp")
    row_count = hidden.shape[0]
    page_piece = latent_cache.shape[1]
    lat_width = latent_cache.shape[2]
    pages_row = page_table.shape[1]
    sent_count = outbox.shape[0]
    same_dest = (out_dest[:, None] == out_dest[None, :]).astype(jnp.int32)
    lower_mask = (
        lax.broadcasted_iota(jnp.int32, (sent_count, sent_count), 0)
        > lax.broadcasted_iota(jnp.int32, (sent_count, sent_count), 1)
    ).astype(jnp.int32)
    dest_rank = jnp.sum(same_dest * lower_mask, axis=1)
    outgoing = jnp.zeros((group_count * CAP, page_piece, lat_width), jnp.bfloat16)
    outgoing = outgoing.at[out_dest * CAP + dest_rank].set(outbox)
    arrived = lax.all_to_all(
        outgoing.reshape(group_count, CAP, page_piece, lat_width),
        "dp",
        split_axis=0,
        concat_axis=0,
        tiled=True,
    )
    page_pool = jnp.concatenate(
        [latent_cache, arrived.reshape(group_count * CAP, page_piece, lat_width)], axis=0
    )
    gathered = page_pool[page_table]
    position = (
        lax.broadcasted_iota(jnp.int32, (pages_row, page_piece), 0) * PAGE
        + tp_index * page_piece
        + lax.broadcasted_iota(jnp.int32, (pages_row, page_piece), 1)
    )
    live_mask = (position[None] < lengths[:, None, None]).astype(jnp.bfloat16)
    partner_bit = group_count.bit_length() - 2
    moved = from_partner(
        (gathered[give_rows], queries[give_rows], hidden[give_rows], live_mask[give_rows]),
        "dp",
        partner_bit,
    )
    gathered = gathered.at[give_rows].set(moved[0])
    queries = queries.at[give_rows].set(moved[1])
    hidden = hidden.at[give_rows].set(moved[2])
    live_mask = live_mask.at[give_rows].set(moved[3])
    partial_raw = jnp.dot(hidden, kva_weight, preferred_element_type=jnp.float32)
    new_latent = normalize(lax.psum(partial_raw, "tp"), kv_gain)
    key_rows = gathered.reshape(row_count, pages_row * page_piece, lat_width)
    live_keys = live_mask.reshape(row_count, pages_row * page_piece) > 0
    scores = SCORE_SCALE * jnp.einsum(
        "rhl,rkl->rhk", queries, key_rows, preferred_element_type=jnp.float32
    )
    scores = jnp.where(live_keys[:, None, :], scores, -jnp.inf)
    block_top = jnp.max(scores, axis=2)
    weights = jnp.exp(scores - block_top[..., None])
    block_total = jnp.sum(weights, axis=2)
    blend = jnp.einsum(
        "rhk,rkc->rhc",
        weights.astype(jnp.bfloat16),
        key_rows[:, :, :KVL],
        preferred_element_type=jnp.float32,
    )
    partial_value = (blend / block_total[..., None]).astype(jnp.bfloat16)
    head_count = queries.shape[1] // shard_count
    own_queries = lax.dynamic_slice_in_dim(queries, tp_index * head_count, head_count, 1)
    own_score = SCORE_SCALE * jnp.einsum(
        "rhl,rl->rh", own_queries, new_latent, preferred_element_type=jnp.float32
    )
    own_value = new_latent[:, :KVL].astype(jnp.float32)
    highest = lax.pmax(block_top, "tp")
    factor = jnp.exp(block_top - highest) * block_total
    numerator, denominator = (
        lax.psum_scatter(
            factor[..., None] * partial_value.astype(jnp.float32),
            "tp",
            scatter_dimension=1,
            tiled=True,
        ),
        lax.psum_scatter(factor, "tp", scatter_dimension=1, tiled=True),
    )
    own_high = lax.dynamic_slice_in_dim(highest, tp_index * head_count, head_count, 1)
    peak_score = jnp.maximum(own_high, own_score)
    carried = jnp.exp(own_high - peak_score)
    fresh_weight = jnp.exp(own_score - peak_score)
    result = (numerator * carried[..., None] + fresh_weight[..., None] * own_value[:, None, :]) / (
        denominator * carried + fresh_weight
    )[..., None]
    final = result.astype(jnp.bfloat16)
    return (final, new_latent)


def solution(mesh):
    placed = (
        P("dp", "tp"),
        P("tp", None),
        P(),
        P("dp", None, None),
        P("dp", "tp", None),
        P("dp", "tp", None),
        P("dp"),
        P("dp", None),
        P("dp"),
        P("dp"),
    )
    return jax.shard_map(
        shards,
        mesh=mesh,
        in_specs=placed,
        out_specs=(P("dp", "tp", None), P("dp", None)),
        check_vma=False,
    )
```

profile of v0, /device:TPU:8, one launch (start us, length us, event | category | flops | bytes accessed | tf_op | source)
XLA Modules:
  0.0 221.6 jit_solution(105380592655211043)
XLA Ops:
  7.2 1.2 copy.29
  8.4 0.7 copy.28
  9.1 0.9 select_reduce_fusion.1
  10.0 0.7 compare_select_fusion.1
  10.7 1.2 broadcast_in_dim.18
  11.8 8.0 %scatter_fusion.2 = bf16[128,8,576]{2,1,0:T(8,128)(2,1)} fusion(bf16[128,8,576]{2,1,0:T(8,128)(2,1)} %broadcast_in_dim.18, s32[64]{0:T(128)S(1)} %compare_select_fusion.1, bf16[64,8,576]{2,1,0:T(8,128)(2,1)S(1)} %copy-done.5), kind=kCustom, calls=%fused_computation.7 | custom fusion | bytes 1769728 | tf_op jit(solution)/shard_map/scatter | solution.py:54
  19.9 16.7 %all-to-all-start = ((bf16[64,2,8,576]{3,2,1,0:T(8,128)(2,1)}), bf16[64,2,8,576]{3,2,1,0:T(8,128)(2,1)S(1)}, u32[]{:S(2)}, u32[]{:S(2)}) async-start(bf16[64,2,8,576]{3,2,1,0:T(8,128)(2,1)} %bitcast), calls=%async_computation | async-start | bytes 2621440 | tf_op jit(solution)/shard_map/all_to_all | solution.py:55
  36.7 1.3 gather_fusion.1
  38.0 6.5 %collective-permute-start.1 = (bf16[2,128,576]{1,2,0:T(8,128)(2,1)}, bf16[2,128,576]{1,2,0:T(8,128)(2,1)}, u32[]{:S(2)}, u32[]{:S(2)}) collective-permute-start(bf16[2,128,576]{1,2,0:T(8,128)(2,1)} %gather_fusion.1), channel_id=1, source_target_pairs={{0,256},{8,264},{16,272},{24,280},{32,288},{40,296},{48,304},{56,3... | collective-permute-start | bytes 884744 | tf_op jit(solution)/shard_map/ppermute | solution.py:16
  44.6 29.3 %all-to-all-done = bf16[64,2,8,576]{3,2,1,0:T(8,128)(2,1)S(1)} async-done(((bf16[64,2,8,576]{3,2,1,0:T(8,128)(2,1)}), bf16[64,2,8,576]{3,2,1,0:T(8,128)(2,1)S(1)}, u32[]{:S(2)}, u32[]{:S(2)}) %all-to-all-start) | async-done | bytes 1179680 | tf_op jit(solution)/shard_map/all_to_all | solution.py:55
  73.9 1.1 copy-done.4
  75.0 1.9 pad_maximum_fusion
  76.9 2.2 %gather_fusion.2 = bf16[160,8,576]{2,1,0:T(8,128)(2,1)} fusion(bf16[224,8,576]{2,1,0:T(8,128)(2,1)S(1)} %pad_maximum_fusion, s32[1024]{0:T(1024)S(1)} %pad_clamp_fusion), kind=kCustom, calls=%fused_computation.2 | custom fusion | bytes 2949760 | tf_op jit(solution)/shard_map/gather | solution.py:65
  79.2 3.1 %gather_fusion.3 = bf16[2,40,8,576]{3,2,1,0:T(8,128)(2,1)} fusion(bf16[4,40,8,576]{3,2,1,0:T(8,128)(2,1)} %bitcast.17, s32[1024]{0:T(1024)S(1)} %pad_clamp_fusion.1), kind=kCustom, calls=%fused_computation.3 | custom fusion | bytes 1474568 | tf_op jit(solution)/shard_map/gather | solution.py:74
  82.3 4.5 %collective-permute-start.2 = (bf16[2,40,8,576]{3,2,1,0:T(8,128)(2,1)}, bf16[2,40,8,576]{3,2,1,0:T(8,128)(2,1)}, u32[]{:S(2)}, u32[]{:S(2)}) collective-permute-start(bf16[2,40,8,576]{3,2,1,0:T(8,128)(2,1)} %gather_fusion.3), channel_id=1, source_target_pairs={{0,256},{8,264},{16,272},{24,280},{32,288},{40,296},{48,304},{56,3... | collective-permute-start | bytes 2211848 | tf_op jit(solution)/shard_map/ppermute | solution.py:16
  87.4 5.3 %collective-permute-start = (bf16[2,40,8]{1,2,0:T(8,128)(2,1)S(1)}, bf16[2,40,8]{1,2,0:T(8,128)(2,1)S(1)}, u32[]{:S(2)}, u32[]{:S(2)}) collective-permute-start(bf16[2,40,8]{1,2,0:T(8,128)(2,1)S(1)} %gather_fusion), channel_id=1, source_target_pairs={{0,256},{8,264},{16,272},{24,280},{32,288},{40,296},{48,304},{56,3... | collective-permute-start | bytes 3848 | tf_op jit(solution)/shard_map/ppermute | solution.py:16
  92.7 27.6 %collective-permute-done = bf16[2,40,8]{1,2,0:T(8,128)(2,1)S(1)} collective-permute-done((bf16[2,40,8]{1,2,0:T(8,128)(2,1)S(1)}, bf16[2,40,8]{1,2,0:T(8,128)(2,1)S(1)}, u32[]{:S(2)}, u32[]{:S(2)}) %collective-permute-start) | collective-permute-done | bytes 1312 | tf_op jit(solution)/shard_map/ppermute | solution.py:16
  121.1 2.4 %scatter_fusion.1 = bf16[4,128,576]{1,2,0:T(8,128)(2,1)} fusion(bf16[4,128,576]{1,2,0:T(8,128)(2,1)} %copy-done.2, s32[2]{0:T(128)S(1)} %compare_select_fusion.2, bf16[2,128,576]{1,2,0:T(8,128)(2,1)} %collective-permute-done.1), kind=kCustom, calls=%fused_computation.6 | custom fusion | bytes 884744 | tf_op jit(solution)/shard_map/scatter | solution.py:79
  123.5 1.8 scatter_fusion.3
  125.4 1.4 select_reduce_fusion
  126.8 12.4 %pmax.7 = f32[4,128]{1,0:T(4,128)S(1)} all-reduce(f32[4,128]{1,0:T(4,128)S(1)} %get-tuple-element.7), channel_id=1, replica_groups=mesh['dp'=64,'tp'=8] {'tp'}, use_global_device_ids=true, to_apply=%region_6.0 | all-reduce | flops 512 | bytes 4096 | tf_op jit(solution)/shard_map/pmax | solution.py:106
  139.2 1.3 fusion.13
  140.6 0.7 copy.17
  141.4 3.0 %fusion.7 = f32[4,128,512]{2,1,0:T(8,128)} fusion(bf16[4,320,576]{2,1,0:T(8,128)(2,1)S(1)} %bitcast.19, f32[4,128]{1,0:T(4,128)S(1)} %fusion.13, f32[4,128]{1,0:T(4,128)S(1)} %exponential_multiply_fusion, f32[4,128,320]{1,2,0:T(8,128)} %get-tuple-element.8, f32[4,128]{1,0:T(4,128)S(1)} %get-tuple-element.7, pred[4,320]{1,0:T(4,128)(4,1)S(1)} %gt.18), kind=kOutput, calls=%fused_computation.15 | convolution fusion | flops 169312256 | bytes 3022336 | tf_op jit(solution)/shard_map/rhk,rkc->rhc/dot_general | solution.py:93
  144.9 7.3 %collective-permute-start.3 = (bf16[2,896]{1,0:T(2,128)(2,1)S(1)}, bf16[2,896]{1,0:T(2,128)(2,1)S(1)}, u32[]{:S(2)}, u32[]{:S(2)}) collective-permute-start(bf16[2,896]{1,0:T(2,128)(2,1)S(1)} %gather_fusion.4), channel_id=1, source_target_pairs={{0,256},{8,264},{16,272},{24,280},{32,288},{40,296},{48,304},{56,3... | collective-permute-start | bytes 10760 | tf_op jit(solution)/shard_map/ppermute | solution.py:16
  152.3 2.0 collective-permute-done.3
  154.3 0.6 scatter_fusion.4
  155.3 23.6 %psum.7 = f32[4,576]{1,0:T(4,128)S(1)} all-reduce(f32[4,576]{1,0:T(4,128)S(1)} %fusion.27), channel_id=1, replica_groups=mesh['dp'=64,'tp'=8] {'tp'}, use_global_device_ids=true, to_apply=%region_10.11 | all-reduce | flops 2304 | bytes 18432 | tf_op jit(solution)/shard_map/psum | solution.py:83
  179.1 0.6 pad_maximum_fusion.1
  180.1 0.8 copy.18
  180.9 32.2 %reduce-scatter.5.cloned.1.call-done = f32[4,16,512]{2,1,0:T(8,128)} async-done(((f32[4,128,512]{2,1,0:T(8,128)}), f32[4,16,512]{2,1,0:T(8,128)}) %reduce-scatter.5.cloned.1.call-update) | async-done | bytes 131088 | tf_op jit(solution)/shard_map/reduce_scatter | solution.py:109
  213.1 1.6 divide_convert_fusion
  (49 shorter events, 3.3 us)
Async XLA Ops:
  7.2 147.8 %copy-start = (bf16[896,576]{0,1:T(8,128)(2,1)S(1)}, bf16[896,576]{0,1:T(8,128)(2,1)}, u32[]{:S(2)}) copy-start(bf16[896,576]{0,1:T(8,128)(2,1)} %param.11) | copy-start | bytes 3096580
  7.2 4.6 %copy-start.5 = (bf16[64,8,576]{2,1,0:T(8,128)(2,1)S(1)}, bf16[64,8,576]{2,1,0:T(8,128)(2,1)}, u32[]{:S(2)}) copy-start(bf16[64,8,576]{2,1,0:T(8,128)(2,1)} %param.15) | copy-start | bytes 1769476
  8.4 28.3 %copy-start.2 = (bf16[4,128,576]{1,2,0:T(8,128)(2,1)}, bf16[4,128,576]{1,2,0:T(8,128)(2,1)S(1)}, u32[]{:S(2)}) copy-start(bf16[4,128,576]{1,2,0:T(8,128)(2,1)S(1)} %copy.29) | copy-start | bytes 1769476
  19.9 16.8 %copy-start.9 = (s32[2]{0:T(128)S(1)}, s32[2]{0:T(128)}, u32[]{:S(2)}) copy-start(s32[2]{0:T(128)} %param.19) | copy-start | bytes 28
  19.9 24.7 %copy-start.7 = (s32[4,40]{1,0:T(4,128)S(1)}, s32[4,40]{1,0:T(4,128)}, u32[]{:S(2)}) copy-start(s32[4,40]{1,0:T(4,128)} %param.17) | copy-start | bytes 1924
  19.9 54.1 %all-to-all-start = ((bf16[64,2,8,576]{3,2,1,0:T(8,128)(2,1)}), bf16[64,2,8,576]{3,2,1,0:T(8,128)(2,1)S(1)}, u32[]{:S(2)}, u32[]{:S(2)}) async-start(bf16[64,2,8,576]{3,2,1,0:T(8,128)(2,1)} %bitcast), calls=%async_computation | async-start | bytes 2621440 | tf_op jit(solution)/shard_map/all_to_all | solution.py:55
  36.6 143.4 %reduce-scatter.7.cloned.1.call-start = ((), (), s32[]{:S(2)}) async-start(), calls=%async_computation.4 | async-start | bytes 73728
  38.0 83.1 %collective-permute-start.1 = (bf16[2,128,576]{1,2,0:T(8,128)(2,1)}, bf16[2,128,576]{1,2,0:T(8,128)(2,1)}, u32[]{:S(2)}, u32[]{:S(2)}) collective-permute-start(bf16[2,128,576]{1,2,0:T(8,128)(2,1)} %gather_fusion.1), channel_id=1, source_target_pairs={{0,256},{8,264},{16,272},{24,280},{32,288},{40,296},{48,304},{56,3... | collective-permute-start | bytes 884744 | tf_op jit(solution)/shard_map/ppermute | solution.py:16
  73.9 1.1 copy-start.4
  79.2 7.6 %copy-start.8 = (s32[4]{0:T(128)S(1)}, s32[4]{0:T(128)}, u32[]{:S(2)}) copy-start(s32[4]{0:T(128)} %param.18) | copy-start | bytes 52
  79.2 44.4 %copy-start.1 = (bf16[160,8,576]{2,1,0:T(8,128)(2,1)S(1)}, bf16[160,8,576]{2,1,0:T(8,128)(2,1)}, u32[]{:S(2)}) copy-start(bf16[160,8,576]{2,1,0:T(8,128)(2,1)} %gather_fusion.2) | copy-start | bytes 4423684
  82.3 41.3 %collective-permute-start.2 = (bf16[2,40,8,576]{3,2,1,0:T(8,128)(2,1)}, bf16[2,40,8,576]{3,2,1,0:T(8,128)(2,1)}, u32[]{:S(2)}, u32[]{:S(2)}) collective-permute-start(bf16[2,40,8,576]{3,2,1,0:T(8,128)(2,1)} %gather_fusion.3), channel_id=1, source_target_pairs={{0,256},{8,264},{16,272},{24,280},{32,288},{40,296},{48,304},{56,3... | collective-permute-start | bytes 2211848 | tf_op jit(solution)/shard_map/ppermute | solution.py:16
  87.4 32.9 %collective-permute-start = (bf16[2,40,8]{1,2,0:T(8,128)(2,1)S(1)}, bf16[2,40,8]{1,2,0:T(8,128)(2,1)S(1)}, u32[]{:S(2)}, u32[]{:S(2)}) collective-permute-start(bf16[2,40,8]{1,2,0:T(8,128)(2,1)S(1)} %gather_fusion), channel_id=1, source_target_pairs={{0,256},{8,264},{16,272},{24,280},{32,288},{40,296},{48,304},{56,3... | collective-permute-start | bytes 3848 | tf_op jit(solution)/shard_map/ppermute | solution.py:16
  123.5 1.8 copy-start.3
  141.3 71.8 %reduce-scatter.5.cloned.1.call-start = ((), (), s32[]{:S(2)}) async-start(), calls=%async_computation.3 | async-start | bytes 1179648 | tf_op jit(solution)/shard_map/reduce_scatter | solution.py:109
  144.3 34.7 %copy-start.6 = (f32[512]{0:T(512)S(1)}, f32[512]{0:T(512)}, u32[]{:S(2)}) copy-start(f32[512]{0:T(512)} %param.12) | copy-start | bytes 6148
  144.9 9.4 %collective-permute-start.3 = (bf16[2,896]{1,0:T(2,128)(2,1)S(1)}, bf16[2,896]{1,0:T(2,128)(2,1)S(1)}, u32[]{:S(2)}, u32[]{:S(2)}) collective-permute-start(bf16[2,896]{1,0:T(2,128)(2,1)S(1)} %gather_fusion.4), channel_id=1, source_target_pairs={{0,256},{8,264},{16,272},{24,280},{32,288},{40,296},{48,304},{56,3... | collective-permute-start | bytes 10760 | tf_op jit(solution)/shard_map/ppermute | solution.py:16
Sparse Core Ops, SparseCore 0:
  141.5 32.5 reduce-scatter.6
  177.1 35.9 reduce-scatter.4
where the time goes:
time: 222 us
  waiting for transfers between devices  91.1 us (41%)
  starting transfers between devices  40.4 us (18%)
  blocking collectives  36 us (16%)
  local copies, waits for them, and re-layouts  27.2 us (12%)
  between operations  14.3 us (6%)
  other arithmetic  7.47 us (3%)
  matrix products  5.1 us (2%)
    reduce_scatter x1, waiting for transfers between devices, shards(): lax.psum_scatter(factor[..., None] * partial_value.astype(jnp.float32), '...  32.2 us
    ppermute x4, waiting for transfers between devices, from_partner(): lax.ppermute(array, axis, [(i, i ^ 1 << stride) for i in range(lax.axis_s...  29.6 us
    all_to_all x1, waiting for transfers between devices, shards(): lax.all_to_all(outgoing.reshape(group_count, CAP, page_piece, lat_width),...  29.3 us
    ppermute x4, starting transfers between devices, from_partner(): lax.ppermute(array, axis, [(i, i ^ 1 << stride) for i in range(lax.axis_s...  23.6 us
    psum x1, blocking collectives, shards(): new_latent = normalize(lax.psum(partial_raw, 'tp'), kv_gain)  23.6 us
    all_to_all x1, starting transfers between devices, shards(): lax.all_to_all(outgoing.reshape(group_count, CAP, page_piece, lat_width),...  16.7 us
    pmax x1, blocking collectives, shards(): highest = lax.pmax(block_top, 'tp')  12.4 us
    scatter x1, local copies, waits for them, and re-layouts, shards(): outgoing = outgoing.at[out_dest * CAP + dest_rank].set(outbox)  8.03 us
  transfers between devices with their start and end apart: 7, of which 4 were waited for; matrix products, arithmetic and copies ran while one was open for 9% of the time, Pallas kernels for 0%

commit v1 on v0

v1 whole, which is shorter than its diff:
```python
import functools

import jax
import jax.numpy as jnp
from jax import lax
from jax.experimental import pallas as pl
from jax.experimental.pallas import tpu as pltpu
from jax.sharding import PartitionSpec as P

KVL = 512
PAGE = 64
CAP = 2
ARR = 16
RESMAX = 24


EPSILON = 1e-06
SCORE_SCALE = 192.0 ** (-0.5)
VMEM_LIMIT = 32 * 1024 * 1024

SMEM = functools.partial(pl.BlockSpec, memory_space=pltpu.SMEM)
VMEM = functools.partial(pl.BlockSpec, memory_space=pltpu.VMEM)


def normalize(raw_latent, kv_gain):
    head_part = raw_latent[:, :KVL]
    inverse = lax.rsqrt(jnp.mean(head_part * head_part, axis=1, keepdims=True) + EPSILON)
    return jnp.concatenate(
        [head_part * inverse * kv_gain[None, :], raw_latent[:, KVL:]], axis=1
    ).astype(jnp.bfloat16)


def pack_kernel(dest_ref, outbox_ref, out_ref, count_ref):
    groups = out_ref.shape[0]
    out_ref[...] = jnp.zeros_like(out_ref)

    def clear(i, _):
        count_ref[i] = 0
        return 0

    lax.fori_loop(0, groups, clear, 0)

    def place(i, _):
        dest = dest_ref[i]
        rank = count_ref[dest]
        count_ref[dest] = rank + 1
        page = outbox_ref[i]

        @pl.when(rank == 0)
        def _():
            out_ref[dest, :, 0:KVL] = page[:, :KVL]
            out_ref[dest, :, 2 * KVL : 2 * KVL + 64] = page[:, KVL:]

        @pl.when(rank == 1)
        def _():
            out_ref[dest, :, KVL : 2 * KVL] = page[:, :KVL]
            out_ref[dest, :, 2 * KVL + 64 : 2 * KVL + 128] = page[:, KVL:]

        return 0

    lax.fori_loop(0, outbox_ref.shape[0], place, 0)


def resident_kernel(table_ref, length_ref, cache_ref, query_ref, score_ref, value_ref, key_ref):
    piece = cache_ref.shape[1]
    for row in range(query_ref.shape[0]):
        count = (length_ref[row] + (PAGE - 1)) // PAGE - ARR

        def fetch(pair, _):
            parts = []
            for half in range(2):
                entry = pair * 2 + half
                index = table_ref[row, jnp.where(entry < count, entry, 0)]
                parts.append(cache_ref[index])
            start = pl.multiple_of(pair * 2 * piece, 2 * piece)
            key_ref[pl.ds(start, 2 * piece), :] = jnp.concatenate(parts, axis=0)
            return 0

        lax.fori_loop(0, RESMAX // 2, fetch, 0)
        keys = key_ref[...]
        scores = SCORE_SCALE * jnp.dot(keys, query_ref[row], preferred_element_type=jnp.float32)
        token = lax.broadcasted_iota(jnp.int32, scores.shape, 0)
        score_ref[row] = jnp.where(token < count * piece, scores, -jnp.inf)
        value_ref[row] = keys[:, :KVL]


def arrived_kernel(
    shard_ref, table_ref, length_ref, arrived_ref, query_ref, score_ref, value_ref, send_ref, key_ref, rope_ref, stat_ref
):
    shards, piece = send_ref.shape[0], arrived_ref.shape[1]
    rows, _, heads = query_ref.shape
    own = heads // shards
    shard = shard_ref[0]
    stat_ref[...] = jnp.zeros_like(stat_ref)
    for row in range(rows):
        length = length_ref[row]
        count = (length + (PAGE - 1)) // PAGE - ARR

        def fetch(pair, _):
            latents, ropes = [], []
            for half in range(2):
                slot = table_ref[row, count + pair * 2 + half] - 96
                source, rank = slot // CAP, lax.rem(slot, CAP)
                first = pl.multiple_of(rank * KVL, KVL)
                latents.append(arrived_ref[source, :, pl.ds(first, KVL)])
                both = arrived_ref[source, :, 2 * KVL : 2 * KVL + 128]
                lane = lax.broadcasted_iota(jnp.int32, both.shape, 1)
                ropes.append(jnp.where(lane // 64 == rank, both.astype(jnp.float32), 0.0).astype(jnp.bfloat16))
            start = pl.multiple_of(pair * 2 * piece, 2 * piece)
            key_ref[pl.ds(start, 2 * piece), :] = jnp.concatenate(latents, axis=0)
            rope_ref[pl.ds(start, 2 * piece), :] = jnp.concatenate(ropes, axis=0)
            return 0

        lax.fori_loop(0, ARR // 2, fetch, 0)
        keys = key_ref[...]
        query = query_ref[row]
        rope_query = query[KVL:]
        scores = jnp.dot(keys, query[:KVL], preferred_element_type=jnp.float32)
        scores += jnp.dot(
            rope_ref[...], jnp.concatenate([rope_query, rope_query], axis=0), preferred_element_type=jnp.float32
        )
        token = lax.broadcasted_iota(jnp.int32, scores.shape, 0)
        position = (count + token // piece) * PAGE + shard * piece + lax.rem(token, piece)
        scores = jnp.where(position < length, SCORE_SCALE * scores, -jnp.inf)
        resident = score_ref[row]
        top = jnp.maximum(jnp.max(scores, axis=0, keepdims=True), jnp.max(resident, axis=0, keepdims=True))
        arrived_weights = jnp.exp(scores - top)
        resident_weights = jnp.exp(resident - top)
        total = jnp.sum(arrived_weights, axis=0, keepdims=True) + jnp.sum(resident_weights, axis=0, keepdims=True)
        inverse = 1.0 / total
        blend = lax.dot_general(
            (resident_weights * inverse).astype(jnp.bfloat16),
            value_ref[row],
            (((0,), (0,)), ((), ())),
            preferred_element_type=jnp.float32,
        ) + lax.dot_general(
            (arrived_weights * inverse).astype(jnp.bfloat16),
            keys,
            (((0,), (0,)), ((), ())),
            preferred_element_type=jnp.float32,
        )
        partial = blend.astype(jnp.bfloat16)
        for shard_to in range(shards):
            part = partial[shard_to * own : (shard_to + 1) * own]
            for chunk in range(KVL // 128):
                start = (chunk * rows + row) * own
                send_ref[shard_to, start : start + own, :] = part[:, chunk * 128 : (chunk + 1) * 128]
        level = top + jnp.log(total)
        for step in range(3):
            rounded = level.astype(jnp.bfloat16).astype(jnp.float32)
            stat_ref[step * rows + row : step * rows + row + 1, :] = rounded
            level = level - rounded
    stats = stat_ref[...].astype(jnp.bfloat16)
    for shard_to in range(shards):
        send_ref[shard_to, KVL // 128 * rows * own :, :] = stats


def combine_kernel(shard_ref, give_ref, received_ref, latent_ref, query_ref, home_ref, give_out_ref, mix_ref):
    shards = received_ref.shape[0]
    rows, _, heads = query_ref.shape
    own = heads // shards
    stat_base = KVL // 128 * rows * own
    latent = latent_ref[...]
    latent_float = latent.astype(jnp.float32)
    levels = []
    for share in range(shards):
        stats = received_ref[share, stat_base:, :].astype(jnp.float32)
        levels.append(stats[0:rows] + stats[rows : 2 * rows] + stats[2 * rows : 3 * rows])
    own_rows = []
    for row in range(rows):
        own_rows.append(jnp.dot(latent, query_ref[row], preferred_element_type=jnp.float32)[row : row + 1])
    own_score = SCORE_SCALE * jnp.concatenate(own_rows, axis=0)
    peak = own_score
    for level in levels:
        peak = jnp.maximum(peak, level)
    weights = [jnp.exp(level - peak) for level in levels] + [jnp.exp(own_score - peak)]
    total = functools.reduce(lambda a, b: a + b, weights)
    inverse = 1.0 / total
    mixed = jnp.concatenate([w * inverse for w in weights], axis=0)
    mixed = jnp.concatenate([mixed, jnp.zeros((heads - mixed.shape[0], heads), jnp.float32)], axis=0)
    mix_ref[...] = mixed.T
    mine = mix_ref[pl.ds(pl.multiple_of(shard_ref[0] * own, own), own), :]
    for row in range(rows):
        last = shards * rows + row
        for chunk in range(KVL // 128):
            lanes = slice(chunk * 128, (chunk + 1) * 128)
            value = mine[:, last : last + 1] * latent_float[row : row + 1, lanes]
            start = (chunk * rows + row) * own
            for share in range(shards):
                column = share * rows + row
                block = received_ref[share, start : start + own, :].astype(jnp.float32)
                value += mine[:, column : column + 1] * block
            home_ref[row, :, lanes] = value.astype(jnp.bfloat16)
    for move in range(give_out_ref.shape[0]):
        give_out_ref[move] = home_ref[give_ref[move]]


def shards(
    hidden,
    kva_weight,
    kv_gain,
    queries,
    latent_cache,
    outbox,
    out_dest,
    page_table,
    lengths,
    give_rows,
):
    group_count = lax.axis_size("dp")
    shard_count = lax.axis_size("tp")
    shard = lax.axis_index("tp").astype(jnp.int32).reshape(1)
    row_count = hidden.shape[0]
    page_piece = latent_cache.shape[1]
    heads = queries.shape[1]
    own = heads // shard_count
    moves = give_rows.shape[0]
    query_t = jnp.swapaxes(queries, 1, 2)
    params = pltpu.CompilerParams(vmem_limit_bytes=VMEM_LIMIT)

    outgoing = pl.pallas_call(
        pack_kernel,
        out_shape=jax.ShapeDtypeStruct((group_count, page_piece, 2 * KVL + 128), jnp.bfloat16),
        in_specs=[SMEM(), VMEM()],
        out_specs=VMEM(),
        scratch_shapes=[pltpu.SMEM((group_count,), jnp.int32)],
        compiler_params=params,
        name="pack",
    )(out_dest, outbox)
    arrived = lax.all_to_all(outgoing, "dp", split_axis=0, concat_axis=0, tiled=True)

    partial_raw = jnp.dot(hidden, kva_weight, preferred_element_type=jnp.float32)
    parts = lax.all_gather(partial_raw, "tp")
    home_latent = normalize(jnp.sum(parts, axis=0), kv_gain)
    partner = [(i, i ^ (group_count // 2)) for i in range(group_count)]
    is_given = (lax.broadcasted_iota(jnp.int32, (moves, row_count), 1) == give_rows[:, None])
    moved_latent = lax.ppermute(
        jnp.sum(jnp.where(is_given[:, :, None], home_latent[None].astype(jnp.float32), 0.0), axis=1).astype(jnp.bfloat16),
        "dp",
        partner,
    )

    def after_move(home, moved):
        shape = (row_count,) + (1,) * (home.ndim - 1)
        for move in range(moves):
            home = jnp.where(is_given[move].reshape(shape), moved[move][None], home)
        return home

    new_latent = after_move(home_latent, moved_latent)

    scores, values = pl.pallas_call(
        resident_kernel,
        out_shape=(
            jax.ShapeDtypeStruct((row_count, RESMAX * page_piece, heads), jnp.float32),
            jax.ShapeDtypeStruct((row_count, RESMAX * page_piece, KVL), jnp.bfloat16),
        ),
        in_specs=[SMEM(), SMEM(), VMEM(), VMEM()],
        out_specs=(VMEM(), VMEM()),
        scratch_shapes=[pltpu.VMEM((RESMAX * page_piece, latent_cache.shape[2]), jnp.bfloat16)],
        compiler_params=params,
        name="resident",
    )(page_table, lengths, latent_cache, query_t)

    send_rows = KVL // 128 * row_count * own + 16
    outbound = pl.pallas_call(
        arrived_kernel,
        out_shape=jax.ShapeDtypeStruct((shard_count, send_rows, 128), jnp.bfloat16),
        in_specs=[SMEM(), SMEM(), SMEM(), VMEM(), VMEM(), VMEM(), VMEM()],
        out_specs=VMEM(),
        scratch_shapes=[
            pltpu.VMEM((ARR * page_piece, KVL), jnp.bfloat16),
            pltpu.VMEM((ARR * page_piece, 128), jnp.bfloat16),
            pltpu.VMEM((16, heads), jnp.float32),
        ],
        compiler_params=params,
        name="arrived",
    )(shard, page_table, lengths, arrived, query_t, scores, values)
    received = lax.all_to_all(outbound, "tp", split_axis=0, concat_axis=0, tiled=True)

    home, given = pl.pallas_call(
        combine_kernel,
        out_shape=(
            jax.ShapeDtypeStruct((row_count, own, KVL), jnp.bfloat16),
            jax.ShapeDtypeStruct((moves, own, KVL), jnp.bfloat16),
        ),
        in_specs=[SMEM(), SMEM(), VMEM(), VMEM(), VMEM()],
        out_specs=(VMEM(), VMEM()),
        scratch_shapes=[pltpu.VMEM((heads, heads), jnp.float32)],
        compiler_params=params,
        name="combine",
    )(shard, give_rows, received, home_latent, query_t)
    attended = after_move(home, lax.ppermute(given, "dp", partner))
    return (attended, new_latent)


def solution(mesh):
    placed = (
        P("dp", "tp"),
        P("tp", None),
        P(),
        P("dp", None, None),
        P("dp", "tp", None),
        P("dp", "tp", None),
        P("dp"),
        P("dp", None),
        P("dp"),
        P("dp"),
    )
    return jax.shard_map(
        shards,
        mesh=mesh,
        in_specs=placed,
        out_specs=(P("dp", "tp", None), P("dp", None)),
        check_vma=False,
    )
```

time: 222 us -> 88.4 us (0.40)
  the two profiles are of different devices: /device:TPU:8 before, /device:TPU:16 now
where the time goes in v1:
time: 88.4 us; the launch traced here: 87.9 us
  starting transfers between devices  30.9 us (35%)
  waiting for transfers between devices  24.6 us (28%)
  blocking collectives  13.1 us (15%)
  Pallas kernels  10.1 us (11%)
  local copies, waits for them, and re-layouts  6.18 us (7%)
  other arithmetic  1.79 us (2%)
    all_to_all x1, starting transfers between devices, shards(): lax.all_to_all(outgoing, 'dp', split_axis=0, concat_axis=0, tiled=True)  16.7 us
    all_gather x1, blocking collectives, shards(): parts = lax.all_gather(partial_raw, 'tp')  13.1 us
    all_to_all x1, waiting for transfers between devices, shards(): lax.all_to_all(outbound, 'tp', split_axis=0, concat_axis=0, tiled=True)  9.98 us
    all_to_all x1, waiting for transfers between devices, shards(): lax.all_to_all(outgoing, 'dp', split_axis=0, concat_axis=0, tiled=True)  9.06 us
    unnamed x26, local copies, waits for them, and re-layouts  6.13 us
    ppermute x1, starting transfers between devices, shards(): lax.ppermute(jnp.sum(jnp.where(is_given[:, :, None], home_latent[None].as...  5.68 us
    ppermute x1, waiting for transfers between devices, shards(): attended = after_move(home, lax.ppermute(given, 'dp', partner))  5.54 us
    all_to_all x1, starting transfers between devices, shards(): lax.all_to_all(outbound, 'tp', split_axis=0, concat_axis=0, tiled=True)  4.31 us
  transfers between devices with their start and end apart: 4, of which 3 were waited for; matrix products, arithmetic and copies ran while one was open for 2% of the time, Pallas kernels for 7%

profile of v1, /device:TPU:16, one launch (start us, length us, event | category | flops | bytes accessed | tf_op | source)
XLA Modules:
  0.0 87.9 jit_solution(7469815815233349760)
XLA Ops:
  0.6 0.0 copy-start
  0.7 1.2 %copy-done.6 = bf16[64,8,576]{2,1,0:T(8,128)(2,1)S(1)} copy-done((bf16[64,8,576]{2,1,0:T(8,128)(2,1)S(1)}, bf16[64,8,576]{2,1,0:T(8,128)(2,1)}, u32[]{:S(2)}) %copy-start.6) | copy-done | bytes 589848
  1.8 0.7 copy-done.10
  2.5 2.6 %pack.1 = bf16[64,8,1152]{2,1,0:T(8,128)(2,1)S(1)} custom-call(s32[64]{0:T(128)S(1)} %copy-done.10, bf16[64,8,576]{2,1,0:T(8,128)(2,1)S(1)} %copy-done.6), custom_call_target="tpu_custom_call" | custom-call | tf_op jit(solution)/shard_map/pack/pallas_call | solution.py:221
  5.1 1.0 %copy-done.2 = bf16[64,8,1152]{2,1,0:T(8,128)(2,1)} copy-done((bf16[64,8,1152]{2,1,0:T(8,128)(2,1)}, bf16[64,8,1152]{2,1,0:T(8,128)(2,1)S(1)}, u32[]{:S(2)}) %copy-start.2) | copy-done | bytes 1179672
  6.1 16.7 %all-to-all-start = ((bf16[64,8,1152]{2,1,0:T(8,128)(2,1)}), bf16[64,8,1152]{2,1,0:T(8,128)(2,1)S(1)}, u32[]{:S(2)}, u32[]{:S(2)}) async-start(bf16[64,8,1152]{2,1,0:T(8,128)(2,1)} %copy-done.2), calls=%async_computation | async-start | bytes 2359296 | tf_op jit(solution)/shard_map/all_to_all | solution.py:230
  22.9 0.0 copy-start.12
  22.9 0.0 copy-start.9
  22.9 0.0 copy-start.1
  22.9 0.0 copy-start.7
  22.9 0.0 copy-start.8
  22.9 0.4 convolution_bitcast_fusion
  23.3 13.1 %all-gather.1 = f32[8,4,576]{2,1,0:T(4,128)S(1)} all-gather(f32[1,4,576]{2,1,0:T(4,128)S(1)} %convolution_bitcast_fusion), channel_id=2, replica_groups=mesh['dp'=64,'tp'=8] {'tp'}, dimensions={0}, use_global_device_ids=true | all-gather | bytes 82944 | tf_op jit(solution)/shard_map/all_gather | solution.py:233
  36.4 0.1 multiply_reduce_fusion
  36.6 0.1 multiply_convert_fusion
  36.7 0.1 iota_compare_fusion
  36.7 0.1 select_reduce_fusion
  36.8 5.7 %collective-permute-start.1 = (bf16[2,576]{1,0:T(2,128)(2,1)S(1)}, bf16[2,576]{1,0:T(2,128)(2,1)S(1)}, u32[]{:S(2)}, u32[]{:S(2)}) collective-permute-start(bf16[2,576]{1,0:T(2,128)(2,1)S(1)} %select_reduce_fusion), channel_id=1, source_target_pairs={{0,256},{8,264},{16,272},{24,280},{32,288},{40,296},{48,304},{56,3... | collective-permute-start | bytes 6920 | tf_op jit(solution)/shard_map/ppermute | solution.py:237
  42.6 0.0 copy-start.3
  42.6 1.2 %copy-done.3 = bf16[96,8,576]{2,1,0:T(8,128)(2,1)S(1)} copy-done((bf16[96,8,576]{2,1,0:T(8,128)(2,1)S(1)}, bf16[96,8,576]{2,1,0:T(8,128)(2,1)}, u32[]{:S(2)}) %copy-start.3) | copy-done | bytes 884760
  43.8 2.1 %resident.1 = (f32[4,192,128]{2,1,0:T(8,128)S(1)}, bf16[4,192,512]{2,1,0:T(8,128)(2,1)S(1)}) custom-call(s32[4,40]{1,0:T(4,128)S(1)} %copy-done.7, s32[4]{0:T(128)S(1)} %copy-done.8, bf16[96,8,576]{2,1,0:T(8,128)(2,1)S(1)} %copy-done.3, bf16[4,576,128]{2,1,0:T(8,128)(2,1)S(1)} %bitcast.14), custom_call_target="tpu_custom_call" | custom-call | tf_op jit(solution)/shard_map/resident/pallas_call | solution.py:251
  45.9 0.9 %copy-done.4 = bf16[4,192,512]{2,1,0:T(8,128)(2,1)} copy-done((bf16[4,192,512]{2,1,0:T(8,128)(2,1)}, bf16[4,192,512]{2,1,0:T(8,128)(2,1)S(1)}, u32[]{:S(2)}) %copy-start.4) | copy-done | bytes 786456
  46.8 9.1 %all-to-all-done.arrived_ref = bf16[64,8,1152]{2,1,0:T(8,128)(2,1)S(1)} async-done(((bf16[64,8,1152]{2,1,0:T(8,128)(2,1)}), bf16[64,8,1152]{2,1,0:T(8,128)(2,1)S(1)}, u32[]{:S(2)}, u32[]{:S(2)}) %all-to-all-start) | async-done | bytes 1179680 | tf_op jit(solution)/shard_map/all_to_all | solution.py:230
  55.9 1.1 %copy-done.5 = bf16[4,192,512]{2,1,0:T(8,128)(2,1)S(1)} copy-done((bf16[4,192,512]{2,1,0:T(8,128)(2,1)S(1)}, bf16[4,192,512]{2,1,0:T(8,128)(2,1)}, u32[]{:S(2)}) %copy-start.5) | copy-done | bytes 786456
  57.0 4.3 %arrived.1 = bf16[8,272,128]{2,1,0:T(8,128)(2,1)} custom-call(s32[1]{0:T(128)} %bitcast.1.shard_ref, s32[4,40]{1,0:T(4,128)S(1)} %copy-done.7, s32[4]{0:T(128)S(1)} %copy-done.8, bf16[64,8,1152]{2,1,0:T(8,128)(2,1)S(1)} %all-to-all-done.arrived_ref, bf16[4,576,128]{2,1,0:T(8,128)(2,1)S(1)} %bitcast.15, f32[4,192,128]{2,1,0:T(8,128)S(1)} %get-tuple-element.6.score_ref, ...), custom_call_target="tpu_custom_call" | custom-call | tf_op jit(solution)/shard_map/arrived/pallas_call | solution.py:265
  61.3 4.3 %all-to-all-start.1 = ((bf16[8,272,128]{2,1,0:T(8,128)(2,1)}), bf16[8,272,128]{2,1,0:T(8,128)(2,1)S(1)}, u32[]{:S(2)}, u32[]{:S(2)}) async-start(bf16[8,272,128]{2,1,0:T(8,128)(2,1)} %arrived.1), calls=%async_computation.1 | async-start | bytes 1114112 | tf_op jit(solution)/shard_map/all_to_all | solution.py:278
  65.7 0.7 select_select_fusion.1
  66.4 10.0 %all-to-all-done.1.received_ref = bf16[8,272,128]{2,1,0:T(8,128)(2,1)S(1)} async-done(((bf16[8,272,128]{2,1,0:T(8,128)(2,1)}), bf16[8,272,128]{2,1,0:T(8,128)(2,1)S(1)}, u32[]{:S(2)}, u32[]{:S(2)}) %all-to-all-start.1) | async-done | bytes 557088 | tf_op jit(solution)/shard_map/all_to_all | solution.py:278
  76.3 1.1 %combine.1 = (bf16[4,16,512]{2,1,0:T(8,128)(2,1)S(1)}, bf16[2,16,512]{2,1,0:T(8,128)(2,1)S(1)}) custom-call(s32[1]{0:T(128)} %bitcast.1.shard_ref, s32[2]{0:T(128)S(1)} %copy-done.9, bf16[8,272,128]{2,1,0:T(8,128)(2,1)S(1)} %all-to-all-done.1.received_ref, bf16[4,576]{1,0:T(4,128)(2,1)S(1)} %get-tuple-element.15.latent_ref, bf16[4,576,128]{2,1,0:T(8,128)(2,1)S(1)} %bitcast.16), custom_call_target="tpu_custom_call" | custom-call | tf_op jit(solution)/shard_map/combine/pallas_call | solution.py:280
  77.4 4.2 %collective-permute-start = (bf16[2,16,512]{2,1,0:T(8,128)(2,1)S(1)}, bf16[2,16,512]{2,1,0:T(8,128)(2,1)S(1)}, u32[]{:S(2)}, u32[]{:S(2)}) collective-permute-start(bf16[2,16,512]{2,1,0:T(8,128)(2,1)S(1)} %get-tuple-element.8), channel_id=1, source_target_pairs={{0,256},{8,264},{16,272},{24,280},{32,288},{40,296},{48,304},{56,3... | collective-permute-start | bytes 98312 | tf_op jit(solution)/shard_map/ppermute | solution.py:292
  81.6 5.5 %collective-permute-done = bf16[2,16,512]{2,1,0:T(8,128)(2,1)S(1)} collective-permute-done((bf16[2,16,512]{2,1,0:T(8,128)(2,1)S(1)}, bf16[2,16,512]{2,1,0:T(8,128)(2,1)S(1)}, u32[]{:S(2)}, u32[]{:S(2)}) %collective-permute-start) | collective-permute-done | bytes 32800 | tf_op jit(solution)/shard_map/ppermute | solution.py:292
  87.2 0.7 select_select_fusion
  (21 shorter events, 0.1 us)
Async XLA Ops:
  0.6 22.2 %copy-start = (bf16[896,576]{0,1:T(8,128)(2,1)S(1)}, bf16[896,576]{0,1:T(8,128)(2,1)}, u32[]{:S(2)}) copy-start(bf16[896,576]{0,1:T(8,128)(2,1)} %param.11) | copy-start | bytes 3096580
  0.6 1.2 %copy-start.6 = (bf16[64,8,576]{2,1,0:T(8,128)(2,1)S(1)}, bf16[64,8,576]{2,1,0:T(8,128)(2,1)}, u32[]{:S(2)}) copy-start(bf16[64,8,576]{2,1,0:T(8,128)(2,1)} %outbox_ref.1) | copy-start | bytes 1769476
  1.8 0.7 copy-start.10
  5.1 1.0 %copy-start.2 = (bf16[64,8,1152]{2,1,0:T(8,128)(2,1)}, bf16[64,8,1152]{2,1,0:T(8,128)(2,1)S(1)}, u32[]{:S(2)}) copy-start(bf16[64,8,1152]{2,1,0:T(8,128)(2,1)S(1)} %pack.1) | copy-start | bytes 3538948
  6.1 16.8 %copy-start.11 = (bf16[4,896]{1,0:T(4,128)(2,1)S(1)}, bf16[4,896]{1,0:T(4,128)(2,1)}, u32[]{:S(2)}) copy-start(bf16[4,896]{1,0:T(4,128)(2,1)} %param.10) | copy-start | bytes 21508
  6.1 49.8 %all-to-all-start = ((bf16[64,8,1152]{2,1,0:T(8,128)(2,1)}), bf16[64,8,1152]{2,1,0:T(8,128)(2,1)S(1)}, u32[]{:S(2)}, u32[]{:S(2)}) async-start(bf16[64,8,1152]{2,1,0:T(8,128)(2,1)} %copy-done.2), calls=%async_computation | async-start | bytes 2359296 | tf_op jit(solution)/shard_map/all_to_all | solution.py:230
  22.9 13.7 %copy-start.12 = (f32[512]{0:T(512)S(1)}, f32[512]{0:T(512)}, u32[]{:S(2)}) copy-start(f32[512]{0:T(512)} %param.12) | copy-start | bytes 6148
  22.9 13.8 %copy-start.9 = (s32[2]{0:T(128)S(1)}, s32[2]{0:T(128)}, u32[]{:S(2)}) copy-start(s32[2]{0:T(128)} %give_ref.1) | copy-start | bytes 28
  22.9 19.7 %copy-start.1 = (bf16[4,128,576]{1,2,0:T(8,128)(2,1)S(1)}, bf16[4,128,576]{1,2,0:T(8,128)(2,1)}, u32[]{:S(2)}) copy-start(bf16[4,128,576]{1,2,0:T(8,128)(2,1)} %param.13) | copy-start | bytes 1769476
  22.9 19.7 %copy-start.7 = (s32[4,40]{1,0:T(4,128)S(1)}, s32[4,40]{1,0:T(4,128)}, u32[]{:S(2)}) copy-start(s32[4,40]{1,0:T(4,128)} %table_ref.3) | copy-start | bytes 1924
  22.9 19.7 %copy-start.8 = (s32[4]{0:T(128)S(1)}, s32[4]{0:T(128)}, u32[]{:S(2)}) copy-start(s32[4]{0:T(128)} %length_ref.3) | copy-start | bytes 52
  36.8 28.8 %collective-permute-start.1 = (bf16[2,576]{1,0:T(2,128)(2,1)S(1)}, bf16[2,576]{1,0:T(2,128)(2,1)S(1)}, u32[]{:S(2)}, u32[]{:S(2)}) collective-permute-start(bf16[2,576]{1,0:T(2,128)(2,1)S(1)} %select_reduce_fusion), channel_id=1, source_target_pairs={{0,256},{8,264},{16,272},{24,280},{32,288},{40,296},{48,304},{56,3... | collective-permute-start | bytes 6920 | tf_op jit(solution)/shard_map/ppermute | solution.py:237
  42.6 1.2 %copy-start.3 = (bf16[96,8,576]{2,1,0:T(8,128)(2,1)S(1)}, bf16[96,8,576]{2,1,0:T(8,128)(2,1)}, u32[]{:S(2)}) copy-start(bf16[96,8,576]{2,1,0:T(8,128)(2,1)} %cache_ref.1) | copy-start | bytes 2654212
  45.9 0.9 %copy-start.4 = (bf16[4,192,512]{2,1,0:T(8,128)(2,1)}, bf16[4,192,512]{2,1,0:T(8,128)(2,1)S(1)}, u32[]{:S(2)}) copy-start(bf16[4,192,512]{2,1,0:T(8,128)(2,1)S(1)} %get-tuple-element.7.value_ref) | copy-start | bytes 2359300
  55.9 1.1 %copy-start.5 = (bf16[4,192,512]{2,1,0:T(8,128)(2,1)S(1)}, bf16[4,192,512]{2,1,0:T(8,128)(2,1)}, u32[]{:S(2)}) copy-start(bf16[4,192,512]{2,1,0:T(8,128)(2,1)} %copy-done.4) | copy-start | bytes 2359300
  61.3 15.0 %all-to-all-start.1 = ((bf16[8,272,128]{2,1,0:T(8,128)(2,1)}), bf16[8,272,128]{2,1,0:T(8,128)(2,1)S(1)}, u32[]{:S(2)}, u32[]{:S(2)}) async-start(bf16[8,272,128]{2,1,0:T(8,128)(2,1)} %arrived.1), calls=%async_computation.1 | async-start | bytes 1114112 | tf_op jit(solution)/shard_map/all_to_all | solution.py:278
  77.4 9.7 %collective-permute-start = (bf16[2,16,512]{2,1,0:T(8,128)(2,1)S(1)}, bf16[2,16,512]{2,1,0:T(8,128)(2,1)S(1)}, u32[]{:S(2)}, u32[]{:S(2)}) collective-permute-start(bf16[2,16,512]{2,1,0:T(8,128)(2,1)S(1)} %get-tuple-element.8), channel_id=1, source_target_pairs={{0,256},{8,264},{16,272},{24,280},{32,288},{40,296},{48,304},{56,3... | collective-permute-start | bytes 98312 | tf_op jit(solution)/shard_map/ppermute | solution.py:292

commit v2 on v0

v2 whole, which is shorter than its diff:
```python
import functools

import jax
import jax.numpy as jnp
from jax import lax
from jax.experimental import pallas as pl
from jax.experimental.pallas import tpu as pltpu
from jax.sharding import PartitionSpec as P

KVL = 512
PAGE = 64
CAP = 2
ARR = 16
RESMAX = 24
MAXROWS = 4
MOVES = 2
ROPE = 64
RES_POOL = 96


EPSILON = 1e-06
SCORE_SCALE = 192.0 ** (-0.5)
VMEM_LIMIT = 32 * 1024 * 1024

SMEM = functools.partial(pl.BlockSpec, memory_space=pltpu.SMEM)
VMEM = functools.partial(pl.BlockSpec, memory_space=pltpu.VMEM)


def normalize(raw_latent, kv_gain):
    head_part = raw_latent[:, :KVL]
    inverse = lax.rsqrt(jnp.mean(head_part * head_part, axis=1, keepdims=True) + EPSILON)
    return jnp.concatenate(
        [head_part * inverse * kv_gain[None, :], raw_latent[:, KVL:]], axis=1
    ).astype(jnp.bfloat16)


def served_order(give_ref):
    first, second = give_ref[0], give_ref[1]
    low, high = jnp.minimum(first, second), jnp.maximum(first, second)
    kept_low = jnp.where(low > 0, 0, jnp.where(high > 1, 1, 2))
    kept_high = jnp.where(high < 3, 3, jnp.where(low < 2, 2, 1))
    return [first, second, kept_low, kept_high]


def resident_count(length):
    return (length + (PAGE - 1)) // PAGE - ARR


def across(a, b):
    return lax.dot_general(a, b, (((1,), (1,)), ((), ())), preferred_element_type=jnp.float32)


def pack_kernel(dest_ref, outbox_ref, out_ref, page_ref, stage_ref, index_ref, in_sems, out_sems):
    sent, groups = outbox_ref.shape[0], out_ref.shape[0]
    parts = in_sems.shape[0]
    step = sent // parts
    loads = [
        pltpu.make_async_copy(outbox_ref.at[pl.ds(i * step, step)], page_ref.at[pl.ds(i * step, step)], in_sems.at[i])
        for i in range(parts)
    ]
    for load in loads:
        load.start()
    page_ref[sent] = jnp.zeros_like(page_ref[sent])
    for i in range(groups * CAP):
        index_ref[i] = sent
    for i in range(sent):
        slot = dest_ref[i] * CAP
        index_ref[slot + (index_ref[slot] != sent).astype(jnp.int32)] = i
    for load in loads:
        load.wait()
    block = groups // out_sems.shape[0]
    stores = []
    for part in range(out_sems.shape[0]):
        for dest in range(part * block, (part + 1) * block):
            for rank in range(CAP):
                page = page_ref.at[index_ref[dest * CAP + rank]]
                stage_ref[dest, :, rank * KVL : (rank + 1) * KVL] = page[:, :KVL]
                stage_ref[dest, :, CAP * KVL + rank * ROPE : CAP * KVL + (rank + 1) * ROPE] = page[:, KVL:]
        span = pl.ds(part * block, block)
        store = pltpu.make_async_copy(stage_ref.at[span], out_ref.at[span], out_sems.at[part])
        store.start()
        stores.append(store)
    for store in stores:
        store.wait()


def resident_kernel(
    give_ref, table_ref, length_ref, cache_ref, query_ref, query_give, query_keep, blend_give, blend_keep, stat_ref, key_ref
):
    piece = cache_ref.shape[1]
    lane = lax.broadcasted_iota(jnp.int32, stat_ref.shape, 1)
    stats = jnp.zeros(stat_ref.shape, jnp.float32)
    for place, row in enumerate(served_order(give_ref)):
        count = resident_count(length_ref[row])
        for pair in range(RESMAX // 2):
            parts = []
            for half in range(2):
                entry = pair * 2 + half
                parts.append(cache_ref[table_ref[row, jnp.where(entry < count, entry, 0)]])
            key_ref[place, pair * 2 * piece : (pair + 1) * 2 * piece, :] = jnp.concatenate(parts, axis=0)
        query_t = query_ref[row].astype(jnp.float32)
        query = jnp.concatenate([query_t, query_t[KVL:]], axis=0).T.astype(jnp.bfloat16)
        queries, blends = (query_give, blend_give) if place < MOVES else (query_keep, blend_keep)
        queries[place % MOVES] = query
        keys = key_ref[place]
        scores = SCORE_SCALE * across(query[:, : KVL + ROPE], keys)
        token = lax.broadcasted_iota(jnp.int32, scores.shape, 1)
        scores = jnp.where(token < count * piece, scores, -jnp.inf)
        top = jnp.max(scores, axis=1, keepdims=True)
        weights = jnp.exp(scores - top)
        total = jnp.sum(weights, axis=1, keepdims=True)
        blends[place % MOVES] = jnp.dot(weights.astype(jnp.bfloat16), keys[:, :KVL], preferred_element_type=jnp.float32)
        stats = jnp.where(lane == place, top, jnp.where(lane == MAXROWS + place, total, stats))
    stat_ref[...] = stats


def own_kernel(latent_ref, query_give, query_keep, own_ref):
    lane = lax.broadcasted_iota(jnp.int32, own_ref.shape[1:], 1)
    latents = latent_ref[...]
    for part, queries in enumerate((query_give, query_keep)):
        own = jnp.zeros(own_ref.shape[1:], jnp.float32)
        for move in range(MOVES):
            place = part * MOVES + move
            scores = SCORE_SCALE * across(queries[move][:, : KVL + ROPE], latents)
            own = jnp.where(lane == move, scores[:, place : place + 1], own)
        own_ref[part] = own


def arrived_kernel(
    base, shard_ref, give_ref, table_ref, length_ref, arrived_ref, query_ref, blend_ref, stat_ref, send_ref
):
    shards, piece = send_ref.shape[0], arrived_ref.shape[1]
    rows, heads, _ = query_ref.shape
    own = heads // shards
    lane = lax.broadcasted_iota(jnp.int32, (heads, 128), 1)
    page_lane = lax.broadcasted_iota(jnp.int32, (piece, 128), 1)
    stats = jnp.zeros((heads, 128), jnp.float32)
    order = served_order(give_ref)
    keys, ropes = [], []
    for move in range(rows):
        row = order[base + move]
        count = resident_count(length_ref[row])
        latent_parts, rope_parts = [], []
        for entry in range(ARR):
            slot = table_ref[row, count + entry] - RES_POOL
            source, rank = slot // CAP, lax.rem(slot, CAP)
            latent_parts.append(arrived_ref[source, :, pl.ds(pl.multiple_of(rank * KVL, KVL), KVL)])
            both = arrived_ref[source, :, CAP * KVL : CAP * KVL + 128].astype(jnp.float32)
            rope_parts.append(jnp.where(page_lane // ROPE == rank, both, 0.0))
        keys.append(jnp.concatenate(latent_parts, axis=0))
        ropes.append(jnp.concatenate(rope_parts, axis=0).astype(jnp.bfloat16))
    for move in range(rows):
        row = order[base + move]
        length = length_ref[row]
        count = resident_count(length)
        query = query_ref[move]
        scores = SCORE_SCALE * (across(query[:, :KVL], keys[move]) + across(query[:, KVL:], ropes[move]))
        token = lax.broadcasted_iota(jnp.int32, scores.shape, 1)
        position = (count + token // piece) * PAGE + shard_ref[0] * piece + lax.rem(token, piece)
        scores = jnp.where(position < length, scores, -jnp.inf)
        old_top = stat_ref[:, base + move : base + move + 1]
        old_total = stat_ref[:, MAXROWS + base + move : MAXROWS + base + move + 1]
        top = jnp.maximum(jnp.max(scores, axis=1, keepdims=True), old_top)
        weights = jnp.exp(scores - top)
        shrink = jnp.exp(old_top - top)
        total = jnp.sum(weights, axis=1, keepdims=True) + shrink * old_total
        blend = jnp.dot(weights.astype(jnp.bfloat16), keys[move], preferred_element_type=jnp.float32)
        partial = ((blend + shrink * blend_ref[move]) * (1.0 / total)).astype(jnp.bfloat16)
        for shard_to in range(shards):
            for chunk in range(KVL // 128):
                start = (chunk * rows + move) * own
                send_ref[shard_to, start : start + own, :] = partial[
                    shard_to * own : (shard_to + 1) * own, chunk * 128 : (chunk + 1) * 128
                ]
        level = top + jnp.log(total)
        for piece_of in range(3):
            rounded = level.astype(jnp.bfloat16).astype(jnp.float32)
            stats = jnp.where(lane == piece_of * rows + move, rounded, stats)
            level = level - rounded
    coded = stats.astype(jnp.bfloat16)
    for shard_to in range(shards):
        send_ref[shard_to, KVL // 128 * rows * own :, :] = coded[shard_to * own : (shard_to + 1) * own]


def combined(base, shard_ref, received_ref, latent_ref, own_ref):
    shards = received_ref.shape[0]
    own = own_ref.shape[1] // shards
    stat_base = received_ref.shape[1] - own
    level_own = own_ref[base // MOVES, pl.ds(pl.multiple_of(shard_ref[0] * own, own), own), :]
    levels = []
    for share in range(shards):
        stats = received_ref[share, stat_base:, :].astype(jnp.float32)
        levels.append(stats + pltpu.roll(stats, 128 - MOVES, 1) + pltpu.roll(stats, 128 - 2 * MOVES, 1))
    peak = functools.reduce(jnp.maximum, levels, level_own)
    weights = [jnp.exp(level - peak) for level in levels] + [jnp.exp(level_own - peak)]
    inverse = 1.0 / functools.reduce(lambda a, b: a + b, weights)
    weights = [weight * inverse for weight in weights]
    results = []
    for move in range(MOVES):
        columns = [jnp.broadcast_to(weight[:, move : move + 1], weight.shape) for weight in weights]
        chunks = []
        for chunk in range(KVL // 128):
            value = columns[-1] * latent_ref[base + move : base + move + 1, chunk * 128 : (chunk + 1) * 128].astype(jnp.float32)
            start = (chunk * MOVES + move) * own
            for share in range(shards):
                value += columns[share] * received_ref[share, start : start + own, :].astype(jnp.float32)
            chunks.append(value.astype(jnp.bfloat16))
        results.append(jnp.concatenate(chunks, axis=1))
    return results


def give_kernel(shard_ref, received_ref, latent_ref, own_ref, out_ref):
    for move, result in enumerate(combined(0, shard_ref, received_ref, latent_ref, own_ref)):
        out_ref[move] = result


def keep_kernel(shard_ref, give_ref, received_ref, latent_ref, own_ref, taken_ref, out_ref):
    order = served_order(give_ref)
    for move, result in enumerate(combined(MOVES, shard_ref, received_ref, latent_ref, own_ref)):
        out_ref[order[MOVES + move]] = result
    for move in range(MOVES):
        out_ref[order[move]] = taken_ref[move]


def shards(
    hidden,
    kva_weight,
    kv_gain,
    queries,
    latent_cache,
    outbox,
    out_dest,
    page_table,
    lengths,
    give_rows,
):
    group_count = lax.axis_size("dp")
    shard_count = lax.axis_size("tp")
    shard = lax.axis_index("tp").astype(jnp.int32).reshape(1)
    row_count = hidden.shape[0]
    page_piece = latent_cache.shape[1]
    heads = queries.shape[1]
    own = heads // shard_count
    moves = give_rows.shape[0]
    query_t = jnp.swapaxes(queries, 1, 2)
    kept = row_count - moves
    wide = KVL + 2 * ROPE
    params = pltpu.CompilerParams(vmem_limit_bytes=VMEM_LIMIT)
    shape = jax.ShapeDtypeStruct

    outgoing = pl.pallas_call(
        pack_kernel,
        out_shape=shape((group_count, page_piece, CAP * (KVL + ROPE)), jnp.bfloat16),
        in_specs=[SMEM(), pl.BlockSpec(memory_space=pltpu.HBM)],
        out_specs=pl.BlockSpec(memory_space=pl.ANY),
        scratch_shapes=[
            pltpu.VMEM((outbox.shape[0] + 1,) + outbox.shape[1:], jnp.bfloat16),
            pltpu.VMEM((group_count, page_piece, CAP * (KVL + ROPE)), jnp.bfloat16),
            pltpu.SMEM((group_count * CAP,), jnp.int32),
            pltpu.SemaphoreType.DMA((8,)),
            pltpu.SemaphoreType.DMA((8,)),
        ],
        compiler_params=params,
        name="pack",
    )(out_dest, pltpu.with_memory_space_constraint(outbox, pltpu.HBM))
    arrived = lax.all_to_all(outgoing, "dp", split_axis=0, concat_axis=0, tiled=True)

    partial_raw = jnp.dot(hidden, kva_weight, preferred_element_type=jnp.float32)
    parts = lax.all_gather(partial_raw, "tp")
    home_latent = normalize(jnp.sum(parts, axis=0), kv_gain).astype(jnp.float32)
    partner = [(i, i ^ (group_count // 2)) for i in range(group_count)]
    row_ids = lax.broadcasted_iota(jnp.int32, (moves, row_count), 1)
    is_given = row_ids == give_rows[:, None]
    given = is_given[0] | is_given[1]
    kept_rank = jnp.cumsum(jnp.where(given, 0, 1)) - 1
    is_kept = jnp.logical_not(given)[None, :] & (kept_rank[None, :] == lax.broadcasted_iota(jnp.int32, (kept, row_count), 0))
    served = jnp.concatenate([is_given, is_kept, jnp.zeros((8 - row_count, row_count), jnp.bool_)], axis=0)
    latent = jnp.sum(jnp.where(served[:, :, None], home_latent[None], 0.0), axis=1).astype(jnp.bfloat16)
    moved_latent = lax.ppermute(latent[:moves], "dp", partner)
    new_latent = home_latent.astype(jnp.bfloat16)
    for move in range(moves):
        new_latent = jnp.where(is_given[move][:, None], moved_latent[move][None], new_latent)

    query_give, query_keep, blend_give, blend_keep, stats = pl.pallas_call(
        resident_kernel,
        out_shape=(
            shape((moves, heads, wide), jnp.bfloat16),
            shape((kept, heads, wide), jnp.bfloat16),
            shape((moves, heads, KVL), jnp.float32),
            shape((kept, heads, KVL), jnp.float32),
            shape((heads, 128), jnp.float32),
        ),
        in_specs=[SMEM(), SMEM(), SMEM(), VMEM(), VMEM()],
        out_specs=(VMEM(),) * 5,
        scratch_shapes=[pltpu.VMEM((row_count, RESMAX * page_piece, latent_cache.shape[2]), jnp.bfloat16)],
        compiler_params=params,
        name="resident",
    )(give_rows, page_table, lengths, latent_cache, query_t)
    own_scores = pl.pallas_call(
        own_kernel,
        out_shape=shape((2, heads, 128), jnp.float32),
        in_specs=[VMEM()] * 3,
        out_specs=VMEM(),
        compiler_params=params,
        name="own",
    )(latent, query_give, query_keep)

    def attend(base, query, blend, stats):
        return pl.pallas_call(
            functools.partial(arrived_kernel, base),
            out_shape=shape((shard_count, (KVL // 128 * moves + 1) * own, 128), jnp.bfloat16),
            in_specs=[SMEM()] * 4 + [VMEM()] * 4,
            out_specs=VMEM(),
            compiler_params=params,
            name="arrived",
        )(shard, give_rows, page_table, lengths, arrived, query, blend, stats)

    def swap(part):
        return lax.all_to_all(part, "tp", split_axis=0, concat_axis=0, tiled=True)

    send_give, stats = lax.optimization_barrier((attend(0, query_give, blend_give, stats), stats))
    received_give = swap(send_give)
    send_keep = attend(moves, query_keep, blend_keep, stats)
    handed = pl.pallas_call(
        give_kernel,
        out_shape=shape((moves, own, KVL), jnp.bfloat16),
        in_specs=[SMEM()] + [VMEM()] * 3,
        out_specs=VMEM(),
        compiler_params=params,
        name="give",
    )(shard, received_give, latent, own_scores)
    handed, send_keep = lax.optimization_barrier((handed, send_keep))
    taken = lax.ppermute(handed, "dp", partner)
    received_keep = swap(send_keep)
    attended = pl.pallas_call(
        keep_kernel,
        out_shape=shape((row_count, own, KVL), jnp.bfloat16),
        in_specs=[SMEM()] * 2 + [VMEM()] * 4,
        out_specs=VMEM(),
        compiler_params=params,
        name="keep",
    )(shard, give_rows, received_keep, latent, own_scores, taken)
    return (attended, new_latent)


def solution(mesh):
    placed = (
        P("dp", "tp"),
        P("tp", None),
        P(),
        P("dp", None, None),
        P("dp", "tp", None),
        P("dp", "tp", None),
        P("dp"),
        P("dp", None),
        P("dp"),
        P("dp"),
    )
    return jax.shard_map(
        shards,
        mesh=mesh,
        in_specs=placed,
        out_specs=(P("dp", "tp", None), P("dp", None)),
        check_vma=False,
    )
```

time: 222 us -> 87 us (0.39)
  the two profiles are of different devices: /device:TPU:8 before, /device:TPU:2 now
where the time goes in v2:
time: 87 us; the launch traced here: 86.4 us
  starting transfers between devices  36 us (41%)
  waiting for transfers between devices  16.5 us (19%)
  blocking collectives  12.8 us (15%)
  Pallas kernels  11.2 us (13%)
  local copies, waits for them, and re-layouts  6.69 us (8%)
  other arithmetic  1.92 us (2%)
    all_to_all x1, starting transfers between devices, shards(): lax.all_to_all(outgoing, 'dp', split_axis=0, concat_axis=0, tiled=True)  16.6 us
    all_gather x1, blocking collectives, shards(): parts = lax.all_gather(partial_raw, 'tp')  12.8 us
    all_to_all x1, waiting for transfers between devices, shards(): lax.all_to_all(outgoing, 'dp', split_axis=0, concat_axis=0, tiled=True)  11.6 us
    all_to_all x2, starting transfers between devices, swap(): return lax.all_to_all(part, 'tp', split_axis=0, concat_axis=0, tiled=True)  9.65 us
    ppermute x1, starting transfers between devices, shards(): moved_latent = lax.ppermute(latent[:moves], 'dp', partner)  5.62 us
    unnamed x34, local copies, waits for them, and re-layouts  5.37 us
    ppermute x1, waiting for transfers between devices, shards(): taken = lax.ppermute(handed, 'dp', partner)  4.91 us
    ppermute x1, starting transfers between devices, shards(): taken = lax.ppermute(handed, 'dp', partner)  4.13 us
  transfers between devices with their start and end apart: 5, of which 2 were waited for; matrix products, arithmetic and copies ran while one was open for 4% of the time, Pallas kernels for 6%

profile of v2, /device:TPU:2, one launch (start us, length us, event | category | flops | bytes accessed | tf_op | source)
XLA Modules:
  0.0 86.4 jit_solution(788432907297156155)
XLA Ops:
  0.7 0.7 copy-done.11
  1.4 2.9 %pack.1 = bf16[64,8,1152]{2,1,0:T(8,128)(2,1)} custom-call(s32[64]{0:T(128)S(1)} %copy-done.11, bf16[64,8,576]{2,1,0:T(8,128)(2,1)} %outbox_ref.1), custom_call_target="tpu_custom_call" | custom-call | tf_op jit(solution)/shard_map/pack/pallas_call | solution.py:251
  4.4 16.6 %all-to-all-start = ((bf16[64,8,1152]{2,1,0:T(8,128)(2,1)}), bf16[64,8,1152]{2,1,0:T(8,128)(2,1)S(1)}, u32[]{:S(2)}, u32[]{:S(2)}) async-start(bf16[64,8,1152]{2,1,0:T(8,128)(2,1)} %pack.1), calls=%async_computation | async-start | bytes 2359296 | tf_op jit(solution)/shard_map/all_to_all | solution.py:266
  21.0 0.1 iota_compare_fusion.1
  21.1 0.6 copy.12
  21.7 0.7 pad.4.clone
  22.4 0.4 convolution_bitcast_fusion
  22.8 12.8 %all-gather.1 = f32[8,4,576]{2,1,0:T(4,128)S(1)} all-gather(f32[1,4,576]{2,1,0:T(4,128)S(1)} %convolution_bitcast_fusion), channel_id=2, replica_groups=mesh['dp'=64,'tp'=8] {'tp'}, dimensions={0}, use_global_device_ids=true | all-gather | bytes 82944 | tf_op jit(solution)/shard_map/all_gather | solution.py:269
  35.6 0.7 reduce-window.8
  36.3 1.2 %copy-done.2 = bf16[96,8,576]{2,1,0:T(8,128)(2,1)S(1)} copy-done((bf16[96,8,576]{2,1,0:T(8,128)(2,1)S(1)}, bf16[96,8,576]{2,1,0:T(8,128)(2,1)}, u32[]{:S(2)}) %copy-start.2) | copy-done | bytes 884760
  37.5 2.1 %resident.1 = (bf16[2,128,640]{2,1,0:T(8,128)(2,1)S(1)}, bf16[2,128,640]{2,1,0:T(8,128)(2,1)S(1)}, f32[2,128,512]{2,1,0:T(8,128)S(1)}, f32[2,128,512]{2,1,0:T(8,128)S(1)}, f32[128,128]{1,0:T(8,128)S(1)}) custom-call(s32[2]{0:T(128)S(1)} %copy-done.9, s32[4,40]{1,0:T(4,128)S(1)} %copy-done.8, s32[4]{0:T(128)S(1)} %copy-done.10, ...), custom_call_target="tpu_custom_call" | custom-call | tf_op jit(solution)/shard_map/resident/pallas_call | solution.py:284
  39.6 0.8 copy-done.4
  40.4 0.8 copy-done.6
  41.3 0.1 multiply_reduce_fusion
  41.4 0.1 fusion
  41.5 0.1 multiply_convert_fusion
  41.6 11.6 %all-to-all-done.arrived_ref = bf16[64,8,1152]{2,1,0:T(8,128)(2,1)S(1)} async-done(((bf16[64,8,1152]{2,1,0:T(8,128)(2,1)}), bf16[64,8,1152]{2,1,0:T(8,128)(2,1)S(1)}, u32[]{:S(2)}, u32[]{:S(2)}) %all-to-all-start) | async-done | bytes 1179680 | tf_op jit(solution)/shard_map/all_to_all | solution.py:266
  53.2 1.0 %copy-done.7 = f32[2,128,512]{2,1,0:T(8,128)S(1)} copy-done((f32[2,128,512]{2,1,0:T(8,128)S(1)}, f32[2,128,512]{2,1,0:T(8,128)}, u32[]{:S(2)}) %copy-start.7) | copy-done | bytes 524312
  54.2 1.7 %arrived.2 = bf16[8,144,128]{2,1,0:T(8,128)(2,1)S(1)} custom-call(s32[1]{0:T(128)} %bitcast.shard_ref, s32[2]{0:T(128)S(1)} %copy-done.9, s32[4,40]{1,0:T(4,128)S(1)} %copy-done.8, s32[4]{0:T(128)S(1)} %copy-done.10, bf16[64,8,1152]{2,1,0:T(8,128)(2,1)S(1)} %all-to-all-done.arrived_ref, bf16[2,128,640]{2,1,0:T(8,128)(2,1)S(1)} %get-tuple-element.11.query_ref.query_give, ...), custom_call_target="tpu_custom_call" | custom-call | tf_op jit(solution)/shard_map/arrived/pallas_call | solution.py:309
  55.9 0.7 copy-done.1
  56.6 4.8 %all-to-all-start.1 = ((bf16[8,144,128]{2,1,0:T(8,128)(2,1)}), bf16[8,144,128]{2,1,0:T(8,128)(2,1)S(1)}, u32[]{:S(2)}, u32[]{:S(2)}) async-start(bf16[8,144,128]{2,1,0:T(8,128)(2,1)} %copy-done.1), calls=%async_computation.1 | async-start | bytes 589824 | tf_op jit(solution)/shard_map/all_to_all | solution.py:319
  61.5 0.1 add_add_fusion
  61.6 0.1 select_reduce_fusion.latent_ref
  61.7 5.6 %collective-permute-start.1 = (bf16[2,576]{1,0:T(2,128)(2,1)S(1)}, bf16[2,576]{1,0:T(2,128)(2,1)S(1)}, u32[]{:S(2)}, u32[]{:S(2)}) collective-permute-start(bf16[2,576]{1,0:T(2,128)(2,1)S(1)} %slice.33), channel_id=1, source_target_pairs={{0,256},{8,264},{16,272},{24,280},{32,288},{40,296},{48,304},{56,3... | collective-permute-start | bytes 6920 | tf_op jit(solution)/shard_map/ppermute | solution.py:279
  67.3 0.4 own.1.own_ref
  67.7 2.4 %arrived.3 = bf16[8,144,128]{2,1,0:T(8,128)(2,1)} custom-call(s32[1]{0:T(128)} %bitcast.shard_ref, s32[2]{0:T(128)S(1)} %copy-done.9, s32[4,40]{1,0:T(4,128)S(1)} %copy-done.8, s32[4]{0:T(128)S(1)} %copy-done.10, bf16[64,8,1152]{2,1,0:T(8,128)(2,1)S(1)} %all-to-all-done.arrived_ref, bf16[2,128,640]{2,1,0:T(8,128)(2,1)S(1)} %get-tuple-element.15.query_keep.query_ref, ...), custom_call_target="tpu_custom_call" | custom-call | tf_op jit(solution)/shard_map/arrived/pallas_call | solution.py:309
  70.1 0.2 give.1
  70.4 4.8 %all-to-all-start.2 = ((bf16[8,144,128]{2,1,0:T(8,128)(2,1)}), bf16[8,144,128]{2,1,0:T(8,128)(2,1)S(1)}, u32[]{:S(2)}, u32[]{:S(2)}) async-start(bf16[8,144,128]{2,1,0:T(8,128)(2,1)} %arrived.3), calls=%async_computation.2 | async-start | bytes 589824 | tf_op jit(solution)/shard_map/all_to_all | solution.py:319
  75.2 4.1 %collective-permute-start = (bf16[2,16,512]{2,1,0:T(8,128)(2,1)S(1)}, bf16[2,16,512]{2,1,0:T(8,128)(2,1)S(1)}, u32[]{:S(2)}, u32[]{:S(2)}) collective-permute-start(bf16[2,16,512]{2,1,0:T(8,128)(2,1)S(1)} %give.1), channel_id=1, source_target_pairs={{0,256},{8,264},{16,272},{24,280},{32,288},{40,296},{48,304},{56,3... | collective-permute-start | bytes 98312 | tf_op jit(solution)/shard_map/ppermute | solution.py:333
  79.4 0.7 select_select_fusion
  80.0 4.9 %collective-permute-done.taken_ref = bf16[2,16,512]{2,1,0:T(8,128)(2,1)S(1)} collective-permute-done((bf16[2,16,512]{2,1,0:T(8,128)(2,1)S(1)}, bf16[2,16,512]{2,1,0:T(8,128)(2,1)S(1)}, u32[]{:S(2)}, u32[]{:S(2)}) %collective-permute-start) | collective-permute-done | bytes 32800 | tf_op jit(solution)/shard_map/ppermute | solution.py:333
  84.9 1.4 %keep.1 = bf16[4,16,512]{2,1,0:T(8,128)(2,1)} custom-call(s32[1]{0:T(128)} %bitcast.shard_ref, s32[2]{0:T(128)S(1)} %copy-done.9, bf16[8,144,128]{2,1,0:T(8,128)(2,1)S(1)} %all-to-all-done.2.received_ref, bf16[8,576]{1,0:T(8,128)(2,1)S(1)} %select_reduce_fusion.latent_ref, f32[2,128,128]{2,1,0:T(8,128)S(1)} %own.1.own_ref, ...), custom_call_target="tpu_custom_call" | custom-call | tf_op jit(solution)/shard_map/keep/pallas_call | solution.py:335
  (41 shorter events, 0.2 us)
Async XLA Ops:
  0.6 21.7 %copy-start = (bf16[896,576]{0,1:T(8,128)(2,1)S(1)}, bf16[896,576]{0,1:T(8,128)(2,1)}, u32[]{:S(2)}) copy-start(bf16[896,576]{0,1:T(8,128)(2,1)} %param.11) | copy-start | bytes 3096580
  0.6 0.7 copy-start.11
  4.3 16.7 %copy-start.9 = (s32[2]{0:T(128)S(1)}, s32[2]{0:T(128)}, u32[]{:S(2)}) copy-start(s32[2]{0:T(128)} %give_ref.7) | copy-start | bytes 28
  4.4 18.0 %copy-start.12 = (bf16[4,896]{1,0:T(4,128)(2,1)S(1)}, bf16[4,896]{1,0:T(4,128)(2,1)}, u32[]{:S(2)}) copy-start(bf16[4,896]{1,0:T(4,128)(2,1)} %param.10) | copy-start | bytes 21508
  4.4 48.8 %all-to-all-start = ((bf16[64,8,1152]{2,1,0:T(8,128)(2,1)}), bf16[64,8,1152]{2,1,0:T(8,128)(2,1)S(1)}, u32[]{:S(2)}, u32[]{:S(2)}) async-start(bf16[64,8,1152]{2,1,0:T(8,128)(2,1)} %pack.1), calls=%async_computation | async-start | bytes 2359296 | tf_op jit(solution)/shard_map/all_to_all | solution.py:266
  21.0 15.3 %copy-start.3 = (bf16[4,128,576]{1,2,0:T(8,128)(2,1)S(1)}, bf16[4,128,576]{1,2,0:T(8,128)(2,1)}, u32[]{:S(2)}) copy-start(bf16[4,128,576]{1,2,0:T(8,128)(2,1)} %param.13) | copy-start | bytes 1769476
  21.0 15.3 %copy-start.8 = (s32[4,40]{1,0:T(4,128)S(1)}, s32[4,40]{1,0:T(4,128)}, u32[]{:S(2)}) copy-start(s32[4,40]{1,0:T(4,128)} %table_ref.5) | copy-start | bytes 1924
  21.0 15.3 %copy-start.10 = (s32[4]{0:T(128)S(1)}, s32[4]{0:T(128)}, u32[]{:S(2)}) copy-start(s32[4]{0:T(128)} %length_ref.5) | copy-start | bytes 52
  22.4 19.1 %copy-start.13 = (f32[512]{0:T(512)S(1)}, f32[512]{0:T(512)}, u32[]{:S(2)}) copy-start(f32[512]{0:T(512)} %param.12) | copy-start | bytes 6148
  36.3 5.1 %copy-start.16 = (s32[4,1]{0,1:T(1,128)S(1)}, s32[4,1]{0,1:T(1,128)}, u32[]{:S(2)}) copy-start(s32[4,1]{0,1:T(1,128)} %reduce-window.8) | copy-start | bytes 52
  36.3 1.2 %copy-start.2 = (bf16[96,8,576]{2,1,0:T(8,128)(2,1)S(1)}, bf16[96,8,576]{2,1,0:T(8,128)(2,1)}, u32[]{:S(2)}) copy-start(bf16[96,8,576]{2,1,0:T(8,128)(2,1)} %cache_ref.1) | copy-start | bytes 2654212
  39.6 0.8 copy-start.4
  40.4 0.8 copy-start.6
  53.2 1.0 %copy-start.7 = (f32[2,128,512]{2,1,0:T(8,128)S(1)}, f32[2,128,512]{2,1,0:T(8,128)}, u32[]{:S(2)}) copy-start(f32[2,128,512]{2,1,0:T(8,128)} %copy-done.6) | copy-start | bytes 1572868
  54.2 7.2 %copy-start.14 = (pred[2,4]{0,1:T(4,128)(4,1)S(1)}, pred[2,4]{0,1:T(4,128)(4,1)}, u32[]{:S(2)}) copy-start(pred[2,4]{0,1:T(4,128)(4,1)} %copy.12) | copy-start | bytes 28
  54.2 7.2 %copy-start.15 = (pred[8]{0:T(512)(128)(4,1)S(1)}, pred[8]{0:T(512)(128)(4,1)}, u32[]{:S(2)}) copy-start(pred[8]{0:T(512)(128)(4,1)} %pad.4.clone) | copy-start | bytes 28
  55.9 0.7 copy-start.1
  56.6 13.5 %all-to-all-start.1 = ((bf16[8,144,128]{2,1,0:T(8,128)(2,1)}), bf16[8,144,128]{2,1,0:T(8,128)(2,1)S(1)}, u32[]{:S(2)}, u32[]{:S(2)}) async-start(bf16[8,144,128]{2,1,0:T(8,128)(2,1)} %copy-done.1), calls=%async_computation.1 | async-start | bytes 589824 | tf_op jit(solution)/shard_map/all_to_all | solution.py:319
  61.5 6.2 %copy-start.5 = (f32[2,128,512]{2,1,0:T(8,128)S(1)}, f32[2,128,512]{2,1,0:T(8,128)}, u32[]{:S(2)}) copy-start(f32[2,128,512]{2,1,0:T(8,128)} %copy-done.4) | copy-start | bytes 1572868
  61.7 13.5 %collective-permute-start.1 = (bf16[2,576]{1,0:T(2,128)(2,1)S(1)}, bf16[2,576]{1,0:T(2,128)(2,1)S(1)}, u32[]{:S(2)}, u32[]{:S(2)}) collective-permute-start(bf16[2,576]{1,0:T(2,128)(2,1)S(1)} %slice.33), channel_id=1, source_target_pairs={{0,256},{8,264},{16,272},{24,280},{32,288},{40,296},{48,304},{56,3... | collective-permute-start | bytes 6920 | tf_op jit(solution)/shard_map/ppermute | solution.py:279
  70.4 14.6 %all-to-all-start.2 = ((bf16[8,144,128]{2,1,0:T(8,128)(2,1)}), bf16[8,144,128]{2,1,0:T(8,128)(2,1)S(1)}, u32[]{:S(2)}, u32[]{:S(2)}) async-start(bf16[8,144,128]{2,1,0:T(8,128)(2,1)} %arrived.3), calls=%async_computation.2 | async-start | bytes 589824 | tf_op jit(solution)/shard_map/all_to_all | solution.py:319
  75.2 9.7 %collective-permute-start = (bf16[2,16,512]{2,1,0:T(8,128)(2,1)S(1)}, bf16[2,16,512]{2,1,0:T(8,128)(2,1)S(1)}, u32[]{:S(2)}, u32[]{:S(2)}) collective-permute-start(bf16[2,16,512]{2,1,0:T(8,128)(2,1)S(1)} %give.1), channel_id=1, source_target_pairs={{0,256},{8,264},{16,272},{24,280},{32,288},{40,296},{48,304},{56,3... | collective-permute-start | bytes 98312 | tf_op jit(solution)/shard_map/ppermute | solution.py:333

commit v3 on v2

v3 whole, which is shorter than its diff:
```python
import functools

import jax
import jax.numpy as jnp
from jax import lax
from jax.experimental import pallas as pl
from jax.experimental.pallas import tpu as pltpu
from jax.sharding import Mesh
from jax.sharding import PartitionSpec as P

KVL = 512
PAGE = 64
CAP = 2
ARR = 16
RESMAX = 24
MAXROWS = 4
MOVES = 2
ROPE = 64
RES_POOL = 96
SHARES = 8
DP, TP = ("half", "group"), ("x", "core")


EPSILON = 1e-06
SCORE_SCALE = 192.0 ** (-0.5)
VMEM_LIMIT = 32 * 1024 * 1024

SMEM = functools.partial(pl.BlockSpec, memory_space=pltpu.SMEM)
VMEM = functools.partial(pl.BlockSpec, memory_space=pltpu.VMEM)
HBM = functools.partial(pl.BlockSpec, memory_space=pltpu.HBM)
ANY = functools.partial(pl.BlockSpec, memory_space=pl.ANY)


def normalize(raw_latent, kv_gain):
    head_part = raw_latent[:, :KVL]
    inverse = lax.rsqrt(jnp.mean(head_part * head_part, axis=1, keepdims=True) + EPSILON)
    return jnp.concatenate(
        [head_part * inverse * kv_gain[None, :], raw_latent[:, KVL:]], axis=1
    )


def served_order(give_ref):
    first, second = give_ref[0], give_ref[1]
    low, high = jnp.minimum(first, second), jnp.maximum(first, second)
    kept_low = jnp.where(low > 0, 0, jnp.where(high > 1, 1, 2))
    kept_high = jnp.where(high < 3, 3, jnp.where(low < 2, 2, 1))
    return [first, second, kept_low, kept_high]


def resident_count(length):
    return (length + (PAGE - 1)) // PAGE - ARR


def across(a, b):
    return lax.dot_general(a, b, (((1,), (1,)), ((), ())), preferred_element_type=jnp.float32)


def pack_kernel(dest_hbm, outbox_ref, out_ref, page_ref, stage_ref, dest_ref, index_ref, in_sems, out_sems, dest_sem):
    sent, groups = outbox_ref.shape[0], out_ref.shape[0]
    parts = in_sems.shape[0]
    step = sent // parts
    dest_load = pltpu.make_async_copy(dest_hbm, dest_ref, dest_sem)
    dest_load.start()
    loads = [
        pltpu.make_async_copy(outbox_ref.at[pl.ds(i * step, step)], page_ref.at[pl.ds(i * step, step)], in_sems.at[i])
        for i in range(parts)
    ]
    for load in loads:
        load.start()
    page_ref[sent] = jnp.zeros_like(page_ref[sent])
    for i in range(groups * CAP):
        index_ref[i] = sent
    dest_load.wait()
    for i in range(sent):
        slot = dest_ref[i] * CAP
        index_ref[slot + (index_ref[slot] != sent).astype(jnp.int32)] = i
    for load in loads:
        load.wait()
    block = groups // out_sems.shape[0]
    stores = []
    for part in range(out_sems.shape[0]):
        for dest in range(part * block, (part + 1) * block):
            for rank in range(CAP):
                page = page_ref.at[index_ref[dest * CAP + rank]]
                stage_ref[dest, :, rank * KVL : (rank + 1) * KVL] = page[:, :KVL]
                stage_ref[dest, :, CAP * KVL + rank * ROPE : CAP * KVL + (rank + 1) * ROPE] = page[:, KVL:]
        span = pl.ds(part * block, block)
        store = pltpu.make_async_copy(stage_ref.at[span], out_ref.at[span], out_sems.at[part])
        store.start()
        stores.append(store)
    for store in stores:
        store.wait()


def resident_kernel(
    shard_ref, give_ref, table_ref, length_ref, cache_ref, query_ref, latent_ref, query_out, blend_out, stat_ref, key_ref
):
    piece = cache_ref.shape[1]
    heads = query_ref.shape[2]
    own = heads // SHARES
    shard = shard_ref[0]
    core = lax.rem(shard, 2)
    lane = lax.broadcasted_iota(jnp.int32, stat_ref.shape, 1)
    stats = jnp.zeros(stat_ref.shape, jnp.float32)
    order = served_order(give_ref)
    for place, row in enumerate(order):
        query_t = query_ref[row].astype(jnp.float32)
        query = jnp.concatenate([query_t, query_t[KVL:]], axis=0).T.astype(jnp.bfloat16)
        for device in range(SHARES):
            half = lax.rem(core + device, 2)
            start = pl.multiple_of(half * (heads // 2) + device // 2 * own, own)
            query_out[place, pl.ds(start, own), :] = query[device * own : (device + 1) * own]
        count = resident_count(length_ref[row])
        for pair in range(RESMAX // 2):
            parts = []
            for half in range(2):
                entry = pair * 2 + half
                parts.append(cache_ref[table_ref[row, jnp.where(entry < count, entry, 0)]])
            key_ref[place, pair * 2 * piece : (pair + 1) * 2 * piece, :] = jnp.concatenate(parts, axis=0)
    for place, row in enumerate(order):
        count = resident_count(length_ref[row])
        query = query_out[place][:, : KVL + ROPE]
        keys = key_ref[place]
        latent = latent_ref[pl.ds(row, 1), :]
        scores = SCORE_SCALE * across(query, keys)
        token = lax.broadcasted_iota(jnp.int32, scores.shape, 1)
        scores = jnp.where(token < count * piece, scores, -jnp.inf)
        fresh = SCORE_SCALE * jnp.sum(query.astype(jnp.float32) * latent, axis=1, keepdims=True)
        fresh = jnp.where(shard == 0, fresh, -jnp.inf)
        top = jnp.maximum(jnp.max(scores, axis=1, keepdims=True), fresh)
        weights = jnp.exp(scores - top)
        fresh_weight = jnp.exp(fresh - top)
        total = jnp.sum(weights, axis=1, keepdims=True) + fresh_weight
        blend = jnp.dot(weights.astype(jnp.bfloat16), keys[:, :KVL], preferred_element_type=jnp.float32)
        blend_out[place] = blend + fresh_weight * latent[:, :KVL]
        stats = jnp.where(lane == place, top, jnp.where(lane == MAXROWS + place, total, stats))
    stat_ref[...] = stats


def coded(level, lane, stride, place, stats):
    for term in range(3):
        rounded = level.astype(jnp.bfloat16).astype(jnp.float32)
        stats = jnp.where(lane == term * stride + place, rounded, stats)
        level = level - rounded
    return stats


def decoded(stats, stride):
    stats = stats.astype(jnp.float32)
    return stats + pltpu.roll(stats, 128 - stride, 1) + pltpu.roll(stats, 128 - 2 * stride, 1)


def arrived_kernel(
    shard_ref, give_ref, table_ref, length_ref, arrived_ref, query_ref, blend_hbm, stat_ref, mine_ref, other_ref, blend_ref, sems
):
    chips, piece = mine_ref.shape[0], arrived_ref.shape[1]
    rows, heads, _ = query_ref.shape
    own = heads // SHARES
    loads = [pltpu.make_async_copy(blend_hbm.at[place], blend_ref.at[place], sems.at[place]) for place in range(rows)]
    for load in loads:
        load.start()
    lane = lax.broadcasted_iota(jnp.int32, (heads, 128), 1)
    page_lane = lax.broadcasted_iota(jnp.int32, (piece, 128), 1)
    stats = jnp.zeros((heads, 128), jnp.float32)
    order = served_order(give_ref)
    keys, ropes = [], []
    for row in order:
        count = resident_count(length_ref[row])
        latent_parts, rope_parts = [], []
        for entry in range(ARR):
            slot = table_ref[row, count + entry] - RES_POOL
            source, rank = slot // CAP, lax.rem(slot, CAP)
            latent_parts.append(arrived_ref[source, :, pl.ds(pl.multiple_of(rank * KVL, KVL), KVL)])
            both = arrived_ref[source, :, CAP * KVL : CAP * KVL + 128].astype(jnp.float32)
            rope_parts.append(jnp.where(page_lane // ROPE == rank, both, 0.0))
        keys.append(jnp.concatenate(latent_parts, axis=0))
        ropes.append(jnp.concatenate(rope_parts, axis=0).astype(jnp.bfloat16))
    for place, row in enumerate(order):
        length = length_ref[row]
        count = resident_count(length)
        query = query_ref[place]
        scores = SCORE_SCALE * (across(query[:, :KVL], keys[place]) + across(query[:, KVL:], ropes[place]))
        token = lax.broadcasted_iota(jnp.int32, scores.shape, 1)
        position = (count + token // piece) * PAGE + shard_ref[0] * piece + lax.rem(token, piece)
        scores = jnp.where(position < length, scores, -jnp.inf)
        old_top = stat_ref[:, place : place + 1]
        old_total = stat_ref[:, MAXROWS + place : MAXROWS + place + 1]
        top = jnp.maximum(jnp.max(scores, axis=1, keepdims=True), old_top)
        weights = jnp.exp(scores - top)
        shrink = jnp.exp(old_top - top)
        total = jnp.sum(weights, axis=1, keepdims=True) + shrink * old_total
        blend = jnp.dot(weights.astype(jnp.bfloat16), keys[place], preferred_element_type=jnp.float32)
        loads[place].wait()
        partial = ((blend + shrink * blend_ref[place]) * (1.0 / total)).astype(jnp.bfloat16)
        for half, part_ref in enumerate((mine_ref, other_ref)):
            for chip in range(chips):
                first = (half * chips + chip) * own
                for chunk in range(KVL // 128):
                    start = (chunk * rows + place) * own
                    part_ref[chip, start : start + own, :] = partial[first : first + own, chunk * 128 : (chunk + 1) * 128]
        stats = coded(top + jnp.log(total), lane, rows, place, stats)
    stats = stats.astype(jnp.bfloat16)
    for half, part_ref in enumerate((mine_ref, other_ref)):
        for chip in range(chips):
            first = (half * chips + chip) * own
            part_ref[chip, KVL // 128 * rows * own :, :] = stats[first : first + own]


def merge_kernel(side_ref, mine_ref, other_ref, send_ref, stage_ref, sems):
    chips = mine_ref.shape[0]
    rows = MAXROWS
    own = mine_ref.shape[1] // (KVL // 128 * rows + 1)
    lane = lax.broadcasted_iota(jnp.int32, (own, 128), 1)
    side = side_ref[0]
    stat_base = KVL // 128 * rows * own
    stores = []
    for chip in range(chips):
        level_a = decoded(mine_ref[chip, stat_base:, :], rows)
        level_b = decoded(other_ref[chip, stat_base:, :], rows)
        peak = jnp.maximum(level_a, level_b)
        weight_a, weight_b = jnp.exp(level_a - peak), jnp.exp(level_b - peak)
        total = weight_a + weight_b
        level = peak + jnp.log(total)
        weight_a, weight_b = weight_a / total, weight_b / total
        for part in range(2):
            target = jnp.where(side == part, 1, 0) * chips + chip
            stats = jnp.zeros((own, 128), jnp.float32)
            for move in range(MOVES):
                place = part * MOVES + move
                column_a = jnp.broadcast_to(weight_a[:, place : place + 1], (own, 128))
                column_b = jnp.broadcast_to(weight_b[:, place : place + 1], (own, 128))
                for chunk in range(KVL // 128):
                    start = (chunk * rows + place) * own
                    value = column_a * mine_ref[chip, start : start + own, :].astype(jnp.float32)
                    value += column_b * other_ref[chip, start : start + own, :].astype(jnp.float32)
                    to = (chunk * MOVES + move) * own
                    stage_ref[target, to : to + own, :] = value.astype(jnp.bfloat16)
                stats = coded(level[:, place : place + 1], lane, MOVES, move, stats)
            stage_ref[target, KVL // 128 * MOVES * own :, :] = stats.astype(jnp.bfloat16)
            store = pltpu.make_async_copy(stage_ref.at[target], send_ref.at[target], sems.at[chip * 2 + part])
            store.start()
            stores.append(store)
    for store in stores:
        store.wait()


def finish_kernel(side_ref, give_ref, received_ref, out_ref):
    chips = received_ref.shape[0] // 2
    own = received_ref.shape[1] // (KVL // 128 * MOVES + 1)
    stat_base = KVL // 128 * MOVES * own
    order = served_order(give_ref)
    for part in range(2):
        base = jnp.where(side_ref[0] == part, 1, 0) * chips
        levels = [decoded(received_ref[base + chip, stat_base:, :], MOVES) for chip in range(chips)]
        peak = functools.reduce(jnp.maximum, levels)
        weights = [jnp.exp(level - peak) for level in levels]
        inverse = 1.0 / functools.reduce(lambda a, b: a + b, weights)
        weights = [weight * inverse for weight in weights]
        for move in range(MOVES):
            columns = [jnp.broadcast_to(weight[:, move : move + 1], weight.shape) for weight in weights]
            chunks = []
            for chunk in range(KVL // 128):
                start = (chunk * MOVES + move) * own
                value = columns[0] * received_ref[base, start : start + own, :].astype(jnp.float32)
                for chip in range(1, chips):
                    value += columns[chip] * received_ref[base + chip, start : start + own, :].astype(jnp.float32)
                chunks.append(value.astype(jnp.bfloat16))
            out_ref[order[part * MOVES + move]] = jnp.concatenate(chunks, axis=1)


def shards(
    hidden,
    kva_weight,
    kv_gain,
    queries,
    latent_cache,
    outbox,
    out_dest,
    page_table,
    lengths,
    give_rows,
):
    group_count = lax.axis_size(DP)
    chip_count = lax.axis_size("x")
    shard = lax.axis_index(TP).astype(jnp.int32).reshape(1)
    side = lax.axis_index("half").astype(jnp.int32).reshape(1)
    row_count = hidden.shape[0]
    page_piece = latent_cache.shape[1]
    heads = queries.shape[1]
    own = heads // SHARES
    moves = give_rows.shape[0]
    query_t = jnp.swapaxes(queries, 1, 2)
    wide = KVL + 2 * ROPE
    params = pltpu.CompilerParams(vmem_limit_bytes=VMEM_LIMIT)
    shape = jax.ShapeDtypeStruct
    in_hbm = functools.partial(pltpu.with_memory_space_constraint, memory_space=pltpu.HBM)

    outgoing = pl.pallas_call(
        pack_kernel,
        out_shape=shape((group_count, page_piece, CAP * (KVL + ROPE)), jnp.bfloat16),
        in_specs=[HBM(), HBM()],
        out_specs=ANY(),
        scratch_shapes=[
            pltpu.VMEM((outbox.shape[0] + 1,) + outbox.shape[1:], jnp.bfloat16),
            pltpu.VMEM((group_count, page_piece, CAP * (KVL + ROPE)), jnp.bfloat16),
            pltpu.SMEM(out_dest.shape, jnp.int32),
            pltpu.SMEM((group_count * CAP,), jnp.int32),
            pltpu.SemaphoreType.DMA((8,)),
            pltpu.SemaphoreType.DMA((8,)),
            pltpu.SemaphoreType.DMA,
        ],
        compiler_params=params,
        name="pack",
    )(in_hbm(out_dest), in_hbm(outbox))
    arrived = lax.all_to_all(outgoing, DP, split_axis=0, concat_axis=0, tiled=True)

    partial_raw = jnp.dot(hidden, kva_weight, preferred_element_type=jnp.float32)
    parts = lax.all_gather(partial_raw, TP)
    home_latent = lax.reduce_precision(normalize(jnp.sum(parts, axis=0), kv_gain), 8, 7)
    row_ids = lax.broadcasted_iota(jnp.int32, (moves, row_count), 1)
    is_given = row_ids == give_rows[:, None]
    handed_latent = jnp.sum(jnp.where(is_given[:, :, None], home_latent[None], 0.0), axis=1).astype(jnp.bfloat16)
    taken_latent = lax.ppermute(handed_latent, "half", [(0, 1), (1, 0)])
    new_latent = home_latent.astype(jnp.bfloat16)
    for move in range(moves):
        new_latent = jnp.where(is_given[move][:, None], taken_latent[move][None], new_latent)

    query, blend, stats = pl.pallas_call(
        resident_kernel,
        out_shape=(
            shape((row_count, heads, wide), jnp.bfloat16),
            shape((row_count, heads, KVL), jnp.float32),
            shape((heads, 128), jnp.float32),
        ),
        in_specs=[SMEM()] * 4 + [VMEM()] * 3,
        out_specs=(VMEM(),) * 3,
        scratch_shapes=[pltpu.VMEM((row_count, RESMAX * page_piece, latent_cache.shape[2]), jnp.bfloat16)],
        compiler_params=params,
        name="resident",
    )(shard, give_rows, page_table, lengths, latent_cache, query_t, home_latent)
    stats, new_latent = lax.optimization_barrier((stats, new_latent))

    part_shape = shape((chip_count, (KVL // 128 * row_count + 1) * own, 128), jnp.bfloat16)
    mine, other = pl.pallas_call(
        arrived_kernel,
        out_shape=(part_shape, part_shape),
        in_specs=[SMEM()] * 4 + [VMEM()] * 2 + [HBM(), VMEM()],
        out_specs=(VMEM(), VMEM()),
        scratch_shapes=[pltpu.VMEM((row_count, heads, KVL), jnp.float32), pltpu.SemaphoreType.DMA((row_count,))],
        compiler_params=params,
        name="arrived",
    )(shard, give_rows, page_table, lengths, arrived, query, in_hbm(blend), stats)
    other = lax.ppermute(other, "core", [(0, 1), (1, 0)])
    send_shape = (2 * chip_count, (KVL // 128 * moves + 1) * own, 128)
    outbound = pl.pallas_call(
        merge_kernel,
        out_shape=shape(send_shape, jnp.bfloat16),
        in_specs=[SMEM()] + [VMEM()] * 2,
        out_specs=ANY(),
        scratch_shapes=[pltpu.VMEM(send_shape, jnp.bfloat16), pltpu.SemaphoreType.DMA((2 * chip_count,))],
        compiler_params=params,
        name="merge",
    )(side, mine, other)
    received = lax.all_to_all(outbound, ("half", "x"), split_axis=0, concat_axis=0, tiled=True)
    attended = pl.pallas_call(
        finish_kernel,
        out_shape=shape((row_count, own, KVL), jnp.bfloat16),
        in_specs=[SMEM()] * 2 + [VMEM()],
        out_specs=VMEM(),
        compiler_params=params,
        name="finish",
    )(side, give_rows, received)
    return (attended, new_latent)


def solution(mesh):
    groups, shares = mesh.devices.shape
    split = Mesh(mesh.devices.reshape(2, groups // 2, shares // 2, 2), DP + TP)
    placed = (
        P(DP, TP),
        P(TP, None),
        P(),
        P(DP, None, None),
        P(DP, TP, None),
        P(DP, TP, None),
        P(DP),
        P(DP, None),
        P(DP),
        P(DP),
    )
    return jax.shard_map(
        shards,
        mesh=split,
        in_specs=placed,
        out_specs=(P(DP, TP, None), P(DP, None)),
        check_vma=False,
    )
```

time: 87 us -> 85.4 us (0.982)
  the two profiles are of different devices: /device:TPU:2 before, /device:TPU:16 now
where the time goes in v3:
time: 85.4 us; the launch traced here: 85 us
  blocking collectives  34.1 us (40%)
  starting transfers between devices  24.1 us (28%)
  Pallas kernels  11.4 us (13%)
  waiting for transfers between devices  8.97 us (11%)
  local copies, waits for them, and re-layouts  4.08 us (5%)
  other arithmetic  1.08 us (1%)
    all_to_all x1, blocking collectives, shards(): lax.all_to_all(outbound, ('half', 'x'), split_axis=0, concat_axis=0, tile...  21 us
    all_to_all x1, starting transfers between devices, shards(): lax.all_to_all(outgoing, DP, split_axis=0, concat_axis=0, tiled=True)  16.5 us
    all_gather x1, blocking collectives, shards(): parts = lax.all_gather(partial_raw, TP)  13.1 us
    ppermute x1, starting transfers between devices, shards(): taken_latent = lax.ppermute(handed_latent, 'half', [(0, 1), (1, 0)])  5.68 us
    unnamed x22, local copies, waits for them, and re-layouts  4.04 us
    ppermute x1, waiting for transfers between devices, shards(): taken_latent = lax.ppermute(handed_latent, 'half', [(0, 1), (1, 0)])  3.8 us
    pallas_call x1, Pallas kernels, shards(): pl.pallas_call(arrived_kernel, out_shape=(part_shape, part_shape), in_spe...  3.78 us
    all_to_all x1, waiting for transfers between devices, shards(): lax.all_to_all(outgoing, DP, split_axis=0, concat_axis=0, tiled=True)  3.65 us
  transfers between devices with their start and end apart: 3, of which 3 were waited for; matrix products, arithmetic and copies ran while one was open for 2% of the time, Pallas kernels for 3%

profile of v3, /device:TPU:16, one launch (start us, length us, event | category | flops | bytes accessed | tf_op | source)
XLA Modules:
  0.0 85.0 jit_solution(3031280936481406118)
XLA Ops:
  0.6 0.0 copy-start
  0.6 2.5 %pack.1 = bf16[64,8,1152]{2,1,0:T(8,128)(2,1)} custom-call(s32[64]{0:T(128)} %dest_hbm.1, bf16[64,8,576]{2,1,0:T(8,128)(2,1)} %outbox_ref.1), custom_call_target="tpu_custom_call" | custom-call | tf_op jit(solution)/shard_map/pack/pallas_call | solution.py:298
  3.2 0.0 copy-start.9
  3.2 16.5 %all-to-all-start = ((bf16[64,8,1152]{2,1,0:T(8,128)(2,1)}), bf16[64,8,1152]{2,1,0:T(8,128)(2,1)S(1)}, u32[]{:S(2)}, u32[]{:S(2)}) async-start(bf16[64,8,1152]{2,1,0:T(8,128)(2,1)} %pack.1), calls=%async_computation | async-start | bytes 2359296 | tf_op jit(solution)/shard_map/all_to_all | solution.py:315
  19.7 0.0 copy-done
  19.7 0.0 copy-start.10
  19.7 0.0 copy-start.7
  19.7 0.0 copy-start.2
  19.7 0.0 copy-start.6
  19.7 0.0 copy-start.8
  19.7 0.4 convolution_bitcast_fusion
  20.1 13.1 %all-gather.1 = f32[8,4,576]{2,1,0:T(4,128)S(1)} all-gather(f32[1,4,576]{2,1,0:T(4,128)S(1)} %convolution_bitcast_fusion), channel_id=2, replica_groups=mesh['half'=2,'group'=32,'x'=4,'core'=2] {'x','core'}, dimensions={0}, use_global_device_ids=true | all-gather | bytes 82944 | tf_op jit(solution)/shard_map/all_gather | solution.py:318
  33.3 0.1 multiply_reduce_fusion
  33.4 0.1 multiply_multiply_fusion
  33.5 0.1 iota_compare_fusion
  33.6 0.1 select_reduce_fusion
  33.7 5.7 %collective-permute-start = (bf16[2,576]{1,0:T(2,128)(2,1)S(1)}, bf16[2,576]{1,0:T(2,128)(2,1)S(1)}, u32[]{:S(2)}, u32[]{:S(2)}) collective-permute-start(bf16[2,576]{1,0:T(2,128)(2,1)S(1)} %select_reduce_fusion), channel_id=1, source_target_pairs={{0,256},{256,0},{1,257},{257,1},{2,258},{258,2},{3,259},{259,3},{4... | collective-permute-start | bytes 6920 | tf_op jit(solution)/shard_map/ppermute | solution.py:323
  39.4 0.0 copy-start.5
  39.4 1.1 %copy-done.5 = bf16[4,128,576]{1,2,0:T(8,128)(2,1)S(1)} copy-done((bf16[4,128,576]{1,2,0:T(8,128)(2,1)S(1)}, bf16[4,128,576]{1,2,0:T(8,128)(2,1)}, u32[]{:S(2)}) %copy-start.5) | copy-done | bytes 589848
  40.5 2.2 %resident.1 = (bf16[4,128,640]{2,1,0:T(8,128)(2,1)S(1)}, f32[4,128,512]{2,1,0:T(8,128)S(1)}, f32[128,128]{1,0:T(8,128)S(1)}) custom-call(s32[1]{0:T(128)} %bitcast.1.shard_ref, s32[2]{0:T(128)S(1)} %copy-done.7, s32[4,40]{1,0:T(4,128)S(1)} %copy-done.6, s32[4]{0:T(128)S(1)} %copy-done.8, bf16[96,8,576]{2,1,0:T(8,128)(2,1)S(1)} %copy-done.2, ...), custom_call_target="tpu_custom_call" | custom-call | tf_op jit(solution)/shard_map/resident/pallas_call | solution.py:328
  42.7 1.0 %copy-done.1 = f32[4,128,512]{2,1,0:T(8,128)} copy-done((f32[4,128,512]{2,1,0:T(8,128)}, f32[4,128,512]{2,1,0:T(8,128)S(1)}, u32[]{:S(2)}) %copy-start.1) | copy-done | bytes 1048600
  43.7 0.8 copy-done.3
  44.6 3.8 %collective-permute-done = bf16[2,576]{1,0:T(2,128)(2,1)S(1)} collective-permute-done((bf16[2,576]{1,0:T(2,128)(2,1)S(1)}, bf16[2,576]{1,0:T(2,128)(2,1)S(1)}, u32[]{:S(2)}, u32[]{:S(2)}) %collective-permute-start) | collective-permute-done | bytes 2336 | tf_op jit(solution)/shard_map/ppermute | solution.py:323
  48.4 0.7 select_select_fusion
  49.1 3.7 %all-to-all-done.arrived_ref = bf16[64,8,1152]{2,1,0:T(8,128)(2,1)S(1)} async-done(((bf16[64,8,1152]{2,1,0:T(8,128)(2,1)}), bf16[64,8,1152]{2,1,0:T(8,128)(2,1)S(1)}, u32[]{:S(2)}, u32[]{:S(2)}) %all-to-all-start) | async-done | bytes 1179680 | tf_op jit(solution)/shard_map/all_to_all | solution.py:315
  52.7 1.1 %copy-done.4 = bf16[4,128,640]{2,1,0:T(8,128)(2,1)S(1)} copy-done((bf16[4,128,640]{2,1,0:T(8,128)(2,1)S(1)}, bf16[4,128,640]{2,1,0:T(8,128)(2,1)}, u32[]{:S(2)}) %copy-start.4) | copy-done | bytes 655384
  53.8 3.8 %arrived.1 = (bf16[4,272,128]{2,1,0:T(8,128)(2,1)S(1)}, bf16[4,272,128]{2,1,0:T(8,128)(2,1)S(1)}) custom-call(s32[1]{0:T(128)} %bitcast.1.shard_ref, s32[2]{0:T(128)S(1)} %copy-done.7, s32[4,40]{1,0:T(4,128)S(1)} %copy-done.6, s32[4]{0:T(128)S(1)} %copy-done.8, bf16[64,8,1152]{2,1,0:T(8,128)(2,1)S(1)} %all-to-all-done.arrived_ref, ...), custom_call_target="tpu_custom_call" | custom-call | tf_op jit(solution)/shard_map/arrived/pallas_call | solution.py:344
  57.6 1.9 %collective-permute-start.1 = (bf16[4,272,128]{2,1,0:T(8,128)(2,1)S(1)}, bf16[4,272,128]{2,1,0:T(8,128)(2,1)S(1)}, u32[]{:S(2)}, u32[]{:S(2)}) collective-permute-start(bf16[4,272,128]{2,1,0:T(8,128)(2,1)S(1)} %get-tuple-element.14), channel_id=1, source_target_pairs={{0,1},{1,0},{2,3},{3,2},{4,5},{5,4},{6,7},{7,6},{8,9},{9,8},{10,11... | collective-permute-start | bytes 835592 | tf_op jit(solution)/shard_map/ppermute | solution.py:353
  59.5 1.5 %collective-permute-done.1.other_ref = bf16[4,272,128]{2,1,0:T(8,128)(2,1)S(1)} collective-permute-done((bf16[4,272,128]{2,1,0:T(8,128)(2,1)S(1)}, bf16[4,272,128]{2,1,0:T(8,128)(2,1)S(1)}, u32[]{:S(2)}, u32[]{:S(2)}) %collective-permute-start.1) | collective-permute-done | bytes 278560 | tf_op jit(solution)/shard_map/ppermute | solution.py:353
  61.1 1.5 %merge.1 = bf16[8,144,128]{2,1,0:T(8,128)(2,1)S(1)} custom-call(s32[1]{0:T(128)} %bitcast.side_ref, bf16[4,272,128]{2,1,0:T(8,128)(2,1)S(1)} %get-tuple-element.13.mine_ref, bf16[4,272,128]{2,1,0:T(8,128)(2,1)S(1)} %collective-permute-done.1.other_ref), custom_call_target="tpu_custom_call" | custom-call | tf_op jit(solution)/shard_map/merge/pallas_call | solution.py:355
  62.6 21.0 %all_to_all.10.received_ref = bf16[8,144,128]{2,1,0:T(8,128)(2,1)S(1)} all-to-all(bf16[8,144,128]{2,1,0:T(8,128)(2,1)S(1)} %merge.1), channel_id=1, replica_groups=mesh['half'=2,'group'=32,'x'=4,'core'=2] {'half','x'}, dimensions={0} | all-to-all | bytes 589824 | tf_op jit(solution)/shard_map/all_to_all | solution.py:364
  83.6 1.4 %finish.1 = bf16[4,16,512]{2,1,0:T(8,128)(2,1)} custom-call(s32[1]{0:T(128)} %bitcast.side_ref, s32[2]{0:T(128)S(1)} %copy-done.7, bf16[8,144,128]{2,1,0:T(8,128)(2,1)S(1)} %all_to_all.10.received_ref), custom_call_target="tpu_custom_call" | custom-call | tf_op jit(solution)/shard_map/finish/pallas_call | solution.py:365
  (15 shorter events, 0.1 us)
Async XLA Ops:
  0.6 19.0 %copy-start = (bf16[896,576]{0,1:T(8,128)(2,1)S(1)}, bf16[896,576]{0,1:T(8,128)(2,1)}, u32[]{:S(2)}) copy-start(bf16[896,576]{0,1:T(8,128)(2,1)} %param.11) | copy-start | bytes 3096580
  3.2 16.5 %copy-start.9 = (bf16[4,896]{1,0:T(4,128)(2,1)S(1)}, bf16[4,896]{1,0:T(4,128)(2,1)}, u32[]{:S(2)}) copy-start(bf16[4,896]{1,0:T(4,128)(2,1)} %param.10) | copy-start | bytes 21508
  3.2 49.6 %all-to-all-start = ((bf16[64,8,1152]{2,1,0:T(8,128)(2,1)}), bf16[64,8,1152]{2,1,0:T(8,128)(2,1)S(1)}, u32[]{:S(2)}, u32[]{:S(2)}) async-start(bf16[64,8,1152]{2,1,0:T(8,128)(2,1)} %pack.1), calls=%async_computation | async-start | bytes 2359296 | tf_op jit(solution)/shard_map/all_to_all | solution.py:315
  19.7 13.7 %copy-start.10 = (f32[512]{0:T(512)S(1)}, f32[512]{0:T(512)}, u32[]{:S(2)}) copy-start(f32[512]{0:T(512)} %param.12) | copy-start | bytes 6148
  19.7 13.8 %copy-start.7 = (s32[2]{0:T(128)S(1)}, s32[2]{0:T(128)}, u32[]{:S(2)}) copy-start(s32[2]{0:T(128)} %give_ref.5) | copy-start | bytes 28
  19.7 19.7 %copy-start.2 = (bf16[96,8,576]{2,1,0:T(8,128)(2,1)S(1)}, bf16[96,8,576]{2,1,0:T(8,128)(2,1)}, u32[]{:S(2)}) copy-start(bf16[96,8,576]{2,1,0:T(8,128)(2,1)} %cache_ref.1) | copy-start | bytes 2654212
  19.7 19.7 %copy-start.6 = (s32[4,40]{1,0:T(4,128)S(1)}, s32[4,40]{1,0:T(4,128)}, u32[]{:S(2)}) copy-start(s32[4,40]{1,0:T(4,128)} %table_ref.3) | copy-start | bytes 1924
  19.7 19.7 %copy-start.8 = (s32[4]{0:T(128)S(1)}, s32[4]{0:T(128)}, u32[]{:S(2)}) copy-start(s32[4]{0:T(128)} %length_ref.3) | copy-start | bytes 52
  33.7 14.7 %collective-permute-start = (bf16[2,576]{1,0:T(2,128)(2,1)S(1)}, bf16[2,576]{1,0:T(2,128)(2,1)S(1)}, u32[]{:S(2)}, u32[]{:S(2)}) collective-permute-start(bf16[2,576]{1,0:T(2,128)(2,1)S(1)} %select_reduce_fusion), channel_id=1, source_target_pairs={{0,256},{256,0},{1,257},{257,1},{2,258},{258,2},{3,259},{259,3},{4... | collective-permute-start | bytes 6920 | tf_op jit(solution)/shard_map/ppermute | solution.py:323
  39.4 1.1 %copy-start.5 = (bf16[4,128,576]{1,2,0:T(8,128)(2,1)S(1)}, bf16[4,128,576]{1,2,0:T(8,128)(2,1)}, u32[]{:S(2)}) copy-start(bf16[4,128,576]{1,2,0:T(8,128)(2,1)} %param.13) | copy-start | bytes 1769476
  42.7 1.0 %copy-start.1 = (f32[4,128,512]{2,1,0:T(8,128)}, f32[4,128,512]{2,1,0:T(8,128)S(1)}, u32[]{:S(2)}) copy-start(f32[4,128,512]{2,1,0:T(8,128)S(1)} %get-tuple-element.10.blend_hbm) | copy-start | bytes 3145732
  43.7 0.8 copy-start.3
  52.7 1.1 %copy-start.4 = (bf16[4,128,640]{2,1,0:T(8,128)(2,1)S(1)}, bf16[4,128,640]{2,1,0:T(8,128)(2,1)}, u32[]{:S(2)}) copy-start(bf16[4,128,640]{2,1,0:T(8,128)(2,1)} %copy-done.3) | copy-start | bytes 1966084
  57.6 3.5 %collective-permute-start.1 = (bf16[4,272,128]{2,1,0:T(8,128)(2,1)S(1)}, bf16[4,272,128]{2,1,0:T(8,128)(2,1)S(1)}, u32[]{:S(2)}, u32[]{:S(2)}) collective-permute-start(bf16[4,272,128]{2,1,0:T(8,128)(2,1)S(1)} %get-tuple-element.14), channel_id=1, source_target_pairs={{0,1},{1,0},{2,3},{3,2},{4,5},{5,4},{6,7},{7,6},{8,9},{9,8},{10,11... | collective-permute-start | bytes 835592 | tf_op jit(solution)/shard_map/ppermute | solution.py:353

commit v4 on v3

v4 whole, which is shorter than its diff:
```python
import functools

import jax
import jax.numpy as jnp
from jax import lax
from jax.experimental import pallas as pl
from jax.experimental.pallas import tpu as pltpu
from jax.sharding import Mesh
from jax.sharding import PartitionSpec as P

KVL = 512
PAGE = 64
CAP = 2
ARR = 16
RESMAX = 24
MAXROWS = 4
MOVES = 2
ROPE = 64
RES_POOL = 96
SHARES = 8
DP, TP = ("half", "group"), ("x", "core")
LATENT_ROWS = 5
META_SHARD, META_ROW, META_LEFT, META_SLOT = 0, 4, 8, 16


def interleaved(rank):
    y = (rank >> 5 & 1) * 4 + (rank >> 3 & 1) * 2 + (rank >> 1 & 1)
    z = (rank >> 4 & 1) * 4 + (rank >> 2 & 1) * 2 + (rank & 1)
    return y * 8 + z


ORDER = [interleaved(rank) for rank in range(64)]


EPSILON = 1e-06
SCORE_SCALE = 192.0 ** (-0.5)
VMEM_LIMIT = 32 * 1024 * 1024

SMEM = functools.partial(pl.BlockSpec, memory_space=pltpu.SMEM)
VMEM = functools.partial(pl.BlockSpec, memory_space=pltpu.VMEM)
HBM = functools.partial(pl.BlockSpec, memory_space=pltpu.HBM)
ANY = functools.partial(pl.BlockSpec, memory_space=pl.ANY)


def normalize(raw_latent, kv_gain):
    head_part = raw_latent[:, :KVL]
    inverse = lax.rsqrt(jnp.mean(head_part * head_part, axis=1, keepdims=True) + EPSILON)
    return jnp.concatenate(
        [head_part * inverse * kv_gain[None, :], raw_latent[:, KVL:]], axis=1
    )


def served_order(give_ref):
    first, second = give_ref[0], give_ref[1]
    low, high = jnp.minimum(first, second), jnp.maximum(first, second)
    kept_low = jnp.where(low > 0, 0, jnp.where(high > 1, 1, 2))
    kept_high = jnp.where(high < 3, 3, jnp.where(low < 2, 2, 1))
    return [first, second, kept_low, kept_high]


def resident_count(length):
    return (length + (PAGE - 1)) // PAGE - ARR


def stacked(rows, start=0, count=8):
    place = lax.broadcasted_iota(jnp.int32, (count, 128), 0)
    result = jnp.zeros((count, 128), jnp.float32)
    for index, row in enumerate(rows):
        result = jnp.where(place == start + index, row, result)
    return result


def turned(rows):
    return jnp.concatenate([rows, jnp.zeros((128 - rows.shape[0], 128), jnp.float32)], axis=0).T


def coded(level):
    terms = []
    for _ in range(3):
        terms.append(level.astype(jnp.bfloat16).astype(jnp.float32))
        level = level - terms[-1]
    return terms


def decoded(stats, count):
    stats = stats.astype(jnp.float32)
    return stats[:count] + stats[count : 2 * count] + stats[2 * count : 3 * count]


def blended(weights, values):
    return lax.dot_general(weights, values, (((0,), (0,)), ((), ())), preferred_element_type=jnp.float32)


def pack_kernel(dest_hbm, outbox_ref, out_ref, page_ref, stage_ref, dest_ref, index_ref, in_sems, out_sems, dest_sem):
    sent, groups = outbox_ref.shape[0], out_ref.shape[0]
    parts = in_sems.shape[0]
    step = sent // parts
    dest_load = pltpu.make_async_copy(dest_hbm, dest_ref, dest_sem)
    dest_load.start()
    loads = [
        pltpu.make_async_copy(outbox_ref.at[pl.ds(i * step, step)], page_ref.at[pl.ds(i * step, step)], in_sems.at[i])
        for i in range(parts)
    ]
    for load in loads:
        load.start()
    page_ref[sent] = jnp.zeros_like(page_ref[sent])
    for i in range(groups * CAP):
        index_ref[i] = sent
    dest_load.wait()
    for i in range(sent):
        slot = dest_ref[i] * CAP
        index_ref[slot + (index_ref[slot] != sent).astype(jnp.int32)] = i
    for load in loads:
        load.wait()
    block = groups // out_sems.shape[0]
    stores = []
    for part in range(out_sems.shape[0]):
        for dest in range(part * block, (part + 1) * block):
            for rank in range(CAP):
                page = page_ref.at[index_ref[ORDER[dest] * CAP + rank]]
                stage_ref[dest, :, rank * KVL : (rank + 1) * KVL] = page[:, :KVL]
                stage_ref[dest, :, CAP * KVL + rank * ROPE : CAP * KVL + (rank + 1) * ROPE] = page[:, KVL:]
        span = pl.ds(part * block, block)
        store = pltpu.make_async_copy(stage_ref.at[span], out_ref.at[span], out_sems.at[part])
        store.start()
        stores.append(store)
    for store in stores:
        store.wait()


def resident_kernel(
    shard_ref, give_ref, table_ref, length_ref, places_ref, cache_ref, query_ref, latent_ref,
    meta_ref, blend_out, stat_ref, handed_ref, key_ref,
):
    piece = cache_ref.shape[1]
    shard = shard_ref[0]
    resident = RESMAX * piece
    order = served_order(give_ref)
    tops, totals, handed = [], [], []
    meta_ref[META_SHARD] = shard
    for place, row in enumerate(order):
        length = length_ref[row]
        count = resident_count(length)
        meta_ref[META_ROW + place] = row
        meta_ref[META_LEFT + place] = length - count * PAGE
        for entry in range(ARR):
            slot = table_ref[row, count + entry] - RES_POOL
            meta_ref[META_SLOT + place * ARR + entry] = places_ref[slot // CAP] * CAP + lax.rem(slot, CAP)
        for pair in range(RESMAX // 2):
            parts = []
            for half in range(2):
                entry = pair * 2 + half
                parts.append(cache_ref[table_ref[row, jnp.where(entry < count, entry, 0)]])
            key_ref[place, pair * 2 * piece : (pair + 1) * 2 * piece, :] = jnp.concatenate(parts, axis=0)
        latent = latent_ref[pl.ds(row, 1), :]
        key_ref[place, resident:, :] = jnp.broadcast_to(latent, (16, latent.shape[1])).astype(jnp.bfloat16)
        if place < MOVES:
            latent = jnp.concatenate([latent, jnp.zeros((1, 128 - ROPE), jnp.float32)], axis=1)
            handed.extend(latent[:, chunk * 128 : (chunk + 1) * 128] for chunk in range(LATENT_ROWS))
    handed_ref[...] = stacked(handed, 3 * MOVES, 16)
    for place, row in enumerate(order):
        count = resident_count(length_ref[row])
        keys = key_ref[place]
        scores = SCORE_SCALE * jnp.dot(keys, query_ref[row], preferred_element_type=jnp.float32)
        token = lax.broadcasted_iota(jnp.int32, scores.shape, 0)
        fresh = jnp.where(shard == 0, resident, -1)
        scores = jnp.where((token < count * piece) | (token == fresh), scores, -jnp.inf)
        top = jnp.max(scores, axis=0, keepdims=True)
        weights = jnp.exp(scores - top)
        blend_out[place] = blended(weights.astype(jnp.bfloat16), keys[:, :KVL])
        tops.append(top)
        totals.append(jnp.sum(weights, axis=0, keepdims=True))
    stat_ref[...] = stacked(tops + totals)


def arrived_kernel(
    meta_ref, arrived_ref, query_hbm, blend_hbm, stat_ref, mine_ref, other_ref, query_ref, blend_ref, key_ref, rope_ref, sems
):
    piece = arrived_ref.shape[1]
    rows, _, heads = query_ref.shape
    own = heads // SHARES
    chips = SHARES // 2
    query_loads, blend_loads = [], []
    for place in range(rows):
        source = query_hbm.at[meta_ref[META_ROW + place]]
        query_loads.append(pltpu.make_async_copy(source, query_ref.at[place], sems.at[place]))
        query_loads[-1].start()
    for place in range(rows):
        blend_loads.append(pltpu.make_async_copy(blend_hbm.at[place], blend_ref.at[place], sems.at[rows + place]))
        blend_loads[-1].start()
    first_half = lax.broadcasted_iota(jnp.int32, (piece, 128), 1) // ROPE
    for place in range(rows):
        for pair in range(ARR // 2):
            latents, ropes = [], []
            for half in range(2):
                slot = meta_ref[META_SLOT + place * ARR + pair * 2 + half]
                source, rank = slot // CAP, lax.rem(slot, CAP)
                latents.append(arrived_ref[source, :, pl.ds(pl.multiple_of(rank * KVL, KVL), KVL)])
                both = arrived_ref[source, :, CAP * KVL : CAP * KVL + 128].astype(jnp.float32)
                ropes.append(jnp.where(first_half == rank, both, 0.0))
            span = slice(pair * 2 * piece, (pair + 1) * 2 * piece)
            key_ref[place, span, :] = jnp.concatenate(latents, axis=0)
            rope_ref[place, span, :] = jnp.concatenate(ropes, axis=0).astype(jnp.bfloat16)
    token = lax.broadcasted_iota(jnp.int32, (ARR * piece, heads), 0)
    position = token // piece * PAGE + meta_ref[META_SHARD] * piece + lax.rem(token, piece)
    levels, shrinks, weights = [], [], []
    for place in range(rows):
        query_loads[place].wait()
        query = query_ref[place]
        rope_query = jnp.concatenate([query[KVL:], query[KVL:]], axis=0)
        scores = jnp.dot(key_ref[place], query[:KVL], preferred_element_type=jnp.float32)
        scores += jnp.dot(rope_ref[place], rope_query, preferred_element_type=jnp.float32)
        scores = jnp.where(position < meta_ref[META_LEFT + place], SCORE_SCALE * scores, -jnp.inf)
        old_top, old_total = stat_ref[place : place + 1, :], stat_ref[MAXROWS + place : MAXROWS + place + 1, :]
        top = jnp.maximum(jnp.max(scores, axis=0, keepdims=True), old_top)
        shrink = jnp.exp(old_top - top)
        weight = jnp.exp(scores - top)
        total = jnp.sum(weight, axis=0, keepdims=True) + shrink * old_total
        inverse = 1.0 / total
        weights.append((weight * inverse).astype(jnp.bfloat16))
        shrinks.append(shrink * inverse)
        levels.append(top + jnp.log(total))
    columns = turned(stacked(shrinks))
    even = lax.rem(meta_ref[META_SHARD], 2) == 0
    for place in range(rows):
        blend = blended(weights[place], key_ref[place])
        blend_loads[place].wait()
        partial = (blend + columns[:, place : place + 1] * blend_ref[place]).astype(jnp.bfloat16)
        for chip in range(chips):
            block_even = partial[2 * chip * own : (2 * chip + 1) * own]
            block_odd = partial[(2 * chip + 1) * own : (2 * chip + 2) * own]
            block_mine = jnp.where(even, block_even, block_odd)
            block_other = jnp.where(even, block_odd, block_even)
            for chunk in range(KVL // 128):
                start = ((chip * (KVL // 128) + chunk) * rows + place) * own
                lanes = slice(chunk * 128, (chunk + 1) * 128)
                mine_ref[start : start + own, :] = block_mine[:, lanes]
                other_ref[start : start + own, :] = block_other[:, lanes]
    terms = coded(stacked(levels))
    stats = jnp.concatenate([terms[0][:rows], terms[1][:rows], terms[2][:rows], terms[0][rows:]], axis=0)
    stats = stats.astype(jnp.bfloat16)
    mine_ref[chips * (KVL // 128) * rows * own :, :] = stats
    other_ref[chips * (KVL // 128) * rows * own :, :] = stats


def merge_kernel(side_ref, meta_ref, mine_ref, other_ref, handed_ref, send_ref, column_ref):
    chips = SHARES // 2
    rows, own = MAXROWS, (mine_ref.shape[0] - 16) // (chips * (KVL // 128) * MAXROWS)
    side = side_ref[0]
    stat_base = chips * (KVL // 128) * rows * own
    level_a = decoded(mine_ref[stat_base:, :], rows)
    level_b = decoded(other_ref[stat_base:, :], rows)
    peak = jnp.maximum(level_a, level_b)
    weight_a, weight_b = jnp.exp(level_a - peak), jnp.exp(level_b - peak)
    total = weight_a + weight_b
    terms = coded(peak + jnp.log(total))
    inverse = 1.0 / total
    column_ref[...] = turned(jnp.concatenate([weight_a * inverse, weight_b * inverse], axis=0))
    core = lax.rem(meta_ref[META_SHARD], 2)
    stats = []
    for part in range(2):
        places = range(part * MOVES, (part + 1) * MOVES)
        kept = stacked([term[place : place + 1] for term in terms for place in places], 0, 16)
        stats.append((kept + handed_ref[...]).astype(jnp.bfloat16))
    for chip in range(chips):
        columns = column_ref[pl.ds(pl.multiple_of((2 * chip + core) * own, own), own), :]
        for part in range(2):
            target = jnp.where(side == part, 1, 0) * chips + chip
            for move in range(MOVES):
                place = part * MOVES + move
                column_a = jnp.broadcast_to(columns[:, place : place + 1], (own, 128))
                column_b = jnp.broadcast_to(columns[:, rows + place : rows + place + 1], (own, 128))
                for chunk in range(KVL // 128):
                    start = ((chip * (KVL // 128) + chunk) * rows + place) * own
                    value = column_a * mine_ref[start : start + own, :].astype(jnp.float32)
                    value += column_b * other_ref[start : start + own, :].astype(jnp.float32)
                    to = (chunk * MOVES + move) * own
                    send_ref[target, to : to + own, :] = value.astype(jnp.bfloat16)
            send_ref[target, KVL // 128 * MOVES * own :, :] = stats[part]


def finish_kernel(side_ref, meta_ref, received_ref, latent_ref, out_ref, latent_out, column_ref):
    chips = SHARES // 2
    own = out_ref.shape[1]
    stat_base = KVL // 128 * MOVES * own
    bases, weights = [], []
    for part in range(2):
        base = jnp.where(side_ref[0] == part, 1, 0) * chips
        bases.append(base)
        levels = [decoded(received_ref[base + chip, stat_base:, :], MOVES) for chip in range(chips)]
        peak = functools.reduce(jnp.maximum, levels)
        shares = [jnp.exp(level - peak) for level in levels]
        inverse = 1.0 / functools.reduce(lambda a, b: a + b, shares)
        weights.extend(share * inverse for share in shares)
    column_ref[...] = turned(jnp.concatenate(weights, axis=0))
    columns = column_ref[pl.ds(pl.multiple_of(meta_ref[META_SHARD] * own, own), own), :]
    for part in range(2):
        for move in range(MOVES):
            values = [0.0] * (KVL // 128)
            for chip in range(chips):
                lane = (part * chips + chip) * MOVES + move
                column = jnp.broadcast_to(columns[:, lane : lane + 1], (own, 128))
                for chunk in range(KVL // 128):
                    start = (chunk * MOVES + move) * own
                    block = received_ref[bases[part] + chip, start : start + own, :].astype(jnp.float32)
                    values[chunk] = values[chunk] + column * block
            row = meta_ref[META_ROW + part * MOVES + move]
            out_ref[row] = jnp.concatenate([value.astype(jnp.bfloat16) for value in values], axis=1)
    taken = received_ref[bases[0], stat_base:, :].astype(jnp.float32)
    latent = latent_ref[...]
    place = lax.broadcasted_iota(jnp.int32, latent.shape, 0)
    for move in range(MOVES):
        first = 3 * MOVES + move * LATENT_ROWS
        entry = jnp.concatenate([taken[first + chunk : first + chunk + 1] for chunk in range(LATENT_ROWS)], axis=1)
        latent = jnp.where(place == meta_ref[META_ROW + move], entry[:, : latent.shape[1]], latent)
    latent_out[...] = latent.astype(jnp.bfloat16)


def shards(
    hidden,
    kva_weight,
    kv_gain,
    queries,
    latent_cache,
    outbox,
    out_dest,
    page_table,
    lengths,
    give_rows,
):
    group_count = lax.axis_size(DP)
    chip_count = lax.axis_size("x")
    shard = lax.axis_index(TP).astype(jnp.int32).reshape(1)
    side = lax.axis_index("half").astype(jnp.int32).reshape(1)
    row_count = hidden.shape[0]
    page_piece = latent_cache.shape[1]
    heads = queries.shape[1]
    own = heads // SHARES
    moves = give_rows.shape[0]
    query_t = jnp.swapaxes(queries, 1, 2)
    params = pltpu.CompilerParams(vmem_limit_bytes=VMEM_LIMIT)
    shape = jax.ShapeDtypeStruct
    in_hbm = functools.partial(pltpu.with_memory_space_constraint, memory_space=pltpu.HBM)

    outgoing = pl.pallas_call(
        pack_kernel,
        out_shape=shape((group_count, page_piece, CAP * (KVL + ROPE)), jnp.bfloat16),
        in_specs=[HBM(), HBM()],
        out_specs=ANY(),
        scratch_shapes=[
            pltpu.VMEM((outbox.shape[0] + 1,) + outbox.shape[1:], jnp.bfloat16),
            pltpu.VMEM((group_count, page_piece, CAP * (KVL + ROPE)), jnp.bfloat16),
            pltpu.SMEM(out_dest.shape, jnp.int32),
            pltpu.SMEM((group_count * CAP,), jnp.int32),
            pltpu.SemaphoreType.DMA((8,)),
            pltpu.SemaphoreType.DMA((8,)),
            pltpu.SemaphoreType.DMA,
        ],
        compiler_params=params,
        name="pack",
    )(in_hbm(out_dest), in_hbm(outbox))
    arrived = lax.all_to_all(outgoing, DP, split_axis=0, concat_axis=0, tiled=True, axis_index_groups=[ORDER])

    partial_raw = jnp.dot(hidden, kva_weight, preferred_element_type=jnp.float32)
    parts = lax.all_gather(partial_raw, TP)
    latent = lax.reduce_precision(normalize(jnp.sum(parts, axis=0), kv_gain), 8, 7)

    places = [0] * group_count
    for place, group in enumerate(ORDER):
        places[group] = place
    meta, blend, stats, handed = pl.pallas_call(
        resident_kernel,
        out_shape=(
            shape((128,), jnp.int32),
            shape((row_count, heads, KVL), jnp.float32),
            shape((2 * MAXROWS, heads), jnp.float32),
            shape((16, 128), jnp.float32),
        ),
        in_specs=[SMEM()] * 5 + [VMEM()] * 3,
        out_specs=(SMEM(),) + (VMEM(),) * 3,
        scratch_shapes=[pltpu.VMEM((row_count, RESMAX * page_piece + 16, latent_cache.shape[2]), jnp.bfloat16)],
        compiler_params=params,
        name="resident",
    )(shard, give_rows, page_table, lengths, jnp.array(places, jnp.int32), latent_cache, query_t, latent)

    part_shape = shape((chip_count * (KVL // 128) * row_count * own + 16, 128), jnp.bfloat16)
    mine, other = pl.pallas_call(
        arrived_kernel,
        out_shape=(part_shape, part_shape),
        in_specs=[SMEM(), VMEM(), HBM(), HBM(), VMEM()],
        out_specs=(VMEM(), VMEM()),
        scratch_shapes=[
            pltpu.VMEM(query_t.shape, jnp.bfloat16),
            pltpu.VMEM((row_count, heads, KVL), jnp.float32),
            pltpu.VMEM((row_count, ARR * page_piece, KVL), jnp.bfloat16),
            pltpu.VMEM((row_count, ARR * page_piece, 128), jnp.bfloat16),
            pltpu.SemaphoreType.DMA((2 * row_count,)),
        ],
        compiler_params=params,
        name="arrived",
    )(meta, arrived, in_hbm(query_t), in_hbm(blend), stats)
    other = lax.ppermute(other, "core", [(0, 1), (1, 0)])
    outbound = pl.pallas_call(
        merge_kernel,
        out_shape=shape((2 * chip_count, KVL // 128 * moves * own + 16, 128), jnp.bfloat16),
        in_specs=[SMEM()] * 2 + [VMEM()] * 3,
        out_specs=VMEM(),
        scratch_shapes=[pltpu.VMEM((heads, 128), jnp.float32)],
        compiler_params=params,
        name="merge",
    )(side, meta, mine, other, handed)
    received = lax.all_to_all(outbound, ("half", "x"), split_axis=0, concat_axis=0, tiled=True)
    return pl.pallas_call(
        finish_kernel,
        out_shape=(
            shape((row_count, own, KVL), jnp.bfloat16),
            shape(latent.shape, jnp.bfloat16),
        ),
        in_specs=[SMEM()] * 2 + [VMEM()] * 2,
        out_specs=(VMEM(), VMEM()),
        scratch_shapes=[pltpu.VMEM((heads, 128), jnp.float32)],
        compiler_params=params,
        name="finish",
    )(side, meta, received, latent)


def solution(mesh):
    groups, shares = mesh.devices.shape
    split = Mesh(mesh.devices.reshape(2, groups // 2, shares // 2, 2), DP + TP)
    placed = (
        P(DP, TP),
        P(TP, None),
        P(),
        P(DP, None, None),
        P(DP, TP, None),
        P(DP, TP, None),
        P(DP),
        P(DP, None),
        P(DP),
        P(DP),
    )
    return jax.shard_map(
        shards,
        mesh=split,
        in_specs=placed,
        out_specs=(P(DP, TP, None), P(DP, None)),
        check_vma=False,
    )
```

time: 85.4 us -> 82.9 us (0.971)
  the two profiles are of different devices: /device:TPU:16 before, /device:TPU:8 now
where the time goes in v4:
time: 82.9 us; the launch traced here: 82.5 us
  blocking collectives  34.2 us (41%)
  starting transfers between devices  18.5 us (22%)
  waiting for transfers between devices  15.2 us (18%)
  Pallas kernels  10.9 us (13%)
  local copies, waits for them, and re-layouts  2.25 us (3%)
  between operations  0.83 us (1%)
    all_to_all x1, blocking collectives, shards(): lax.all_to_all(outbound, ('half', 'x'), split_axis=0, concat_axis=0, tile...  21.1 us
    all_to_all x1, starting transfers between devices, shards(): lax.all_to_all(outgoing, DP, split_axis=0, concat_axis=0, tiled=True, axi...  16.6 us
    all_to_all x1, waiting for transfers between devices, shards(): lax.all_to_all(outgoing, DP, split_axis=0, concat_axis=0, tiled=True, axi...  13.7 us
    all_gather x1, blocking collectives, shards(): parts = lax.all_gather(partial_raw, TP)  13.1 us
    pallas_call x1, Pallas kernels, shards(): pl.pallas_call(arrived_kernel, out_shape=(part_shape, part_shape), in_spe...  3.51 us
    pallas_call x1, Pallas kernels, shards(): pl.pallas_call(resident_kernel, out_shape=(shape((128,), jnp.int32), shap...  2.54 us
    pallas_call x1, Pallas kernels, shards(): pl.pallas_call(pack_kernel, out_shape=shape((group_count, page_piece, CAP...  2.51 us
    unnamed x20, local copies, waits for them, and re-layouts  2.24 us
  transfers between devices with their start and end apart: 2, of which 2 were waited for; matrix products, arithmetic and copies ran while one was open for 1% of the time, Pallas kernels for 3%

profile of v4, /device:TPU:8, one launch (start us, length us, event | category | flops | bytes accessed | tf_op | source)
XLA Modules:
  0.0 82.5 jit_solution(3390478356829548975)
XLA Ops:
  0.6 0.0 copy-start
  0.6 2.5 %pack.1 = bf16[64,8,1152]{2,1,0:T(8,128)(2,1)} custom-call(s32[64]{0:T(128)} %dest_hbm.1, bf16[64,8,576]{2,1,0:T(8,128)(2,1)} %outbox_ref.1), custom_call_target="tpu_custom_call" | custom-call | tf_op jit(solution)/shard_map/pack/pallas_call | solution.py:345
  3.2 0.0 copy-start.8
  3.2 16.6 %all-to-all-start = ((bf16[64,8,1152]{2,1,0:T(8,128)(2,1)}), bf16[64,8,1152]{2,1,0:T(8,128)(2,1)S(1)}, u32[]{:S(2)}, u32[]{:S(2)}) async-start(bf16[64,8,1152]{2,1,0:T(8,128)(2,1)} %pack.1), calls=%async_computation | async-start | bytes 2359296 | tf_op jit(solution)/shard_map/all_to_all | solution.py:362
  19.8 0.0 copy-start.9
  19.8 0.0 copy-start.1
  19.8 0.0 copy-start.4
  19.8 0.0 copy-start.5
  19.8 0.0 copy-start.6
  19.8 0.0 copy-start.7
  19.9 0.0 copy-done
  19.9 0.0 copy-done.8
  19.9 0.4 convolution_bitcast_fusion
  20.2 13.1 %all-gather.1 = f32[8,4,576]{2,1,0:T(4,128)S(1)} all-gather(f32[1,4,576]{2,1,0:T(4,128)S(1)} %convolution_bitcast_fusion), channel_id=2, replica_groups=mesh['half'=2,'group'=32,'x'=4,'core'=2] {'x','core'}, dimensions={0}, use_global_device_ids=true | all-gather | bytes 82944 | tf_op jit(solution)/shard_map/all_gather | solution.py:365
  33.4 0.1 multiply_reduce_fusion
  33.5 0.0 copy-done.9
  33.5 0.1 multiply_multiply_fusion
  33.6 0.0 copy-done.1
  33.6 0.0 copy-done.4
  33.6 0.0 copy-done.5
  33.7 0.0 copy-start.3
  33.7 1.2 %copy-done.3 = bf16[96,8,576]{2,1,0:T(8,128)(2,1)S(1)} copy-done((bf16[96,8,576]{2,1,0:T(8,128)(2,1)S(1)}, bf16[96,8,576]{2,1,0:T(8,128)(2,1)}, u32[]{:S(2)}) %copy-start.3) | copy-done | bytes 884760
  34.9 2.5 %resident.1 = (s32[128]{0:T(128)S(1)}, f32[4,128,512]{2,1,0:T(8,128)S(1)}, f32[8,128]{1,0:T(8,128)S(1)}, f32[16,128]{1,0:T(8,128)S(1)}) custom-call(s32[1]{0:T(128)} %bitcast.1.shard_ref, s32[2]{0:T(128)S(1)} %copy-done.5, s32[4,40]{1,0:T(4,128)S(1)} %copy-done.4, s32[4]{0:T(128)S(1)} %copy-done.6, s32[64]{0:T(128)S(1)} %copy-done.7, ...), custom_call_target="tpu_custom_call" | custom-call | tf_op jit(solution)/shard_map/resident/pallas_call | solution.py:371
  37.4 0.0 copy-start.2
  37.4 1.0 %copy-done.2 = f32[4,128,512]{2,1,0:T(8,128)} copy-done((f32[4,128,512]{2,1,0:T(8,128)}, f32[4,128,512]{2,1,0:T(8,128)S(1)}, u32[]{:S(2)}) %copy-start.2) | copy-done | bytes 1048600
  38.4 13.7 %all-to-all-done.arrived_ref = bf16[64,8,1152]{2,1,0:T(8,128)(2,1)S(1)} async-done(((bf16[64,8,1152]{2,1,0:T(8,128)(2,1)}), bf16[64,8,1152]{2,1,0:T(8,128)(2,1)S(1)}, u32[]{:S(2)}, u32[]{:S(2)}) %all-to-all-start) | async-done | bytes 1179680 | tf_op jit(solution)/shard_map/all_to_all | solution.py:362
  52.2 3.5 %arrived.1 = (bf16[1040,128]{1,0:T(8,128)(2,1)S(1)}, bf16[1040,128]{1,0:T(8,128)(2,1)S(1)}) custom-call(s32[128]{0:T(128)S(1)} %get-tuple-element.8.meta_ref, bf16[64,8,1152]{2,1,0:T(8,128)(2,1)S(1)} %all-to-all-done.arrived_ref, bf16[4,576,128]{2,1,0:T(8,128)(2,1)} %bitcast.7, f32[4,128,512]{2,1,0:T(8,128)} %copy-done.2, ...), custom_call_target="tpu_custom_call" | custom-call | tf_op jit(solution)/shard_map/arrived/pallas_call | solution.py:387
  55.7 1.9 %collective-permute-start = (bf16[1040,128]{1,0:T(8,128)(2,1)S(1)}, bf16[1040,128]{1,0:T(8,128)(2,1)S(1)}, u32[]{:S(2)}, u32[]{:S(2)}) collective-permute-start(bf16[1040,128]{1,0:T(8,128)(2,1)S(1)} %get-tuple-element.12), channel_id=1, source_target_pairs={{0,1},{1,0},{2,3},{3,2},{4,5},{5,4},{6,7},{7,6},{8,9},{9,8},{10,11... | collective-permute-start | bytes 798728 | tf_op jit(solution)/shard_map/ppermute | solution.py:402
  57.6 1.5 %collective-permute-done.other_ref = bf16[1040,128]{1,0:T(8,128)(2,1)S(1)} collective-permute-done((bf16[1040,128]{1,0:T(8,128)(2,1)S(1)}, bf16[1040,128]{1,0:T(8,128)(2,1)S(1)}, u32[]{:S(2)}, u32[]{:S(2)}) %collective-permute-start) | collective-permute-done | bytes 266272 | tf_op jit(solution)/shard_map/ppermute | solution.py:402
  59.1 0.8 %merge.1 = bf16[8,144,128]{2,1,0:T(8,128)(2,1)S(1)} custom-call(s32[1]{0:T(128)} %bitcast.side_ref, s32[128]{0:T(128)S(1)} %get-tuple-element.8.meta_ref, bf16[1040,128]{1,0:T(8,128)(2,1)S(1)} %get-tuple-element.11.mine_ref, bf16[1040,128]{1,0:T(8,128)(2,1)S(1)} %collective-permute-done.other_ref, f32[16,128]{1,0:T(8,128)S(1)} %get-tuple-element.13.handed_ref), custom_call_target="tpu_custom_call" | custom-call | tf_op jit(solution)/shard_map/merge/pallas_call | solution.py:403
  60.0 21.1 %all_to_all.10.received_ref = bf16[8,144,128]{2,1,0:T(8,128)(2,1)S(1)} all-to-all(bf16[8,144,128]{2,1,0:T(8,128)(2,1)S(1)} %merge.1), channel_id=1, replica_groups=mesh['half'=2,'group'=32,'x'=4,'core'=2] {'half','x'}, dimensions={0} | all-to-all | bytes 589824 | tf_op jit(solution)/shard_map/all_to_all | solution.py:412
  81.1 1.4 %finish.1 = (bf16[4,16,512]{2,1,0:T(8,128)(2,1)}, bf16[4,576]{1,0:T(4,128)(2,1)}) custom-call(s32[1]{0:T(128)} %bitcast.side_ref, s32[128]{0:T(128)S(1)} %get-tuple-element.8.meta_ref, bf16[8,144,128]{2,1,0:T(8,128)(2,1)S(1)} %all_to_all.10.received_ref, f32[4,576]{1,0:T(4,128)S(1)} %maximum_reduce-precision_fusion.latent_ref), custom_call_target="tpu_custom_call" | custom-call | tf_op jit(solution)/shard_map/finish/pallas_call | solution.py:413
  (6 shorter events, 0.1 us)
Async XLA Ops:
  0.6 19.2 %copy-start = (bf16[896,576]{0,1:T(8,128)(2,1)S(1)}, bf16[896,576]{0,1:T(8,128)(2,1)}, u32[]{:S(2)}) copy-start(bf16[896,576]{0,1:T(8,128)(2,1)} %param.12) | copy-start | bytes 3096580
  3.2 16.7 %copy-start.8 = (bf16[4,896]{1,0:T(4,128)(2,1)S(1)}, bf16[4,896]{1,0:T(4,128)(2,1)}, u32[]{:S(2)}) copy-start(bf16[4,896]{1,0:T(4,128)(2,1)} %param.11) | copy-start | bytes 21508
  3.2 49.0 %all-to-all-start = ((bf16[64,8,1152]{2,1,0:T(8,128)(2,1)}), bf16[64,8,1152]{2,1,0:T(8,128)(2,1)S(1)}, u32[]{:S(2)}, u32[]{:S(2)}) async-start(bf16[64,8,1152]{2,1,0:T(8,128)(2,1)} %pack.1), calls=%async_computation | async-start | bytes 2359296 | tf_op jit(solution)/shard_map/all_to_all | solution.py:362
  19.8 13.8 %copy-start.9 = (f32[512]{0:T(512)S(1)}, f32[512]{0:T(512)}, u32[]{:S(2)}) copy-start(f32[512]{0:T(512)} %param.13) | copy-start | bytes 6148
  19.8 13.8 %copy-start.1 = (bf16[4,128,576]{1,2,0:T(8,128)(2,1)S(1)}, bf16[4,128,576]{1,2,0:T(8,128)(2,1)}, u32[]{:S(2)}) copy-start(bf16[4,128,576]{1,2,0:T(8,128)(2,1)} %param.14) | copy-start | bytes 1769476
  19.8 13.8 %copy-start.4 = (s32[4,40]{1,0:T(4,128)S(1)}, s32[4,40]{1,0:T(4,128)}, u32[]{:S(2)}) copy-start(s32[4,40]{1,0:T(4,128)} %table_ref.1) | copy-start | bytes 1924
  19.8 13.8 %copy-start.5 = (s32[2]{0:T(128)S(1)}, s32[2]{0:T(128)}, u32[]{:S(2)}) copy-start(s32[2]{0:T(128)} %give_ref.1) | copy-start | bytes 28
  19.8 13.8 %copy-start.6 = (s32[4]{0:T(128)S(1)}, s32[4]{0:T(128)}, u32[]{:S(2)}) copy-start(s32[4]{0:T(128)} %length_ref.1) | copy-start | bytes 52
  19.8 13.8 %copy-start.7 = (s32[64]{0:T(128)S(1)}, s32[64]{0:T(128)}, u32[]{:S(2)}) copy-start(s32[64]{0:T(128)} %constant.23.clone.places_ref) | copy-start | bytes 772
  33.7 1.2 %copy-start.3 = (bf16[96,8,576]{2,1,0:T(8,128)(2,1)S(1)}, bf16[96,8,576]{2,1,0:T(8,128)(2,1)}, u32[]{:S(2)}) copy-start(bf16[96,8,576]{2,1,0:T(8,128)(2,1)} %cache_ref.1) | copy-start | bytes 2654212
  37.4 1.0 %copy-start.2 = (f32[4,128,512]{2,1,0:T(8,128)}, f32[4,128,512]{2,1,0:T(8,128)S(1)}, u32[]{:S(2)}) copy-start(f32[4,128,512]{2,1,0:T(8,128)S(1)} %get-tuple-element.9.blend_hbm) | copy-start | bytes 3145732
  55.7 3.4 %collective-permute-start = (bf16[1040,128]{1,0:T(8,128)(2,1)S(1)}, bf16[1040,128]{1,0:T(8,128)(2,1)S(1)}, u32[]{:S(2)}, u32[]{:S(2)}) collective-permute-start(bf16[1040,128]{1,0:T(8,128)(2,1)S(1)} %get-tuple-element.12), channel_id=1, source_target_pairs={{0,1},{1,0},{2,3},{3,2},{4,5},{5,4},{6,7},{7,6},{8,9},{9,8},{10,11... | collective-permute-start | bytes 798728 | tf_op jit(solution)/shard_map/ppermute | solution.py:402

commit v5 on v4

--- a/solution.py
+++ b/solution.py
@@ -20,16 +20,10 @@
 SHARES = 8
 DP, TP = ("half", "group"), ("x", "core")
 LATENT_ROWS = 5
-META_SHARD, META_ROW, META_LEFT, META_SLOT = 0, 4, 8, 16
-
-
-def interleaved(rank):
-    y = (rank >> 5 & 1) * 4 + (rank >> 3 & 1) * 2 + (rank >> 1 & 1)
-    z = (rank >> 4 & 1) * 4 + (rank >> 2 & 1) * 2 + (rank & 1)
-    return y * 8 + z
-
-
-ORDER = [interleaved(rank) for rank in range(64)]
+META_LEFT, META_SLOT = 8, 16
+
+
+ORDER = [y * 8 + z for y in range(7, -1, -1) for z in (7, 6, 5, 4, 0, 1, 2, 3)]
 
 
 EPSILON = 1e-06
@@ -56,6 +50,10 @@
     kept_low = jnp.where(low > 0, 0, jnp.where(high > 1, 1, 2))
     kept_high = jnp.where(high < 3, 3, jnp.where(low < 2, 2, 1))
     return [first, second, kept_low, kept_high]
+
+
+def share_index():
+    return lax.axis_index("x") * 2 + lax.axis_index("core")
 
 
 def resident_count(length):
@@ -129,19 +127,21 @@
 
 
 def resident_kernel(
-    shard_ref, give_ref, table_ref, length_ref, places_ref, cache_ref, query_ref, latent_ref,
-    meta_ref, blend_out, stat_ref, handed_ref, key_ref,
+    give_ref, table_ref, length_ref, places_ref, cache_ref, query_ref, latent_ref, meta_ref, stat_ref, handed_ref, place_ref, *refs
 ):
+    query_outs, blend_out, key_ref = refs[:-2], refs[-2], refs[-1]
     piece = cache_ref.shape[1]
-    shard = shard_ref[0]
+    shard = share_index()
     resident = RESMAX * piece
     order = served_order(give_ref)
     tops, totals, handed = [], [], []
-    meta_ref[META_SHARD] = shard
+    row_ids = lax.broadcasted_iota(jnp.int32, place_ref.shape, 0)
+    places = jnp.zeros(place_ref.shape, jnp.int32)
     for place, row in enumerate(order):
+        places = jnp.where(row_ids == row, place, places)
+        query_outs[0][place] = query_ref[row]
         length = length_ref[row]
         count = resident_count(length)
-        meta_ref[META_ROW + place] = row
         meta_ref[META_LEFT + place] = length - count * PAGE
         for entry in range(ARR):
             slot = table_ref[row, count + entry] - RES_POOL
@@ -158,10 +158,11 @@
             latent = jnp.concatenate([latent, jnp.zeros((1, 128 - ROPE), jnp.float32)], axis=1)
             handed.extend(latent[:, chunk * 128 : (chunk + 1) * 128] for chunk in range(LATENT_ROWS))
     handed_ref[...] = stacked(handed, 3 * MOVES, 16)
+    place_ref[...] = places
     for place, row in enumerate(order):
         count = resident_count(length_ref[row])
         keys = key_ref[place]
-        scores = SCORE_SCALE * jnp.dot(keys, query_ref[row], preferred_element_type=jnp.float32)
+        scores = SCORE_SCALE * jnp.dot(keys, query_outs[0][place], preferred_element_type=jnp.float32)
         token = lax.broadcasted_iota(jnp.int32, scores.shape, 0)
         fresh = jnp.where(shard == 0, resident, -1)
         scores = jnp.where((token < count * piece) | (token == fresh), scores, -jnp.inf)
@@ -173,21 +174,18 @@
     stat_ref[...] = stacked(tops + totals)
 
 
-def arrived_kernel(
-    meta_ref, arrived_ref, query_hbm, blend_hbm, stat_ref, mine_ref, other_ref, query_ref, blend_ref, key_ref, rope_ref, sems
-):
+def arrived_kernel(meta_hbm, blend_hbm, query_hbm, arrived_ref, stat_ref, *refs):
+    mine_ref, other_ref, key_ref, rope_ref, blend_refs, query_refs, meta_ref, sems = refs
+    loads = [pltpu.make_async_copy(meta_hbm, meta_ref, sems.at[MAXROWS])]
+    query_loads = [pltpu.make_async_copy(query_hbm.at[place], query_refs.at[place], sems.at[MAXROWS + 1 + place]) for place in range(MAXROWS)]
+    loads += [pltpu.make_async_copy(blend_hbm.at[place], blend_refs.at[place], sems.at[place]) for place in range(MAXROWS)]
+    for load in loads[:1] + query_loads + loads[1:]:
+        load.start()
+    loads[0].wait()
     piece = arrived_ref.shape[1]
-    rows, _, heads = query_ref.shape
+    rows, heads = MAXROWS, stat_ref.shape[1]
     own = heads // SHARES
     chips = SHARES // 2
-    query_loads, blend_loads = [], []
-    for place in range(rows):
-        source = query_hbm.at[meta_ref[META_ROW + place]]
-        query_loads.append(pltpu.make_async_copy(source, query_ref.at[place], sems.at[place]))
-        query_loads[-1].start()
-    for place in range(rows):
-        blend_loads.append(pltpu.make_async_copy(blend_hbm.at[place], blend_ref.at[place], sems.at[rows + place]))
-        blend_loads[-1].start()
     first_half = lax.broadcasted_iota(jnp.int32, (piece, 128), 1) // ROPE
     for place in range(rows):
         for pair in range(ARR // 2):
@@ -202,11 +200,12 @@
             key_ref[place, span, :] = jnp.concatenate(latents, axis=0)
             rope_ref[place, span, :] = jnp.concatenate(ropes, axis=0).astype(jnp.bfloat16)
     token = lax.broadcasted_iota(jnp.int32, (ARR * piece, heads), 0)
-    position = token // piece * PAGE + meta_ref[META_SHARD] * piece + lax.rem(token, piece)
+    position = token // piece * PAGE + share_index() * piece + lax.rem(token, piece)
     levels, shrinks, weights = [], [], []
+    for load in query_loads:
+        load.wait()
     for place in range(rows):
-        query_loads[place].wait()
-        query = query_ref[place]
+        query = query_refs[place]
         rope_query = jnp.concatenate([query[KVL:], query[KVL:]], axis=0)
         scores = jnp.dot(key_ref[place], query[:KVL], preferred_element_type=jnp.float32)
         scores += jnp.dot(rope_ref[place], rope_query, preferred_element_type=jnp.float32)
@@ -221,11 +220,12 @@
         shrinks.append(shrink * inverse)
         levels.append(top + jnp.log(total))
     columns = turned(stacked(shrinks))
-    even = lax.rem(meta_ref[META_SHARD], 2) == 0
+    for load in loads[1:]:
+        load.wait()
+    even = lax.axis_index("core") == 0
     for place in range(rows):
         blend = blended(weights[place], key_ref[place])
-        blend_loads[place].wait()
-        partial = (blend + columns[:, place : place + 1] * blend_ref[place]).astype(jnp.bfloat16)
+        partial = (blend + columns[:, place : place + 1] * blend_refs[place]).astype(jnp.bfloat16)
         for chip in range(chips):
             block_even = partial[2 * chip * own : (2 * chip + 1) * own]
             block_odd = partial[(2 * chip + 1) * own : (2 * chip + 2) * own]
@@ -243,10 +243,10 @@
     other_ref[chips * (KVL // 128) * rows * own :, :] = stats
 
 
-def merge_kernel(side_ref, meta_ref, mine_ref, other_ref, handed_ref, send_ref, column_ref):
+def merge_kernel(mine_ref, other_ref, handed_ref, send_ref, column_ref):
     chips = SHARES // 2
     rows, own = MAXROWS, (mine_ref.shape[0] - 16) // (chips * (KVL // 128) * MAXROWS)
-    side = side_ref[0]
+    side = lax.axis_index("half")
     stat_base = chips * (KVL // 128) * rows * own
     level_a = decoded(mine_ref[stat_base:, :], rows)
     level_b = decoded(other_ref[stat_base:, :], rows)
@@ -256,7 +256,7 @@
     terms = coded(peak + jnp.log(total))
     inverse = 1.0 / total
     column_ref[...] = turned(jnp.concatenate([weight_a * inverse, weight_b * inverse], axis=0))
-    core = lax.rem(meta_ref[META_SHARD], 2)
+    core = lax.axis_index("core")
     stats = []
     for part in range(2):
         places = range(part * MOVES, (part + 1) * MOVES)
@@ -279,13 +279,13 @@
             send_ref[target, KVL // 128 * MOVES * own :, :] = stats[part]
 
 
-def finish_kernel(side_ref, meta_ref, received_ref, latent_ref, out_ref, latent_out, column_ref):
+def finish_kernel(received_ref, latent_ref, place_ref, out_ref, latent_out, column_ref):
     chips = SHARES // 2
     own = out_ref.shape[1]
     stat_base = KVL // 128 * MOVES * own
     bases, weights = [], []
     for part in range(2):
-        base = jnp.where(side_ref[0] == part, 1, 0) * chips
+        base = jnp.where(lax.axis_index("half") == part, 1, 0) * chips
         bases.append(base)
         levels = [decoded(received_ref[base + chip, stat_base:, :], MOVES) for chip in range(chips)]
         peak = functools.reduce(jnp.maximum, levels)
@@ -293,7 +293,8 @@
         inverse = 1.0 / functools.reduce(lambda a, b: a + b, shares)
         weights.extend(share * inverse for share in shares)
     column_ref[...] = turned(jnp.concatenate(weights, axis=0))
-    columns = column_ref[pl.ds(pl.multiple_of(meta_ref[META_SHARD] * own, own), own), :]
+    columns = column_ref[pl.ds(pl.multiple_of(share_index() * own, own), own), :]
+    results = []
     for part in range(2):
         for move in range(MOVES):
             values = [0.0] * (KVL // 128)
@@ -304,15 +305,22 @@
                     start = (chunk * MOVES + move) * own
                     block = received_ref[bases[part] + chip, start : start + own, :].astype(jnp.float32)
                     values[chunk] = values[chunk] + column * block
-            row = meta_ref[META_ROW + part * MOVES + move]
-            out_ref[row] = jnp.concatenate([value.astype(jnp.bfloat16) for value in values], axis=1)
+            results.append(values)
+    for row in range(MAXROWS):
+        at = jnp.broadcast_to(place_ref[row : row + 1, :], (own, 128))
+        for chunk in range(KVL // 128):
+            value = results[MAXROWS - 1][chunk]
+            for place in range(MAXROWS - 1):
+                value = jnp.where(at == place, results[place][chunk], value)
+            out_ref[row, :, chunk * 128 : (chunk + 1) * 128] = value.astype(jnp.bfloat16)
     taken = received_ref[bases[0], stat_base:, :].astype(jnp.float32)
     latent = latent_ref[...]
-    place = lax.broadcasted_iota(jnp.int32, latent.shape, 0)
+    rows, width = latent.shape
+    at = jnp.concatenate([place_ref[:rows, :]] * LATENT_ROWS, axis=1)[:, :width]
     for move in range(MOVES):
         first = 3 * MOVES + move * LATENT_ROWS
         entry = jnp.concatenate([taken[first + chunk : first + chunk + 1] for chunk in range(LATENT_ROWS)], axis=1)
-        latent = jnp.where(place == meta_ref[META_ROW + move], entry[:, : latent.shape[1]], latent)
+        latent = jnp.where(at == move, entry[:, :width], latent)
     latent_out[...] = latent.astype(jnp.bfloat16)
 
 
@@ -330,8 +338,6 @@
 ):
     group_count = lax.axis_size(DP)
     chip_count = lax.axis_size("x")
-    shard = lax.axis_index(TP).astype(jnp.int32).reshape(1)
-    side = lax.axis_index("half").astype(jnp.int32).reshape(1)
     row_count = hidden.shape[0]
     page_piece = latent_cache.shape[1]
     heads = queries.shape[1]
@@ -368,47 +374,50 @@
     places = [0] * group_count
     for place, group in enumerate(ORDER):
         places[group] = place
-    meta, blend, stats, handed = pl.pallas_call(
+    meta, stats, handed, place, *operands, blend = pl.pallas_call(
         resident_kernel,
         out_shape=(
             shape((128,), jnp.int32),
-            shape((row_count, heads, KVL), jnp.float32),
             shape((2 * MAXROWS, heads), jnp.float32),
             shape((16, 128), jnp.float32),
-        ),
-        in_specs=[SMEM()] * 5 + [VMEM()] * 3,
-        out_specs=(SMEM(),) + (VMEM(),) * 3,
+            shape((8, 128), jnp.int32),
+        )
+        + (shape(query_t.shape, jnp.bfloat16),)
+        + (shape((row_count, heads, KVL), jnp.float32),),
+        in_specs=[SMEM()] * 4 + [VMEM()] * 3,
+        out_specs=(SMEM(),) + (VMEM(),) * 5,
         scratch_shapes=[pltpu.VMEM((row_count, RESMAX * page_piece + 16, latent_cache.shape[2]), jnp.bfloat16)],
         compiler_params=params,
         name="resident",
-    )(shard, give_rows, page_table, lengths, jnp.array(places, jnp.int32), latent_cache, query_t, latent)
+    )(give_rows, page_table, lengths, jnp.array(places, jnp.int32), latent_cache, query_t, latent)
 
     part_shape = shape((chip_count * (KVL // 128) * row_count * own + 16, 128), jnp.bfloat16)
     mine, other = pl.pallas_call(
         arrived_kernel,
         out_shape=(part_shape, part_shape),
-        in_specs=[SMEM(), VMEM(), HBM(), HBM(), VMEM()],
+        in_specs=[HBM()] * 3 + [VMEM()] * 2,
         out_specs=(VMEM(), VMEM()),
         scratch_shapes=[
-            pltpu.VMEM(query_t.shape, jnp.bfloat16),
-            pltpu.VMEM((row_count, heads, KVL), jnp.float32),
             pltpu.VMEM((row_count, ARR * page_piece, KVL), jnp.bfloat16),
             pltpu.VMEM((row_count, ARR * page_piece, 128), jnp.bfloat16),
-            pltpu.SemaphoreType.DMA((2 * row_count,)),
+            pltpu.VMEM((row_count, heads, KVL), jnp.float32),
+            pltpu.VMEM(query_t.shape, jnp.bfloat16),
+            pltpu.SMEM((128,), jnp.int32),
+            pltpu.SemaphoreType.DMA((2 * row_count + 1,)),
         ],
         compiler_params=params,
         name="arrived",
-    )(meta, arrived, in_hbm(query_t), in_hbm(blend), stats)
+    )(in_hbm(meta), in_hbm(blend), in_hbm(operands[0]), arrived, stats)
     other = lax.ppermute(other, "core", [(0, 1), (1, 0)])
     outbound = pl.pallas_call(
         merge_kernel,
         out_shape=shape((2 * chip_count, KVL // 128 * moves * own + 16, 128), jnp.bfloat16),
-        in_specs=[SMEM()] * 2 + [VMEM()] * 3,
+        in_specs=[VMEM()] * 3,
         out_specs=VMEM(),
         scratch_shapes=[pltpu.VMEM((heads, 128), jnp.float32)],
         compiler_params=params,
         name="merge",
-    )(side, meta, mine, other, handed)
+    )(mine, other, handed)
     received = lax.all_to_all(outbound, ("half", "x"), split_axis=0, concat_axis=0, tiled=True)
     return pl.pallas_call(
         finish_kernel,
@@ -416,12 +425,12 @@
             shape((row_count, own, KVL), jnp.bfloat16),
             shape(latent.shape, jnp.bfloat16),
         ),
-        in_specs=[SMEM()] * 2 + [VMEM()] * 2,
+        in_specs=[VMEM()] * 3,
         out_specs=(VMEM(), VMEM()),
         scratch_shapes=[pltpu.VMEM((heads, 128), jnp.float32)],
         compiler_params=params,
         name="finish",
-    )(side, meta, received, latent)
+    )(received, latent, place)
 
 
 def solution(mesh):

time: 82.9 us -> 76.5 us (0.923)
  the two profiles are of different devices: /device:TPU:8 before, /device:TPU:72 now
where the time goes in v5:
time: 76.5 us; the launch traced here: 76.2 us
  blocking collectives  34.5 us (45%)
  starting transfers between devices  17.8 us (23%)
  waiting for transfers between devices  10.6 us (14%)
  Pallas kernels  8.34 us (11%)
  local copies, waits for them, and re-layouts  3.41 us (4%)
  between operations  0.82 us (1%)
    all_to_all x1, blocking collectives, shards(): lax.all_to_all(outbound, ('half', 'x'), split_axis=0, concat_axis=0, tile...  21.4 us
    all_to_all x1, starting transfers between devices, shards(): lax.all_to_all(outgoing, DP, split_axis=0, concat_axis=0, tiled=True, axi...  15.9 us
    all_gather x1, blocking collectives, shards(): parts = lax.all_gather(partial_raw, TP)  13.1 us
    all_to_all x1, waiting for transfers between devices, shards(): lax.all_to_all(outgoing, DP, split_axis=0, concat_axis=0, tiled=True, axi...  9.08 us
    unnamed x24, local copies, waits for them, and re-layouts  3.4 us
    pallas_call x1, Pallas kernels, shards(): pl.pallas_call(resident_kernel, out_shape=(shape((128,), jnp.int32), shap...  2.57 us
    pallas_call x1, Pallas kernels, shards(): pl.pallas_call(pack_kernel, out_shape=shape((group_count, page_piece, CAP...  2.5 us
    pallas_call x1, Pallas kernels, shards(): pl.pallas_call(arrived_kernel, out_shape=(part_shape, part_shape), in_spe...  2.04 us
  transfers between devices with their start and end apart: 2, of which 2 were waited for; matrix products, arithmetic and copies ran while one was open for 1% of the time, Pallas kernels for 3%

profile of v5, /device:TPU:72, one launch (start us, length us, event | category | flops | bytes accessed | tf_op | source)
XLA Modules:
  0.0 76.2 jit_solution(7602805273852085116)
XLA Ops:
  0.6 0.0 copy-start
  0.6 2.5 %pack.1 = bf16[64,8,1152]{2,1,0:T(8,128)(2,1)} custom-call(s32[64]{0:T(128)} %dest_hbm.1, bf16[64,8,576]{2,1,0:T(8,128)(2,1)} %outbox_ref.1), custom_call_target="tpu_custom_call" | custom-call | tf_op jit(solution)/shard_map/pack/pallas_call | solution.py:351
  3.2 0.0 copy-start.10
  3.2 15.9 %all-to-all-start = ((bf16[64,8,1152]{2,1,0:T(8,128)(2,1)}), bf16[64,8,1152]{2,1,0:T(8,128)(2,1)S(1)}, u32[]{:S(2)}, u32[]{:S(2)}) async-start(bf16[64,8,1152]{2,1,0:T(8,128)(2,1)} %pack.1), calls=%async_computation | async-start | bytes 2359296 | tf_op jit(solution)/shard_map/all_to_all | solution.py:368
  19.1 0.0 copy-done
  19.1 0.0 copy-done.10
  19.1 0.0 copy-start.11
  19.1 0.0 copy-start.2
  19.1 0.0 copy-start.5
  19.2 0.0 copy-start.6
  19.2 0.0 copy-start.7
  19.2 0.0 copy-start.8
  19.2 0.4 convolution_bitcast_fusion
  19.6 13.1 %all-gather.1 = f32[8,4,576]{2,1,0:T(4,128)S(1)} all-gather(f32[1,4,576]{2,1,0:T(4,128)S(1)} %convolution_bitcast_fusion), channel_id=2, replica_groups=mesh['half'=2,'group'=32,'x'=4,'core'=2] {'x','core'}, dimensions={0}, use_global_device_ids=true | all-gather | bytes 82944 | tf_op jit(solution)/shard_map/all_gather | solution.py:371
  32.7 0.1 multiply_reduce_fusion
  32.9 0.1 multiply_multiply_fusion
  32.9 0.0 copy-done.5
  33.0 0.0 copy-done.6
  33.0 0.0 copy-done.7
  33.0 0.0 copy-start.3
  33.0 1.1 %copy-done.3 = bf16[4,128,576]{1,2,0:T(8,128)(2,1)S(1)} copy-done((bf16[4,128,576]{1,2,0:T(8,128)(2,1)S(1)}, bf16[4,128,576]{1,2,0:T(8,128)(2,1)}, u32[]{:S(2)}) %copy-start.3) | copy-done | bytes 589848
  34.1 2.6 %resident.1 = (s32[128]{0:T(128)S(1)}, f32[8,128]{1,0:T(8,128)S(1)}, f32[16,128]{1,0:T(8,128)S(1)}, s32[8,128]{1,0:T(8,128)S(1)}, bf16[4,576,128]{2,1,0:T(8,128)(2,1)S(1)}, /*index=5*/f32[4,128,512]{2,1,0:T(8,128)S(1)}) custom-call(s32[2]{0:T(128)S(1)} %copy-done.6, s32[4,40]{1,0:T(4,128)S(1)} %copy-done.5, s32[4]{0:T(128)S(1)} %copy-done.7, ...), custom_call_target="tpu_custom_call" | custom-call | tf_op jit(solution)/shard_map/resident/pallas_call | solution.py:377
  36.6 1.0 %copy-done.1 = f32[4,128,512]{2,1,0:T(8,128)} copy-done((f32[4,128,512]{2,1,0:T(8,128)}, f32[4,128,512]{2,1,0:T(8,128)S(1)}, u32[]{:S(2)}) %copy-start.1) | copy-done | bytes 1048600
  37.6 0.8 %copy-done.4 = bf16[4,576,128]{2,1,0:T(8,128)(2,1)} copy-done((bf16[4,576,128]{2,1,0:T(8,128)(2,1)}, bf16[4,576,128]{2,1,0:T(8,128)(2,1)S(1)}, u32[]{:S(2)}) %copy-start.4) | copy-done | bytes 589848
  38.4 0.5 copy-done.9
  38.9 9.1 %all-to-all-done.arrived_ref = bf16[64,8,1152]{2,1,0:T(8,128)(2,1)S(1)} async-done(((bf16[64,8,1152]{2,1,0:T(8,128)(2,1)}), bf16[64,8,1152]{2,1,0:T(8,128)(2,1)S(1)}, u32[]{:S(2)}, u32[]{:S(2)}) %all-to-all-start) | async-done | bytes 1179680 | tf_op jit(solution)/shard_map/all_to_all | solution.py:368
  48.0 2.0 %arrived.1 = (bf16[1040,128]{1,0:T(8,128)(2,1)S(1)}, bf16[1040,128]{1,0:T(8,128)(2,1)S(1)}) custom-call(s32[128]{0:T(128)} %copy-done.9, f32[4,128,512]{2,1,0:T(8,128)} %copy-done.1, bf16[4,576,128]{2,1,0:T(8,128)(2,1)} %copy-done.4, bf16[64,8,1152]{2,1,0:T(8,128)(2,1)S(1)} %all-to-all-done.arrived_ref, f32[8,128]{1,0:T(8,128)S(1)} %get-tuple-element.13.stat_ref), custom_call_target="tpu_custom_call" | custom-call | tf_op jit(solution)/shard_map/arrived/pallas_call | solution.py:395
  50.1 1.9 %collective-permute-start = (bf16[1040,128]{1,0:T(8,128)(2,1)S(1)}, bf16[1040,128]{1,0:T(8,128)(2,1)S(1)}, u32[]{:S(2)}, u32[]{:S(2)}) collective-permute-start(bf16[1040,128]{1,0:T(8,128)(2,1)S(1)} %get-tuple-element.15), channel_id=1, source_target_pairs={{0,1},{1,0},{2,3},{3,2},{4,5},{5,4},{6,7},{7,6},{8,9},{9,8},{10,11... | collective-permute-start | bytes 798728 | tf_op jit(solution)/shard_map/ppermute | solution.py:411
  52.0 1.5 %collective-permute-done.other_ref = bf16[1040,128]{1,0:T(8,128)(2,1)S(1)} collective-permute-done((bf16[1040,128]{1,0:T(8,128)(2,1)S(1)}, bf16[1040,128]{1,0:T(8,128)(2,1)S(1)}, u32[]{:S(2)}, u32[]{:S(2)}) %collective-permute-start) | collective-permute-done | bytes 266272 | tf_op jit(solution)/shard_map/ppermute | solution.py:411
  53.5 0.3 merge.1
  53.8 21.4 %all_to_all.10.received_ref = bf16[8,144,128]{2,1,0:T(8,128)(2,1)S(1)} all-to-all(bf16[8,144,128]{2,1,0:T(8,128)(2,1)S(1)} %merge.1), channel_id=1, replica_groups=mesh['half'=2,'group'=32,'x'=4,'core'=2] {'half','x'}, dimensions={0} | all-to-all | bytes 589824 | tf_op jit(solution)/shard_map/all_to_all | solution.py:421
  75.2 0.9 %finish.1 = (bf16[4,16,512]{2,1,0:T(8,128)(2,1)}, bf16[4,576]{1,0:T(4,128)(2,1)}) custom-call(bf16[8,144,128]{2,1,0:T(8,128)(2,1)S(1)} %all_to_all.10.received_ref, f32[4,576]{1,0:T(4,128)S(1)} %maximum_reduce-precision_fusion.latent_ref, s32[8,128]{1,0:T(8,128)S(1)} %get-tuple-element.17.place_ref), custom_call_target="tpu_custom_call" | custom-call | tf_op jit(solution)/shard_map/finish/pallas_call | solution.py:422
  (10 shorter events, 0.1 us)
Async XLA Ops:
  0.6 18.5 %copy-start = (bf16[896,576]{0,1:T(8,128)(2,1)S(1)}, bf16[896,576]{0,1:T(8,128)(2,1)}, u32[]{:S(2)}) copy-start(bf16[896,576]{0,1:T(8,128)(2,1)} %param.12) | copy-start | bytes 3096580
  3.2 16.0 %copy-start.10 = (bf16[4,896]{1,0:T(4,128)(2,1)S(1)}, bf16[4,896]{1,0:T(4,128)(2,1)}, u32[]{:S(2)}) copy-start(bf16[4,896]{1,0:T(4,128)(2,1)} %param.11) | copy-start | bytes 21508
  3.2 44.8 %all-to-all-start = ((bf16[64,8,1152]{2,1,0:T(8,128)(2,1)}), bf16[64,8,1152]{2,1,0:T(8,128)(2,1)S(1)}, u32[]{:S(2)}, u32[]{:S(2)}) async-start(bf16[64,8,1152]{2,1,0:T(8,128)(2,1)} %pack.1), calls=%async_computation | async-start | bytes 2359296 | tf_op jit(solution)/shard_map/all_to_all | solution.py:368
  19.1 13.7 %copy-start.11 = (f32[512]{0:T(512)S(1)}, f32[512]{0:T(512)}, u32[]{:S(2)}) copy-start(f32[512]{0:T(512)} %param.13) | copy-start | bytes 6148
  19.1 13.8 %copy-start.2 = (bf16[96,8,576]{2,1,0:T(8,128)(2,1)S(1)}, bf16[96,8,576]{2,1,0:T(8,128)(2,1)}, u32[]{:S(2)}) copy-start(bf16[96,8,576]{2,1,0:T(8,128)(2,1)} %cache_ref.1) | copy-start | bytes 2654212
  19.1 13.8 %copy-start.5 = (s32[4,40]{1,0:T(4,128)S(1)}, s32[4,40]{1,0:T(4,128)}, u32[]{:S(2)}) copy-start(s32[4,40]{1,0:T(4,128)} %table_ref.1) | copy-start | bytes 1924
  19.2 13.8 %copy-start.6 = (s32[2]{0:T(128)S(1)}, s32[2]{0:T(128)}, u32[]{:S(2)}) copy-start(s32[2]{0:T(128)} %give_ref.1) | copy-start | bytes 28
  19.2 13.8 %copy-start.7 = (s32[4]{0:T(128)S(1)}, s32[4]{0:T(128)}, u32[]{:S(2)}) copy-start(s32[4]{0:T(128)} %length_ref.1) | copy-start | bytes 52
  19.2 13.8 %copy-start.8 = (s32[64]{0:T(128)S(1)}, s32[64]{0:T(128)}, u32[]{:S(2)}) copy-start(s32[64]{0:T(128)} %constant.9.clone.places_ref) | copy-start | bytes 772
  33.0 1.1 %copy-start.3 = (bf16[4,128,576]{1,2,0:T(8,128)(2,1)S(1)}, bf16[4,128,576]{1,2,0:T(8,128)(2,1)}, u32[]{:S(2)}) copy-start(bf16[4,128,576]{1,2,0:T(8,128)(2,1)} %param.14) | copy-start | bytes 1769476
  36.6 1.0 %copy-start.1 = (f32[4,128,512]{2,1,0:T(8,128)}, f32[4,128,512]{2,1,0:T(8,128)S(1)}, u32[]{:S(2)}) copy-start(f32[4,128,512]{2,1,0:T(8,128)S(1)} %get-tuple-element.11.blend_hbm) | copy-start | bytes 3145732
  37.6 0.8 %copy-start.4 = (bf16[4,576,128]{2,1,0:T(8,128)(2,1)}, bf16[4,576,128]{2,1,0:T(8,128)(2,1)S(1)}, u32[]{:S(2)}) copy-start(bf16[4,576,128]{2,1,0:T(8,128)(2,1)S(1)} %get-tuple-element.12.query_hbm) | copy-start | bytes 1769476
  38.4 0.5 copy-start.9
  50.1 3.4 %collective-permute-start = (bf16[1040,128]{1,0:T(8,128)(2,1)S(1)}, bf16[1040,128]{1,0:T(8,128)(2,1)S(1)}, u32[]{:S(2)}, u32[]{:S(2)}) collective-permute-start(bf16[1040,128]{1,0:T(8,128)(2,1)S(1)} %get-tuple-element.15), channel_id=1, source_target_pairs={{0,1},{1,0},{2,3},{3,2},{4,5},{5,4},{6,7},{7,6},{8,9},{9,8},{10,11... | collective-permute-start | bytes 798728 | tf_op jit(solution)/shard_map/ppermute | solution.py:411

commit v6 on v5

--- a/solution.py
+++ b/solution.py
@@ -21,11 +21,8 @@
 DP, TP = ("half", "group"), ("x", "core")
 LATENT_ROWS = 5
 META_LEFT, META_SLOT = 8, 16
-
-
 ORDER = [y * 8 + z for y in range(7, -1, -1) for z in (7, 6, 5, 4, 0, 1, 2, 3)]
-
-
+PEERS = list(range(7, -1, -1))
 EPSILON = 1e-06
 SCORE_SCALE = 192.0 ** (-0.5)
 VMEM_LIMIT = 32 * 1024 * 1024
@@ -265,7 +262,7 @@
     for chip in range(chips):
         columns = column_ref[pl.ds(pl.multiple_of((2 * chip + core) * own, own), own), :]
         for part in range(2):
-            target = jnp.where(side == part, 1, 0) * chips + chip
+            target = jnp.where(side == part, PEERS.index(chips + chip), PEERS.index(chip))
             for move in range(MOVES):
                 place = part * MOVES + move
                 column_a = jnp.broadcast_to(columns[:, place : place + 1], (own, 128))
@@ -283,11 +280,13 @@
     chips = SHARES // 2
     own = out_ref.shape[1]
     stat_base = KVL // 128 * MOVES * own
-    bases, weights = [], []
+    side = lax.axis_index("half")
+    sources, weights = [], []
     for part in range(2):
-        base = jnp.where(lax.axis_index("half") == part, 1, 0) * chips
-        bases.append(base)
-        levels = [decoded(received_ref[base + chip, stat_base:, :], MOVES) for chip in range(chips)]
+        sources.append(
+            [jnp.where(side == part, PEERS.index(chips + chip), PEERS.index(chip)) for chip in range(chips)]
+        )
+        levels = [decoded(received_ref[source, stat_base:, :], MOVES) for source in sources[part]]
         peak = functools.reduce(jnp.maximum, levels)
         shares = [jnp.exp(level - peak) for level in levels]
         inverse = 1.0 / functools.reduce(lambda a, b: a + b, shares)
@@ -303,7 +302,7 @@
                 column = jnp.broadcast_to(columns[:, lane : lane + 1], (own, 128))
                 for chunk in range(KVL // 128):
                     start = (chunk * MOVES + move) * own
-                    block = received_ref[bases[part] + chip, start : start + own, :].astype(jnp.float32)
+                    block = received_ref[sources[part][chip], start : start + own, :].astype(jnp.float32)
                     values[chunk] = values[chunk] + column * block
             results.append(values)
     for row in range(MAXROWS):
@@ -313,7 +312,7 @@
             for place in range(MAXROWS - 1):
                 value = jnp.where(at == place, results[place][chunk], value)
             out_ref[row, :, chunk * 128 : (chunk + 1) * 128] = value.astype(jnp.bfloat16)
-    taken = received_ref[bases[0], stat_base:, :].astype(jnp.float32)
+    taken = received_ref[sources[0][0], stat_base:, :].astype(jnp.float32)
     latent = latent_ref[...]
     rows, width = latent.shape
     at = jnp.concatenate([place_ref[:rows, :]] * LATENT_ROWS, axis=1)[:, :width]
@@ -418,7 +417,9 @@
         compiler_params=params,
         name="merge",
     )(mine, other, handed)
-    received = lax.all_to_all(outbound, ("half", "x"), split_axis=0, concat_axis=0, tiled=True)
+    received = lax.all_to_all(
+        outbound, ("half", "x"), split_axis=0, concat_axis=0, tiled=True, axis_index_groups=[PEERS]
+    )
     return pl.pallas_call(
         finish_kernel,
         out_shape=(

time: 76.5 us -> 75.1 us (0.982)
  the two profiles are of different devices: /device:TPU:72 before, /device:TPU:48 now
where the time goes in v6:
time: 75.1 us; the launch traced here: 74.8 us
  blocking collectives  34.2 us (46%)
  starting transfers between devices  15.8 us (21%)
  waiting for transfers between devices  11.6 us (15%)
  Pallas kernels  8.34 us (11%)
  local copies, waits for them, and re-layouts  3.41 us (5%)
  between operations  0.82 us (1%)
    all_to_all x1, blocking collectives, shards(): lax.all_to_all(outbound, ('half', 'x'), split_axis=0, concat_axis=0, tile...  21.1 us
    all_to_all x1, starting transfers between devices, shards(): lax.all_to_all(outgoing, DP, split_axis=0, concat_axis=0, tiled=True, axi...  13.9 us
    all_gather x1, blocking collectives, shards(): parts = lax.all_gather(partial_raw, TP)  13.1 us
    all_to_all x1, waiting for transfers between devices, shards(): lax.all_to_all(outgoing, DP, split_axis=0, concat_axis=0, tiled=True, axi...  10.1 us
    unnamed x24, local copies, waits for them, and re-layouts  3.4 us
    pallas_call x1, Pallas kernels, shards(): pl.pallas_call(resident_kernel, out_shape=(shape((128,), jnp.int32), shap...  2.57 us
    pallas_call x1, Pallas kernels, shards(): pl.pallas_call(pack_kernel, out_shape=shape((group_count, page_piece, CAP...  2.5 us
    pallas_call x1, Pallas kernels, shards(): pl.pallas_call(arrived_kernel, out_shape=(part_shape, part_shape), in_spe...  2.04 us
  transfers between devices with their start and end apart: 2, of which 2 were waited for; matrix products, arithmetic and copies ran while one was open for 1% of the time, Pallas kernels for 3%

profile of v6, /device:TPU:48, one launch (start us, length us, event | category | flops | bytes accessed | tf_op | source)
XLA Modules:
  0.0 74.8 jit_solution(9832530319160055313)
XLA Ops:
  0.6 0.0 copy-start
  0.6 2.5 %pack.1 = bf16[64,8,1152]{2,1,0:T(8,128)(2,1)} custom-call(s32[64]{0:T(128)} %dest_hbm.1, bf16[64,8,576]{2,1,0:T(8,128)(2,1)} %outbox_ref.1), custom_call_target="tpu_custom_call" | custom-call | tf_op jit(solution)/shard_map/pack/pallas_call | solution.py:350
  3.2 0.0 copy-start.10
  3.2 13.9 %all-to-all-start = ((bf16[64,8,1152]{2,1,0:T(8,128)(2,1)}), bf16[64,8,1152]{2,1,0:T(8,128)(2,1)S(1)}, u32[]{:S(2)}, u32[]{:S(2)}) async-start(bf16[64,8,1152]{2,1,0:T(8,128)(2,1)} %pack.1), calls=%async_computation | async-start | bytes 2359296 | tf_op jit(solution)/shard_map/all_to_all | solution.py:367
  17.1 0.0 copy-done
  17.1 0.0 copy-done.10
  17.1 0.0 copy-start.11
  17.1 0.0 copy-start.2
  17.1 0.0 copy-start.5
  17.2 0.0 copy-start.6
  17.2 0.0 copy-start.7
  17.2 0.0 copy-start.8
  17.2 0.4 convolution_bitcast_fusion
  17.6 13.1 %all-gather.1 = f32[8,4,576]{2,1,0:T(4,128)S(1)} all-gather(f32[1,4,576]{2,1,0:T(4,128)S(1)} %convolution_bitcast_fusion), channel_id=2, replica_groups=mesh['half'=2,'group'=32,'x'=4,'core'=2] {'x','core'}, dimensions={0}, use_global_device_ids=true | all-gather | bytes 82944 | tf_op jit(solution)/shard_map/all_gather | solution.py:370
  30.7 0.1 multiply_reduce_fusion
  30.8 0.0 copy-done.11
  30.8 0.1 multiply_multiply_fusion
  30.9 0.0 copy-done.2
  31.0 0.0 copy-start.3
  31.0 1.1 %copy-done.3 = bf16[4,128,576]{1,2,0:T(8,128)(2,1)S(1)} copy-done((bf16[4,128,576]{1,2,0:T(8,128)(2,1)S(1)}, bf16[4,128,576]{1,2,0:T(8,128)(2,1)}, u32[]{:S(2)}) %copy-start.3) | copy-done | bytes 589848
  32.0 2.6 %resident.1 = (s32[128]{0:T(128)S(1)}, f32[8,128]{1,0:T(8,128)S(1)}, f32[16,128]{1,0:T(8,128)S(1)}, s32[8,128]{1,0:T(8,128)S(1)}, bf16[4,576,128]{2,1,0:T(8,128)(2,1)S(1)}, /*index=5*/f32[4,128,512]{2,1,0:T(8,128)S(1)}) custom-call(s32[2]{0:T(128)S(1)} %copy-done.6, s32[4,40]{1,0:T(4,128)S(1)} %copy-done.5, s32[4]{0:T(128)S(1)} %copy-done.7, ...), custom_call_target="tpu_custom_call" | custom-call | tf_op jit(solution)/shard_map/resident/pallas_call | solution.py:376
  34.6 0.0 copy-start.1
  34.6 1.0 %copy-done.1 = f32[4,128,512]{2,1,0:T(8,128)} copy-done((f32[4,128,512]{2,1,0:T(8,128)}, f32[4,128,512]{2,1,0:T(8,128)S(1)}, u32[]{:S(2)}) %copy-start.1) | copy-done | bytes 1048600
  35.6 0.8 %copy-done.4 = bf16[4,576,128]{2,1,0:T(8,128)(2,1)} copy-done((bf16[4,576,128]{2,1,0:T(8,128)(2,1)}, bf16[4,576,128]{2,1,0:T(8,128)(2,1)S(1)}, u32[]{:S(2)}) %copy-start.4) | copy-done | bytes 589848
  36.4 0.5 copy-done.9
  36.9 10.1 %all-to-all-done.arrived_ref = bf16[64,8,1152]{2,1,0:T(8,128)(2,1)S(1)} async-done(((bf16[64,8,1152]{2,1,0:T(8,128)(2,1)}), bf16[64,8,1152]{2,1,0:T(8,128)(2,1)S(1)}, u32[]{:S(2)}, u32[]{:S(2)}) %all-to-all-start) | async-done | bytes 1179680 | tf_op jit(solution)/shard_map/all_to_all | solution.py:367
  47.0 2.0 %arrived.1 = (bf16[1040,128]{1,0:T(8,128)(2,1)S(1)}, bf16[1040,128]{1,0:T(8,128)(2,1)S(1)}) custom-call(s32[128]{0:T(128)} %copy-done.9, f32[4,128,512]{2,1,0:T(8,128)} %copy-done.1, bf16[4,576,128]{2,1,0:T(8,128)(2,1)} %copy-done.4, bf16[64,8,1152]{2,1,0:T(8,128)(2,1)S(1)} %all-to-all-done.arrived_ref, f32[8,128]{1,0:T(8,128)S(1)} %get-tuple-element.13.stat_ref), custom_call_target="tpu_custom_call" | custom-call | tf_op jit(solution)/shard_map/arrived/pallas_call | solution.py:394
  49.0 1.9 %collective-permute-start = (bf16[1040,128]{1,0:T(8,128)(2,1)S(1)}, bf16[1040,128]{1,0:T(8,128)(2,1)S(1)}, u32[]{:S(2)}, u32[]{:S(2)}) collective-permute-start(bf16[1040,128]{1,0:T(8,128)(2,1)S(1)} %get-tuple-element.15), channel_id=1, source_target_pairs={{0,1},{1,0},{2,3},{3,2},{4,5},{5,4},{6,7},{7,6},{8,9},{9,8},{10,11... | collective-permute-start | bytes 798728 | tf_op jit(solution)/shard_map/ppermute | solution.py:410
  51.0 1.5 %collective-permute-done.other_ref = bf16[1040,128]{1,0:T(8,128)(2,1)S(1)} collective-permute-done((bf16[1040,128]{1,0:T(8,128)(2,1)S(1)}, bf16[1040,128]{1,0:T(8,128)(2,1)S(1)}, u32[]{:S(2)}, u32[]{:S(2)}) %collective-permute-start) | collective-permute-done | bytes 266272 | tf_op jit(solution)/shard_map/ppermute | solution.py:410
  52.5 0.3 merge.1
  52.8 21.1 %all_to_all.10.received_ref = bf16[8,144,128]{2,1,0:T(8,128)(2,1)S(1)} all-to-all(bf16[8,144,128]{2,1,0:T(8,128)(2,1)S(1)} %merge.1), channel_id=1, replica_groups={{262,260,258,256,6,4,2,0},{263,261,259,257,7,5,3,1},{270,268,266,264,14..., dimensions={0} | all-to-all | bytes 589824 | tf_op jit(solution)/shard_map/all_to_all | solution.py:420
  73.8 0.9 %finish.1 = (bf16[4,16,512]{2,1,0:T(8,128)(2,1)}, bf16[4,576]{1,0:T(4,128)(2,1)}) custom-call(bf16[8,144,128]{2,1,0:T(8,128)(2,1)S(1)} %all_to_all.10.received_ref, f32[4,576]{1,0:T(4,128)S(1)} %maximum_reduce-precision_fusion.latent_ref, s32[8,128]{1,0:T(8,128)S(1)} %get-tuple-element.17.place_ref), custom_call_target="tpu_custom_call" | custom-call | tf_op jit(solution)/shard_map/finish/pallas_call | solution.py:423
  (10 shorter events, 0.1 us)
Async XLA Ops:
  0.6 16.5 %copy-start = (bf16[896,576]{0,1:T(8,128)(2,1)S(1)}, bf16[896,576]{0,1:T(8,128)(2,1)}, u32[]{:S(2)}) copy-start(bf16[896,576]{0,1:T(8,128)(2,1)} %param.12) | copy-start | bytes 3096580
  3.2 14.0 %copy-start.10 = (bf16[4,896]{1,0:T(4,128)(2,1)S(1)}, bf16[4,896]{1,0:T(4,128)(2,1)}, u32[]{:S(2)}) copy-start(bf16[4,896]{1,0:T(4,128)(2,1)} %param.11) | copy-start | bytes 21508
  3.2 43.8 %all-to-all-start = ((bf16[64,8,1152]{2,1,0:T(8,128)(2,1)}), bf16[64,8,1152]{2,1,0:T(8,128)(2,1)S(1)}, u32[]{:S(2)}, u32[]{:S(2)}) async-start(bf16[64,8,1152]{2,1,0:T(8,128)(2,1)} %pack.1), calls=%async_computation | async-start | bytes 2359296 | tf_op jit(solution)/shard_map/all_to_all | solution.py:367
  17.1 13.7 %copy-start.11 = (f32[512]{0:T(512)S(1)}, f32[512]{0:T(512)}, u32[]{:S(2)}) copy-start(f32[512]{0:T(512)} %param.13) | copy-start | bytes 6148
  17.1 13.8 %copy-start.2 = (bf16[96,8,576]{2,1,0:T(8,128)(2,1)S(1)}, bf16[96,8,576]{2,1,0:T(8,128)(2,1)}, u32[]{:S(2)}) copy-start(bf16[96,8,576]{2,1,0:T(8,128)(2,1)} %cache_ref.1) | copy-start | bytes 2654212
  17.1 13.8 %copy-start.5 = (s32[4,40]{1,0:T(4,128)S(1)}, s32[4,40]{1,0:T(4,128)}, u32[]{:S(2)}) copy-start(s32[4,40]{1,0:T(4,128)} %table_ref.1) | copy-start | bytes 1924
  17.2 13.8 %copy-start.6 = (s32[2]{0:T(128)S(1)}, s32[2]{0:T(128)}, u32[]{:S(2)}) copy-start(s32[2]{0:T(128)} %give_ref.1) | copy-start | bytes 28
  17.2 13.8 %copy-start.7 = (s32[4]{0:T(128)S(1)}, s32[4]{0:T(128)}, u32[]{:S(2)}) copy-start(s32[4]{0:T(128)} %length_ref.1) | copy-start | bytes 52
  17.2 13.8 %copy-start.8 = (s32[64]{0:T(128)S(1)}, s32[64]{0:T(128)}, u32[]{:S(2)}) copy-start(s32[64]{0:T(128)} %constant.9.clone.places_ref) | copy-start | bytes 772
  31.0 1.1 %copy-start.3 = (bf16[4,128,576]{1,2,0:T(8,128)(2,1)S(1)}, bf16[4,128,576]{1,2,0:T(8,128)(2,1)}, u32[]{:S(2)}) copy-start(bf16[4,128,576]{1,2,0:T(8,128)(2,1)} %param.14) | copy-start | bytes 1769476
  34.6 1.0 %copy-start.1 = (f32[4,128,512]{2,1,0:T(8,128)}, f32[4,128,512]{2,1,0:T(8,128)S(1)}, u32[]{:S(2)}) copy-start(f32[4,128,512]{2,1,0:T(8,128)S(1)} %get-tuple-element.11.blend_hbm) | copy-start | bytes 3145732
  35.6 0.8 %copy-start.4 = (bf16[4,576,128]{2,1,0:T(8,128)(2,1)}, bf16[4,576,128]{2,1,0:T(8,128)(2,1)S(1)}, u32[]{:S(2)}) copy-start(bf16[4,576,128]{2,1,0:T(8,128)(2,1)S(1)} %get-tuple-element.12.query_hbm) | copy-start | bytes 1769476
  36.4 0.5 copy-start.9
  49.0 3.4 %collective-permute-start = (bf16[1040,128]{1,0:T(8,128)(2,1)S(1)}, bf16[1040,128]{1,0:T(8,128)(2,1)S(1)}, u32[]{:S(2)}, u32[]{:S(2)}) collective-permute-start(bf16[1040,128]{1,0:T(8,128)(2,1)S(1)} %get-tuple-element.15), channel_id=1, source_target_pairs={{0,1},{1,0},{2,3},{3,2},{4,5},{5,4},{6,7},{7,6},{8,9},{9,8},{10,11... | collective-permute-start | bytes 798728 | tf_op jit(solution)/shard_map/ppermute | solution.py:410

commit v7 on v6

--- a/solution.py
+++ b/solution.py
@@ -21,7 +21,7 @@
 DP, TP = ("half", "group"), ("x", "core")
 LATENT_ROWS = 5
 META_LEFT, META_SLOT = 8, 16
-ORDER = [y * 8 + z for y in range(7, -1, -1) for z in (7, 6, 5, 4, 0, 1, 2, 3)]
+ORDER = [y * 8 + z for y in range(7, -1, -1) for z in (7, 6, 5, 0, 1, 2, 3, 4)]
 PEERS = list(range(7, -1, -1))
 EPSILON = 1e-06
 SCORE_SCALE = 192.0 ** (-0.5)
@@ -111,10 +111,12 @@
     stores = []
     for part in range(out_sems.shape[0]):
         for dest in range(part * block, (part + 1) * block):
+            ropes = []
             for rank in range(CAP):
                 page = page_ref.at[index_ref[ORDER[dest] * CAP + rank]]
                 stage_ref[dest, :, rank * KVL : (rank + 1) * KVL] = page[:, :KVL]
-                stage_ref[dest, :, CAP * KVL + rank * ROPE : CAP * KVL + (rank + 1) * ROPE] = page[:, KVL:]
+                ropes.append(page[:, KVL:])
+            stage_ref[dest, :, CAP * KVL :] = jnp.concatenate(ropes, axis=1)
         span = pl.ds(part * block, block)
         store = pltpu.make_async_copy(stage_ref.at[span], out_ref.at[span], out_sems.at[part])
         store.start()
@@ -357,8 +359,8 @@
             pltpu.VMEM((group_count, page_piece, CAP * (KVL + ROPE)), jnp.bfloat16),
             pltpu.SMEM(out_dest.shape, jnp.int32),
             pltpu.SMEM((group_count * CAP,), jnp.int32),
-            pltpu.SemaphoreType.DMA((8,)),
-            pltpu.SemaphoreType.DMA((8,)),
+            pltpu.SemaphoreType.DMA((2,)),
+            pltpu.SemaphoreType.DMA((4,)),
             pltpu.SemaphoreType.DMA,
         ],
         compiler_params=params,

time: 75.1 us -> 74.8 us (level)
  no operation moved by 1% of the time
where the time goes in v7:
time: 74.8 us; the launch traced here: 74.4 us
  blocking collectives  33.8 us (45%)
  starting transfers between devices  15.8 us (21%)
  waiting for transfers between devices  11.6 us (16%)
  Pallas kernels  8.25 us (11%)
  local copies, waits for them, and re-layouts  3.41 us (5%)
  between operations  0.82 us (1%)
    all_to_all x1, blocking collectives, shards(): lax.all_to_all(outbound, ('half', 'x'), split_axis=0, concat_axis=0, tile...  20.7 us
    all_to_all x1, starting transfers between devices, shards(): lax.all_to_all(outgoing, DP, split_axis=0, concat_axis=0, tiled=True, axi...  13.9 us
    all_gather x1, blocking collectives, shards(): parts = lax.all_gather(partial_raw, TP)  13.1 us
    all_to_all x1, waiting for transfers between devices, shards(): lax.all_to_all(outgoing, DP, split_axis=0, concat_axis=0, tiled=True, axi...  10.1 us
    unnamed x24, local copies, waits for them, and re-layouts  3.4 us
    pallas_call x1, Pallas kernels, shards(): pl.pallas_call(resident_kernel, out_shape=(shape((128,), jnp.int32), shap...  2.57 us
    pallas_call x1, Pallas kernels, shards(): pl.pallas_call(pack_kernel, out_shape=shape((group_count, page_piece, CAP...  2.41 us
    pallas_call x1, Pallas kernels, shards(): pl.pallas_call(arrived_kernel, out_shape=(part_shape, part_shape), in_spe...  2.04 us
  transfers between devices with their start and end apart: 2, of which 2 were waited for; matrix products, arithmetic and copies ran while one was open for 1% of the time, Pallas kernels for 3%

profile of v7, /device:TPU:48, one launch (start us, length us, event | category | flops | bytes accessed | tf_op | source)
XLA Modules:
  0.0 74.4 jit_solution(755965393686926668)
XLA Ops:
  0.6 0.0 copy-start
  0.6 2.4 %pack.1 = bf16[64,8,1152]{2,1,0:T(8,128)(2,1)} custom-call(s32[64]{0:T(128)} %dest_hbm.1, bf16[64,8,576]{2,1,0:T(8,128)(2,1)} %outbox_ref.1), custom_call_target="tpu_custom_call" | custom-call | tf_op jit(solution)/shard_map/pack/pallas_call | solution.py:352
  3.1 0.0 copy-start.10
  3.1 13.9 %all-to-all-start = ((bf16[64,8,1152]{2,1,0:T(8,128)(2,1)}), bf16[64,8,1152]{2,1,0:T(8,128)(2,1)S(1)}, u32[]{:S(2)}, u32[]{:S(2)}) async-start(bf16[64,8,1152]{2,1,0:T(8,128)(2,1)} %pack.1), calls=%async_computation | async-start | bytes 2359296 | tf_op jit(solution)/shard_map/all_to_all | solution.py:369
  17.0 0.0 copy-done
  17.0 0.0 copy-done.10
  17.0 0.0 copy-start.11
  17.0 0.0 copy-start.2
  17.0 0.0 copy-start.5
  17.1 0.0 copy-start.6
  17.1 0.0 copy-start.7
  17.1 0.0 copy-start.8
  17.1 0.4 convolution_bitcast_fusion
  17.5 13.1 %all-gather.1 = f32[8,4,576]{2,1,0:T(4,128)S(1)} all-gather(f32[1,4,576]{2,1,0:T(4,128)S(1)} %convolution_bitcast_fusion), channel_id=2, replica_groups=mesh['half'=2,'group'=32,'x'=4,'core'=2] {'x','core'}, dimensions={0}, use_global_device_ids=true | all-gather | bytes 82944 | tf_op jit(solution)/shard_map/all_gather | solution.py:372
  30.6 0.1 multiply_reduce_fusion
  30.8 0.0 copy-done.11
  30.8 0.1 multiply_multiply_fusion
  30.8 0.0 copy-done.2
  30.9 0.0 copy-start.3
  30.9 1.1 %copy-done.3 = bf16[4,128,576]{1,2,0:T(8,128)(2,1)S(1)} copy-done((bf16[4,128,576]{1,2,0:T(8,128)(2,1)S(1)}, bf16[4,128,576]{1,2,0:T(8,128)(2,1)}, u32[]{:S(2)}) %copy-start.3) | copy-done | bytes 589848
  32.0 2.6 %resident.1 = (s32[128]{0:T(128)S(1)}, f32[8,128]{1,0:T(8,128)S(1)}, f32[16,128]{1,0:T(8,128)S(1)}, s32[8,128]{1,0:T(8,128)S(1)}, bf16[4,576,128]{2,1,0:T(8,128)(2,1)S(1)}, /*index=5*/f32[4,128,512]{2,1,0:T(8,128)S(1)}) custom-call(s32[2]{0:T(128)S(1)} %copy-done.6, s32[4,40]{1,0:T(4,128)S(1)} %copy-done.5, s32[4]{0:T(128)S(1)} %copy-done.7, ...), custom_call_target="tpu_custom_call" | custom-call | tf_op jit(solution)/shard_map/resident/pallas_call | solution.py:378
  34.5 0.0 copy-start.1
  34.5 1.0 %copy-done.1 = f32[4,128,512]{2,1,0:T(8,128)} copy-done((f32[4,128,512]{2,1,0:T(8,128)}, f32[4,128,512]{2,1,0:T(8,128)S(1)}, u32[]{:S(2)}) %copy-start.1) | copy-done | bytes 1048600
  35.5 0.8 %copy-done.4 = bf16[4,576,128]{2,1,0:T(8,128)(2,1)} copy-done((bf16[4,576,128]{2,1,0:T(8,128)(2,1)}, bf16[4,576,128]{2,1,0:T(8,128)(2,1)S(1)}, u32[]{:S(2)}) %copy-start.4) | copy-done | bytes 589848
  36.3 0.5 copy-done.9
  36.8 10.1 %all-to-all-done.arrived_ref = bf16[64,8,1152]{2,1,0:T(8,128)(2,1)S(1)} async-done(((bf16[64,8,1152]{2,1,0:T(8,128)(2,1)}), bf16[64,8,1152]{2,1,0:T(8,128)(2,1)S(1)}, u32[]{:S(2)}, u32[]{:S(2)}) %all-to-all-start) | async-done | bytes 1179680 | tf_op jit(solution)/shard_map/all_to_all | solution.py:369
  47.0 2.0 %arrived.1 = (bf16[1040,128]{1,0:T(8,128)(2,1)S(1)}, bf16[1040,128]{1,0:T(8,128)(2,1)S(1)}) custom-call(s32[128]{0:T(128)} %copy-done.9, f32[4,128,512]{2,1,0:T(8,128)} %copy-done.1, bf16[4,576,128]{2,1,0:T(8,128)(2,1)} %copy-done.4, bf16[64,8,1152]{2,1,0:T(8,128)(2,1)S(1)} %all-to-all-done.arrived_ref, f32[8,128]{1,0:T(8,128)S(1)} %get-tuple-element.13.stat_ref), custom_call_target="tpu_custom_call" | custom-call | tf_op jit(solution)/shard_map/arrived/pallas_call | solution.py:396
  49.0 1.9 %collective-permute-start = (bf16[1040,128]{1,0:T(8,128)(2,1)S(1)}, bf16[1040,128]{1,0:T(8,128)(2,1)S(1)}, u32[]{:S(2)}, u32[]{:S(2)}) collective-permute-start(bf16[1040,128]{1,0:T(8,128)(2,1)S(1)} %get-tuple-element.15), channel_id=1, source_target_pairs={{0,1},{1,0},{2,3},{3,2},{4,5},{5,4},{6,7},{7,6},{8,9},{9,8},{10,11... | collective-permute-start | bytes 798728 | tf_op jit(solution)/shard_map/ppermute | solution.py:412
  50.9 1.5 %collective-permute-done.other_ref = bf16[1040,128]{1,0:T(8,128)(2,1)S(1)} collective-permute-done((bf16[1040,128]{1,0:T(8,128)(2,1)S(1)}, bf16[1040,128]{1,0:T(8,128)(2,1)S(1)}, u32[]{:S(2)}, u32[]{:S(2)}) %collective-permute-start) | collective-permute-done | bytes 266272 | tf_op jit(solution)/shard_map/ppermute | solution.py:412
  52.4 0.3 merge.1
  52.8 20.7 %all_to_all.10.received_ref = bf16[8,144,128]{2,1,0:T(8,128)(2,1)S(1)} all-to-all(bf16[8,144,128]{2,1,0:T(8,128)(2,1)S(1)} %merge.1), channel_id=1, replica_groups={{262,260,258,256,6,4,2,0},{263,261,259,257,7,5,3,1},{270,268,266,264,14..., dimensions={0} | all-to-all | bytes 589824 | tf_op jit(solution)/shard_map/all_to_all | solution.py:422
  73.5 0.9 %finish.1 = (bf16[4,16,512]{2,1,0:T(8,128)(2,1)}, bf16[4,576]{1,0:T(4,128)(2,1)}) custom-call(bf16[8,144,128]{2,1,0:T(8,128)(2,1)S(1)} %all_to_all.10.received_ref, f32[4,576]{1,0:T(4,128)S(1)} %maximum_reduce-precision_fusion.latent_ref, s32[8,128]{1,0:T(8,128)S(1)} %get-tuple-element.17.place_ref), custom_call_target="tpu_custom_call" | custom-call | tf_op jit(solution)/shard_map/finish/pallas_call | solution.py:425
  (10 shorter events, 0.1 us)
Async XLA Ops:
  0.6 16.4 %copy-start = (bf16[896,576]{0,1:T(8,128)(2,1)S(1)}, bf16[896,576]{0,1:T(8,128)(2,1)}, u32[]{:S(2)}) copy-start(bf16[896,576]{0,1:T(8,128)(2,1)} %param.12) | copy-start | bytes 3096580
  3.1 14.0 %copy-start.10 = (bf16[4,896]{1,0:T(4,128)(2,1)S(1)}, bf16[4,896]{1,0:T(4,128)(2,1)}, u32[]{:S(2)}) copy-start(bf16[4,896]{1,0:T(4,128)(2,1)} %param.11) | copy-start | bytes 21508
  3.1 43.9 %all-to-all-start = ((bf16[64,8,1152]{2,1,0:T(8,128)(2,1)}), bf16[64,8,1152]{2,1,0:T(8,128)(2,1)S(1)}, u32[]{:S(2)}, u32[]{:S(2)}) async-start(bf16[64,8,1152]{2,1,0:T(8,128)(2,1)} %pack.1), calls=%async_computation | async-start | bytes 2359296 | tf_op jit(solution)/shard_map/all_to_all | solution.py:369
  17.0 13.7 %copy-start.11 = (f32[512]{0:T(512)S(1)}, f32[512]{0:T(512)}, u32[]{:S(2)}) copy-start(f32[512]{0:T(512)} %param.13) | copy-start | bytes 6148
  17.0 13.8 %copy-start.2 = (bf16[96,8,576]{2,1,0:T(8,128)(2,1)S(1)}, bf16[96,8,576]{2,1,0:T(8,128)(2,1)}, u32[]{:S(2)}) copy-start(bf16[96,8,576]{2,1,0:T(8,128)(2,1)} %cache_ref.1) | copy-start | bytes 2654212
  17.0 13.8 %copy-start.5 = (s32[4,40]{1,0:T(4,128)S(1)}, s32[4,40]{1,0:T(4,128)}, u32[]{:S(2)}) copy-start(s32[4,40]{1,0:T(4,128)} %table_ref.1) | copy-start | bytes 1924
  17.1 13.8 %copy-start.6 = (s32[2]{0:T(128)S(1)}, s32[2]{0:T(128)}, u32[]{:S(2)}) copy-start(s32[2]{0:T(128)} %give_ref.1) | copy-start | bytes 28
  17.1 13.8 %copy-start.7 = (s32[4]{0:T(128)S(1)}, s32[4]{0:T(128)}, u32[]{:S(2)}) copy-start(s32[4]{0:T(128)} %length_ref.1) | copy-start | bytes 52
  17.1 13.8 %copy-start.8 = (s32[64]{0:T(128)S(1)}, s32[64]{0:T(128)}, u32[]{:S(2)}) copy-start(s32[64]{0:T(128)} %constant.9.clone.places_ref) | copy-start | bytes 772
  30.9 1.1 %copy-start.3 = (bf16[4,128,576]{1,2,0:T(8,128)(2,1)S(1)}, bf16[4,128,576]{1,2,0:T(8,128)(2,1)}, u32[]{:S(2)}) copy-start(bf16[4,128,576]{1,2,0:T(8,128)(2,1)} %param.14) | copy-start | bytes 1769476
  34.5 1.0 %copy-start.1 = (f32[4,128,512]{2,1,0:T(8,128)}, f32[4,128,512]{2,1,0:T(8,128)S(1)}, u32[]{:S(2)}) copy-start(f32[4,128,512]{2,1,0:T(8,128)S(1)} %get-tuple-element.11.blend_hbm) | copy-start | bytes 3145732
  35.5 0.8 %copy-start.4 = (bf16[4,576,128]{2,1,0:T(8,128)(2,1)}, bf16[4,576,128]{2,1,0:T(8,128)(2,1)S(1)}, u32[]{:S(2)}) copy-start(bf16[4,576,128]{2,1,0:T(8,128)(2,1)S(1)} %get-tuple-element.12.query_hbm) | copy-start | bytes 1769476
  36.3 0.5 copy-start.9
  49.0 3.4 %collective-permute-start = (bf16[1040,128]{1,0:T(8,128)(2,1)S(1)}, bf16[1040,128]{1,0:T(8,128)(2,1)S(1)}, u32[]{:S(2)}, u32[]{:S(2)}) collective-permute-start(bf16[1040,128]{1,0:T(8,128)(2,1)S(1)} %get-tuple-element.15), channel_id=1, source_target_pairs={{0,1},{1,0},{2,3},{3,2},{4,5},{5,4},{6,7},{7,6},{8,9},{9,8},{10,11... | collective-permute-start | bytes 798728 | tf_op jit(solution)/shard_map/ppermute | solution.py:412

commit v8 on v7

--- a/solution.py
+++ b/solution.py
@@ -396,7 +396,7 @@
     mine, other = pl.pallas_call(
         arrived_kernel,
         out_shape=(part_shape, part_shape),
-        in_specs=[HBM()] * 3 + [VMEM()] * 2,
+        in_specs=[VMEM()] + [HBM()] * 2 + [VMEM()] * 2,
         out_specs=(VMEM(), VMEM()),
         scratch_shapes=[
             pltpu.VMEM((row_count, ARR * page_piece, KVL), jnp.bfloat16),
@@ -408,7 +408,7 @@
         ],
         compiler_params=params,
         name="arrived",
-    )(in_hbm(meta), in_hbm(blend), in_hbm(operands[0]), arrived, stats)
+    )(meta, in_hbm(blend), in_hbm(operands[0]), arrived, stats)
     other = lax.ppermute(other, "core", [(0, 1), (1, 0)])
     outbound = pl.pallas_call(
         merge_kernel,

time: 74.8 us -> 74.8 us (level)
    unnamed x24 -> x22, local copies, waits for them, and re-layouts: 3.4 us -> 2.91 us
where the time goes in v8:
time: 74.8 us; the launch traced here: 74.4 us
  blocking collectives  33.8 us (45%)
  starting transfers between devices  15.8 us (21%)
  waiting for transfers between devices  12.1 us (16%)
  Pallas kernels  8.26 us (11%)
  local copies, waits for them, and re-layouts  2.92 us (4%)
  between operations  0.82 us (1%)
    all_to_all x1, blocking collectives, shards(): lax.all_to_all(outbound, ('half', 'x'), split_axis=0, concat_axis=0, tile...  20.7 us
    all_to_all x1, starting transfers between devices, shards(): lax.all_to_all(outgoing, DP, split_axis=0, concat_axis=0, tiled=True, axi...  13.9 us
    all_gather x1, blocking collectives, shards(): parts = lax.all_gather(partial_raw, TP)  13.1 us
    all_to_all x1, waiting for transfers between devices, shards(): lax.all_to_all(outgoing, DP, split_axis=0, concat_axis=0, tiled=True, axi...  10.6 us
    unnamed x22, local copies, waits for them, and re-layouts  2.91 us
    pallas_call x1, Pallas kernels, shards(): pl.pallas_call(resident_kernel, out_shape=(shape((128,), jnp.int32), shap...  2.57 us
    pallas_call x1, Pallas kernels, shards(): pl.pallas_call(pack_kernel, out_shape=shape((group_count, page_piece, CAP...  2.41 us
    pallas_call x1, Pallas kernels, shards(): pl.pallas_call(arrived_kernel, out_shape=(part_shape, part_shape), in_spe...  2.04 us
  transfers between devices with their start and end apart: 2, of which 2 were waited for; matrix products, arithmetic and copies ran while one was open for 1% of the time, Pallas kernels for 3%

profile of v8, /device:TPU:48, one launch (start us, length us, event | category | flops | bytes accessed | tf_op | source)
XLA Modules:
  0.0 74.4 jit_solution(12448448761425469247)
XLA Ops:
  0.6 0.0 copy-start
  0.6 2.4 %pack.1 = bf16[64,8,1152]{2,1,0:T(8,128)(2,1)} custom-call(s32[64]{0:T(128)} %dest_hbm.1, bf16[64,8,576]{2,1,0:T(8,128)(2,1)} %outbox_ref.1), custom_call_target="tpu_custom_call" | custom-call | tf_op jit(solution)/shard_map/pack/pallas_call | solution.py:352
  3.1 0.0 copy-start.9
  3.1 13.9 %all-to-all-start = ((bf16[64,8,1152]{2,1,0:T(8,128)(2,1)}), bf16[64,8,1152]{2,1,0:T(8,128)(2,1)S(1)}, u32[]{:S(2)}, u32[]{:S(2)}) async-start(bf16[64,8,1152]{2,1,0:T(8,128)(2,1)} %pack.1), calls=%async_computation | async-start | bytes 2359296 | tf_op jit(solution)/shard_map/all_to_all | solution.py:369
  17.0 0.0 copy-done
  17.0 0.0 copy-done.9
  17.0 0.0 copy-start.10
  17.0 0.0 copy-start.2
  17.1 0.0 copy-start.5
  17.1 0.0 copy-start.6
  17.1 0.0 copy-start.7
  17.1 0.0 copy-start.8
  17.1 0.4 convolution_bitcast_fusion
  17.5 13.1 %all-gather.1 = f32[8,4,576]{2,1,0:T(4,128)S(1)} all-gather(f32[1,4,576]{2,1,0:T(4,128)S(1)} %convolution_bitcast_fusion), channel_id=2, replica_groups=mesh['half'=2,'group'=32,'x'=4,'core'=2] {'x','core'}, dimensions={0}, use_global_device_ids=true | all-gather | bytes 82944 | tf_op jit(solution)/shard_map/all_gather | solution.py:372
  30.6 0.1 multiply_reduce_fusion
  30.8 0.0 copy-done.10
  30.8 0.1 multiply_multiply_fusion
  30.8 0.0 copy-done.2
  30.8 0.0 copy-done.5
  30.9 0.0 copy-done.6
  30.9 0.0 copy-start.3
  30.9 1.1 %copy-done.3 = bf16[4,128,576]{1,2,0:T(8,128)(2,1)S(1)} copy-done((bf16[4,128,576]{1,2,0:T(8,128)(2,1)S(1)}, bf16[4,128,576]{1,2,0:T(8,128)(2,1)}, u32[]{:S(2)}) %copy-start.3) | copy-done | bytes 589848
  32.0 2.6 %resident.1 = (s32[128]{0:T(128)S(1)}, f32[8,128]{1,0:T(8,128)S(1)}, f32[16,128]{1,0:T(8,128)S(1)}, s32[8,128]{1,0:T(8,128)S(1)}, bf16[4,576,128]{2,1,0:T(8,128)(2,1)S(1)}, /*index=5*/f32[4,128,512]{2,1,0:T(8,128)S(1)}) custom-call(s32[2]{0:T(128)S(1)} %copy-done.6, s32[4,40]{1,0:T(4,128)S(1)} %copy-done.5, s32[4]{0:T(128)S(1)} %copy-done.7, ...), custom_call_target="tpu_custom_call" | custom-call | tf_op jit(solution)/shard_map/resident/pallas_call | solution.py:378
  34.5 1.0 %copy-done.1 = f32[4,128,512]{2,1,0:T(8,128)} copy-done((f32[4,128,512]{2,1,0:T(8,128)}, f32[4,128,512]{2,1,0:T(8,128)S(1)}, u32[]{:S(2)}) %copy-start.1) | copy-done | bytes 1048600
  35.5 0.8 %copy-done.4 = bf16[4,576,128]{2,1,0:T(8,128)(2,1)} copy-done((bf16[4,576,128]{2,1,0:T(8,128)(2,1)}, bf16[4,576,128]{2,1,0:T(8,128)(2,1)S(1)}, u32[]{:S(2)}) %copy-start.4) | copy-done | bytes 589848
  36.3 10.6 %all-to-all-done.arrived_ref = bf16[64,8,1152]{2,1,0:T(8,128)(2,1)S(1)} async-done(((bf16[64,8,1152]{2,1,0:T(8,128)(2,1)}), bf16[64,8,1152]{2,1,0:T(8,128)(2,1)S(1)}, u32[]{:S(2)}, u32[]{:S(2)}) %all-to-all-start) | async-done | bytes 1179680 | tf_op jit(solution)/shard_map/all_to_all | solution.py:369
  47.0 2.0 %arrived.1 = (bf16[1040,128]{1,0:T(8,128)(2,1)S(1)}, bf16[1040,128]{1,0:T(8,128)(2,1)S(1)}) custom-call(s32[128]{0:T(128)S(1)} %get-tuple-element.10.meta_hbm, f32[4,128,512]{2,1,0:T(8,128)} %copy-done.1, bf16[4,576,128]{2,1,0:T(8,128)(2,1)} %copy-done.4, bf16[64,8,1152]{2,1,0:T(8,128)(2,1)S(1)} %all-to-all-done.arrived_ref, ...), custom_call_target="tpu_custom_call" | custom-call | tf_op jit(solution)/shard_map/arrived/pallas_call | solution.py:396
  49.0 1.9 %collective-permute-start = (bf16[1040,128]{1,0:T(8,128)(2,1)S(1)}, bf16[1040,128]{1,0:T(8,128)(2,1)S(1)}, u32[]{:S(2)}, u32[]{:S(2)}) collective-permute-start(bf16[1040,128]{1,0:T(8,128)(2,1)S(1)} %get-tuple-element.15), channel_id=1, source_target_pairs={{0,1},{1,0},{2,3},{3,2},{4,5},{5,4},{6,7},{7,6},{8,9},{9,8},{10,11... | collective-permute-start | bytes 798728 | tf_op jit(solution)/shard_map/ppermute | solution.py:412
  50.9 1.5 %collective-permute-done.other_ref = bf16[1040,128]{1,0:T(8,128)(2,1)S(1)} collective-permute-done((bf16[1040,128]{1,0:T(8,128)(2,1)S(1)}, bf16[1040,128]{1,0:T(8,128)(2,1)S(1)}, u32[]{:S(2)}, u32[]{:S(2)}) %collective-permute-start) | collective-permute-done | bytes 266272 | tf_op jit(solution)/shard_map/ppermute | solution.py:412
  52.5 0.3 merge.1
  52.8 20.7 %all_to_all.10.received_ref = bf16[8,144,128]{2,1,0:T(8,128)(2,1)S(1)} all-to-all(bf16[8,144,128]{2,1,0:T(8,128)(2,1)S(1)} %merge.1), channel_id=1, replica_groups={{262,260,258,256,6,4,2,0},{263,261,259,257,7,5,3,1},{270,268,266,264,14..., dimensions={0} | all-to-all | bytes 589824 | tf_op jit(solution)/shard_map/all_to_all | solution.py:422
  73.5 0.9 %finish.1 = (bf16[4,16,512]{2,1,0:T(8,128)(2,1)}, bf16[4,576]{1,0:T(4,128)(2,1)}) custom-call(bf16[8,144,128]{2,1,0:T(8,128)(2,1)S(1)} %all_to_all.10.received_ref, f32[4,576]{1,0:T(4,128)S(1)} %maximum_reduce-precision_fusion.latent_ref, s32[8,128]{1,0:T(8,128)S(1)} %get-tuple-element.17.place_ref), custom_call_target="tpu_custom_call" | custom-call | tf_op jit(solution)/shard_map/finish/pallas_call | solution.py:425
  (8 shorter events, 0.1 us)
Async XLA Ops:
  0.6 16.4 %copy-start = (bf16[896,576]{0,1:T(8,128)(2,1)S(1)}, bf16[896,576]{0,1:T(8,128)(2,1)}, u32[]{:S(2)}) copy-start(bf16[896,576]{0,1:T(8,128)(2,1)} %param.12) | copy-start | bytes 3096580
  3.1 14.0 %copy-start.9 = (bf16[4,896]{1,0:T(4,128)(2,1)S(1)}, bf16[4,896]{1,0:T(4,128)(2,1)}, u32[]{:S(2)}) copy-start(bf16[4,896]{1,0:T(4,128)(2,1)} %param.11) | copy-start | bytes 21508
  3.1 43.9 %all-to-all-start = ((bf16[64,8,1152]{2,1,0:T(8,128)(2,1)}), bf16[64,8,1152]{2,1,0:T(8,128)(2,1)S(1)}, u32[]{:S(2)}, u32[]{:S(2)}) async-start(bf16[64,8,1152]{2,1,0:T(8,128)(2,1)} %pack.1), calls=%async_computation | async-start | bytes 2359296 | tf_op jit(solution)/shard_map/all_to_all | solution.py:369
  17.0 13.7 %copy-start.10 = (f32[512]{0:T(512)S(1)}, f32[512]{0:T(512)}, u32[]{:S(2)}) copy-start(f32[512]{0:T(512)} %param.13) | copy-start | bytes 6148
  17.0 13.8 %copy-start.2 = (bf16[96,8,576]{2,1,0:T(8,128)(2,1)S(1)}, bf16[96,8,576]{2,1,0:T(8,128)(2,1)}, u32[]{:S(2)}) copy-start(bf16[96,8,576]{2,1,0:T(8,128)(2,1)} %cache_ref.1) | copy-start | bytes 2654212
  17.1 13.8 %copy-start.5 = (s32[4,40]{1,0:T(4,128)S(1)}, s32[4,40]{1,0:T(4,128)}, u32[]{:S(2)}) copy-start(s32[4,40]{1,0:T(4,128)} %table_ref.1) | copy-start | bytes 1924
  17.1 13.8 %copy-start.6 = (s32[2]{0:T(128)S(1)}, s32[2]{0:T(128)}, u32[]{:S(2)}) copy-start(s32[2]{0:T(128)} %give_ref.1) | copy-start | bytes 28
  17.1 13.8 %copy-start.7 = (s32[4]{0:T(128)S(1)}, s32[4]{0:T(128)}, u32[]{:S(2)}) copy-start(s32[4]{0:T(128)} %length_ref.1) | copy-start | bytes 52
  17.1 13.8 %copy-start.8 = (s32[64]{0:T(128)S(1)}, s32[64]{0:T(128)}, u32[]{:S(2)}) copy-start(s32[64]{0:T(128)} %constant.9.clone.places_ref) | copy-start | bytes 772
  30.9 1.1 %copy-start.3 = (bf16[4,128,576]{1,2,0:T(8,128)(2,1)S(1)}, bf16[4,128,576]{1,2,0:T(8,128)(2,1)}, u32[]{:S(2)}) copy-start(bf16[4,128,576]{1,2,0:T(8,128)(2,1)} %param.14) | copy-start | bytes 1769476
  34.5 1.0 %copy-start.1 = (f32[4,128,512]{2,1,0:T(8,128)}, f32[4,128,512]{2,1,0:T(8,128)S(1)}, u32[]{:S(2)}) copy-start(f32[4,128,512]{2,1,0:T(8,128)S(1)} %get-tuple-element.11.blend_hbm) | copy-start | bytes 3145732
  35.5 0.8 %copy-start.4 = (bf16[4,576,128]{2,1,0:T(8,128)(2,1)}, bf16[4,576,128]{2,1,0:T(8,128)(2,1)S(1)}, u32[]{:S(2)}) copy-start(bf16[4,576,128]{2,1,0:T(8,128)(2,1)S(1)} %get-tuple-element.12.query_hbm) | copy-start | bytes 1769476
  49.0 3.4 %collective-permute-start = (bf16[1040,128]{1,0:T(8,128)(2,1)S(1)}, bf16[1040,128]{1,0:T(8,128)(2,1)S(1)}, u32[]{:S(2)}, u32[]{:S(2)}) collective-permute-start(bf16[1040,128]{1,0:T(8,128)(2,1)S(1)} %get-tuple-element.15), channel_id=1, source_target_pairs={{0,1},{1,0},{2,3},{3,2},{4,5},{5,4},{6,7},{7,6},{8,9},{9,8},{10,11... | collective-permute-start | bytes 798728 | tf_op jit(solution)/shard_map/ppermute | solution.py:412
